TPU v7x, 128 devices: a whole 4x4x4 slice. The times are simulated.
128 devices in a mesh: replica: 8 (over y, x_lo), fsdp: 16 (over z, x_hi, core).
Axes of the slice: x: 4 (x_hi: 2, x_lo: 2; x = x_hi * 2 + x_lo), y: 4, z: 4, core: 2. Of those that a mesh axis runs over, the one named last changes fastest.
Arguments:
- tokens: bfloat16 [8, 12288, 8192], P('replica', 'fsdp'), may hold values from -6 to 6
- gain: float32 [8, 8192], P('replica'), may hold values from 0.1 to 1.9
- next_weights: bfloat16 [8, 8192, 1024], P('replica', 'fsdp'), may hold values from -0.0625 to 0.0625
- weights: bfloat16 [8, 8192, 1024], P('replica', 'fsdp'), may hold values from -6 to 6
- snapshot: float32 [8192, 1024], P('fsdp'), may hold values from -6 to 6
- momentum: bfloat16 [8192, 1024], P('fsdp', 'replica'), may hold values from -3 to 3
Outputs:
- next_keys: bfloat16 [8, 12288, 1024], P('replica', 'fsdp')
- new_weights: bfloat16 [8192, 1024], P('fsdp')
- new_momentum: bfloat16 [8192, 1024], P('fsdp', 'replica')
All inputs are finite; a program needn't handle non-finite values.
Results may differ from a plain program's by a relative error of at most 0.015.
Values may be sent and summed in bfloat16 or wider, within the bound.
No kernel may reach another device: no remote copies, remote signals or barrier semaphores. Data moves between devices by JAX's collectives and lax.ppermute only.
A program may use at most 128 MiB of HBM per device.

v0:
```python
import jax
import jax.numpy as jnp
from jax import lax
from jax.sharding import PartitionSpec as P

BLOCK = 128


momentum_decay = 0.9
outer_rate = 0.7


def to_blocks(values, width):
    lead_dims = values.shape[:-1]
    column_count = values.shape[-1]
    grouped = values.reshape(lead_dims + (column_count // width, width))
    largest = jnp.max(jnp.abs(grouped), axis=-1)
    target = (largest + 1e-06) / 448.0
    high_part = target.astype(jnp.bfloat16)
    low_part = (target - high_part.astype(jnp.float32)).astype(jnp.bfloat16)
    block_scale = high_part.astype(jnp.float32) + low_part.astype(jnp.float32)
    levels = (grouped / block_scale[..., None]).astype(jnp.bfloat16)
    scales = jnp.stack([high_part, low_part], axis=-1)
    return (levels.reshape(values.shape), scales)


def from_blocks(levels, scales, width):
    lead_dims = levels.shape[:-1]
    column_count = levels.shape[-1]
    grouped = levels.astype(jnp.float32).reshape(lead_dims + (column_count // width, width))
    block_scale = scales[..., 0].astype(jnp.float32) + scales[..., 1].astype(jnp.float32)
    return (grouped * block_scale[..., None]).reshape(levels.shape)


def body(tokens, gain, next_weights, weights, snapshot, momentum):
    replicas = lax.axis_size("replica")
    owner = lax.axis_index("replica")
    rows_float = tokens[0].astype(jnp.float32)
    square_mean = jnp.mean(rows_float * rows_float, axis=1, keepdims=True)
    normed = (rows_float * lax.rsqrt(square_mean + 1e-05) * gain[0][None, :]).astype(jnp.bfloat16)
    key_rows = jnp.dot(
        normed,
        lax.all_gather(next_weights[0], "fsdp", axis=0, tiled=True),
        preferred_element_type=jnp.float32,
    )
    next_keys = key_rows.astype(jnp.bfloat16)[None]
    pseudo_grad = snapshot - weights[0].astype(jnp.float32)
    levels, scales = to_blocks(pseudo_grad, BLOCK)
    summed = lax.psum_scatter(
        from_blocks(levels, scales, BLOCK), "replica", scatter_dimension=1, tiled=True
    )
    average = summed / replicas
    own_width = momentum.shape[1]
    own_snapshot = lax.dynamic_slice_in_dim(snapshot, owner * own_width, own_width, 1)
    velocity = (momentum_decay * momentum.astype(jnp.float32) + average).astype(jnp.bfloat16)
    updated = own_snapshot - outer_rate * (average + momentum_decay * velocity.astype(jnp.float32))
    new_levels, new_scales = to_blocks(updated, BLOCK)
    all_levels, all_scales = (
        lax.all_gather(new_levels, "replica", axis=1, tiled=True),
        lax.all_gather(new_scales, "replica", axis=1, tiled=True),
    )
    new_weights = from_blocks(all_levels, all_scales, BLOCK).astype(jnp.bfloat16)
    return (next_keys, new_weights, velocity)


def solution(mesh):
    placed = (
        P("replica", "fsdp", None),
        P("replica", None),
        P("replica", "fsdp", None),
        P("replica", "fsdp", None),
        P("fsdp", None),
        P("fsdp", "replica"),
    )
    return jax.shard_map(
        body,
        mesh=mesh,
        in_specs=placed,
        out_specs=(P("replica", "fsdp", None), P("fsdp", None), P("fsdp", "replica")),
        check_vma=False,
    )
```

profile of v0, /device:TPU:1, one launch (start us, length us, event | category | flops | bytes accessed | tf_op | source)
XLA Modules:
  0.0 254.2 jit_solution(2153154465329583548)
XLA Ops:
  7.2 0.0 reduce-scatter.2.cloned.1.call-start
  7.2 2.2 abs_bitcast_fusion
  9.4 1.8 copy.17
  11.2 0.0 copy-start
  11.2 0.0 copy-start.1
  11.2 2.4 reduce_max.18
  13.6 0.1 copy.13
  13.7 0.1 copy.14
  13.8 0.6 div.50
  14.4 0.0 copy-done
  14.4 0.0 copy-done.1
  14.5 2.2 bitcast_multiply_fusion.1
  16.6 0.0 copy-start.4
  16.6 0.0 reduce-scatter.2.cloned.1.call-update
  16.7 0.0 all-gather.4.cloned.1.call-start
  16.7 55.6 %reduce-scatter.2.cloned.1.call-done = f32[512,128]{1,0:T(8,128)} async-done(((f32[512,1024]{1,0:T(8,128)}), f32[512,128]{1,0:T(8,128)}) %reduce-scatter.2.cloned.1.call-update) | async-done | bytes 262160 | tf_op jit(solution)/shard_map/reduce_scatter | solution.py:49
  72.3 0.0 copy-done.4
  72.3 1.1 abs_reduce_fusion
  73.4 0.0 copy-start.3
  73.5 1.8 divide_convert_fusion
  75.3 0.0 all-gather.4.cloned.1.call-update
  75.3 0.0 all-gather.6.cloned.1.call-start
  75.3 0.7 all-gather.6.cloned.1.call-update
  76.0 7.1 %fusion = f32[768]{0:T(1024)S(1)} fusion(bf16[1,768,8192]{2,1,0:T(8,128)(2,1)} %param.6), kind=kLoop, calls=%fused_computation.2 | loop fusion | flops 18873600 | bytes 12585984 | tf_op jit(solution)/shard_map/reduce_sum | solution.py:39
  83.1 0.0 copy-done.3
  83.2 20.3 %all_gather.11 = bf16[512,8,2]{0,2,1:T(2,128)(2,1)S(1)} all-gather(bf16[512,1,2]{0,2,1:T(2,128)(2,1)S(1)} %pad_maximum_fusion), channel_id=1, replica_groups=mesh['replica'=8,'fsdp'=16] {'replica'}, dimensions={1}, use_global_device_ids=true | all-gather | bytes 18432 | tf_op jit(solution)/shard_map/all_gather | solution.py:60
  103.5 0.1 copy.16
  103.6 7.0 %all-gather.4.cloned.1.call-done = bf16[512,1024]{1,0:T(8,128)(2,1)} async-done(((bf16[512,128]{1,0:T(8,128)(2,1)}), bf16[512,1024]{1,0:T(8,128)(2,1)}) %all-gather.4.cloned.1.call-update) | async-done | bytes 1048592 | tf_op jit(solution)/shard_map/all_gather | solution.py:59
  110.6 0.0 copy-start.2
  110.6 0.6 mul.69
  111.2 0.6 copy-done.2
  111.9 0.0 copy-start.5
  111.9 1.5 fusion.9
  113.4 114.9 %all-gather.6.cloned.1.call-done = bf16[1,8192,1024]{2,1,0:T(8,128)(2,1)} async-done(((bf16[1,512,1024]{2,1,0:T(8,128)(2,1)}), bf16[1,8192,1024]{2,1,0:T(8,128)(2,1)}) %all-gather.6.cloned.1.call-update) | async-done | bytes 16777232 | tf_op jit(solution)/shard_map/all_gather | solution.py:43
  228.3 0.0 copy-done.5
  228.3 19.4 %fusion.16 = bf16[1,768,1024]{2,1,0:T(8,128)(2,1)} fusion(bf16[1,8192,1024]{2,1,0:T(8,128)(2,1)} %all-gather.6.cloned.1.call-done, bf16[1,768,8192]{2,1,0:T(8,128)(2,1)} %param.6, f32[8192]{0:T(1024)S(1)} %bitcast.49, f32[768]{0:T(1024)S(1)} %add_rsqrt_fusion), kind=kOutput, calls=%fused_computation.18 | convolution fusion | flops 12910854144 | bytes 30968832 | tf_op jit(solution)/shard_map/dot_general | solution.py:41
  (7 shorter events, 0.1 us)
Async XLA Ops:
  7.2 65.1 %reduce-scatter.2.cloned.1.call-start = ((), (), s32[]{:S(2)}) async-start(), calls=%async_computation.1 | async-start | bytes 2359296 | tf_op jit(solution)/shard_map/reduce_scatter | solution.py:49
  11.2 3.2 %copy-start = (f32[512,1024]{1,0:T(8,128)S(1)}, f32[512,1024]{1,0:T(8,128)}, u32[]{:S(2)}) copy-start(f32[512,1024]{1,0:T(8,128)} %param.10) | copy-start | bytes 6291460
  11.2 3.2 %copy-start.1 = (bf16[1,512,1024]{2,1,0:T(8,128)(2,1)S(1)}, bf16[1,512,1024]{2,1,0:T(8,128)(2,1)}, u32[]{:S(2)}) copy-start(bf16[1,512,1024]{2,1,0:T(8,128)(2,1)} %param.9) | copy-start | bytes 3145732
  16.6 55.7 %copy-start.4 = (bf16[512,128]{1,0:T(8,128)(2,1)S(1)}, bf16[512,128]{1,0:T(8,128)(2,1)}, u32[]{:S(2)}) copy-start(bf16[512,128]{1,0:T(8,128)(2,1)} %param.11) | copy-start | bytes 393220
  16.7 94.0 %all-gather.4.cloned.1.call-start = ((), (), s32[]{:S(2)}) async-start(), calls=%async_computation.2 | async-start | bytes 1179648 | tf_op jit(solution)/shard_map/all_gather | solution.py:59
  73.4 9.7 %copy-start.3 = (bf16[512,128]{1,0:T(8,128)(2,1)}, bf16[512,128]{1,0:T(8,128)(2,1)S(1)}, u32[]{:S(2)}) copy-start(bf16[512,128]{1,0:T(8,128)(2,1)S(1)} %get-tuple-element.4) | copy-start | bytes 393220
  75.3 153.0 %all-gather.6.cloned.1.call-start = ((), (), s32[]{:S(2)}) async-start(), calls=%async_computation.3 | async-start | bytes 17825792 | tf_op jit(solution)/shard_map/all_gather | solution.py:43
  110.6 1.2 copy-start.2
  111.9 116.4 %copy-start.5 = (f32[1,8192]{1,0:T(1,128)S(1)}, f32[1,8192]{1,0:T(1,128)}, u32[]{:S(2)}) copy-start(f32[1,8192]{1,0:T(1,128)} %param.7) | copy-start | bytes 98308
Sparse Core Ops, SparseCore 0:
  16.8 55.4 reduce-scatter.1
  75.4 35.1 all-gather.3
  113.1 115.1 all-gather.5
where the time goes:
time: 254 us
  waiting for transfers between devices  178 us (70%)
  blocking collectives  20.3 us (8%)
  matrix products  19.4 us (8%)
  other arithmetic  18.4 us (7%)
  between operations  13.9 us (5%)
  local copies, waits for them, and re-layouts  4.01 us (2%)
    all_gather x1, waiting for transfers between devices, body(): lax.all_gather(next_weights[0], 'fsdp', axis=0, tiled=True)  115 us
    reduce_scatter x1, waiting for transfers between devices, body(): lax.psum_scatter(from_blocks(levels, scales, BLOCK), 'replica', scatter_d...  55.6 us
    all_gather x1, blocking collectives, body(): lax.all_gather(new_scales, 'replica', axis=1, tiled=True)  20.3 us
    dot_general x1, matrix products, body(): jnp.dot(normed, lax.all_gather(next_weights[0], 'fsdp', axis=0, tiled=Tru...  19.4 us
    reduce_sum x1, other arithmetic, body(): square_mean = jnp.mean(rows_float * rows_float, axis=1, keepdims=True)  7.1 us
    all_gather x1, waiting for transfers between devices, body(): lax.all_gather(new_levels, 'replica', axis=1, tiled=True)  7.03 us
  transfers between devices with their start and end apart: 3, of which 3 were waited for; matrix products, arithmetic and copies ran while one was open for 4% of the time, Pallas kernels for 0%

commit v1 on v0

v1 whole, which is shorter than its diff:
```python
import functools

import jax
import jax.numpy as jnp
from jax import lax
from jax.experimental import pallas as pl
from jax.experimental.pallas import tpu as pltpu
from jax.sharding import PartitionSpec as P

BLOCK = 128
DECAY = 0.9
RATE = 0.7
EPS = 1e-05
MIB = 1024 * 1024

Z, X, C = 4, 2, 2
Y, XL = 4, 2


def fsdp_perm(dz=0, dx=0, dc=0):
    pairs = []
    for z in range(Z):
        for x in range(X):
            for c in range(C):
                to = ((z + dz) % Z) * 4 + ((x + dx) % X) * 2 + (c + dc) % C
                pairs.append((z * 4 + x * 2 + c, to))
    return pairs


def replica_perm(dy=0, dx=0):
    pairs = []
    for y in range(Y):
        for x in range(XL):
            pairs.append((y * XL + x, ((y + dy) % Y) * XL + (x + dx) % XL))
    return pairs


def shift(value, **by):
    return lax.ppermute(value, "fsdp", fsdp_perm(**by))


def shift_replica(value, **by):
    return lax.ppermute(value, "replica", replica_perm(**by))


def cost(flops, nbytes):
    return pl.CostEstimate(flops=flops, bytes_accessed=nbytes, transcendentals=0)


GROUPS = (
    ((0, 0), (3, 0), (1, 0), (0, 1)),
    ((2, 0), (3, 1), (1, 1)),
    ((2, 1),),
)


def group_order(group):
    return [(dz, dx, dc) for dz, dx in group for dc in (0, 1)]


def norm_kernel(width, tokens_ref, gain_ref, *out_refs):
    me = lax.axis_index("fsdp")
    z, x, c = me // 4, (me // 2) % 2, me % 2
    rows, features = tokens_ref.shape[1:]
    total = jnp.zeros((rows, width), jnp.float32)
    for j in range(features // width):
        part = tokens_ref[0, :, j * width : (j + 1) * width].astype(jnp.float32)
        total = total + part * part
    scale = lax.rsqrt(jnp.sum(total, axis=1, keepdims=True) / features + EPS)
    for group, out_ref in zip(GROUPS, out_refs):
        for j, (dz, dx, dc) in enumerate(group_order(group)):
            shard = ((z + dz) % Z) * 4 + ((x + dx) % X) * 2 + (c + dc) % C
            at = pl.ds(pl.multiple_of(shard * width, width), width)
            part = tokens_ref[0, :, at].astype(jnp.float32)
            out_ref[:, j * width : (j + 1) * width] = (
                part * scale * gain_ref[:, at]
            ).astype(jnp.bfloat16)


def norm(tokens, gain, width):
    _, rows, features = tokens.shape
    tile = 64
    widths = [len(group_order(g)) * width for g in GROUPS]
    return pl.pallas_call(
        functools.partial(norm_kernel, width),
        grid=(rows // tile,),
        in_specs=[
            pl.BlockSpec((1, tile, features), lambda i: (0, i, 0)),
            pl.BlockSpec((1, features), lambda i: (0, 0)),
        ],
        out_specs=[pl.BlockSpec((tile, w), lambda i: (i, 0)) for w in widths],
        out_shape=[jax.ShapeDtypeStruct((rows, w), jnp.bfloat16) for w in widths],
        compiler_params=pltpu.CompilerParams(vmem_limit_bytes=24 * MIB),
        cost_estimate=cost(8 * rows * features, 4 * rows * features),
        name="norm",
    )(tokens, gain)


def matmul_kernel(offsets, has_total, *refs):
    normed_ref = refs[0]
    weight_refs = refs[1 : 1 + len(offsets)]
    out_ref = refs[-1]
    total = refs[-2][...] if has_total else None
    for at, weight_ref in zip(offsets, weight_refs):
        depth = weight_ref.shape[0]
        part = jnp.dot(
            normed_ref[:, at : at + depth],
            weight_ref[...],
            preferred_element_type=jnp.float32,
        )
        total = part if total is None else total + part
    out_ref[...] = total.astype(out_ref.dtype).reshape(out_ref.shape)


def matmul(normed, pieces, total, last):
    rows, depth = normed.shape
    columns = pieces[0][1].shape[1]
    tile = 256
    offsets = tuple(at for at, _ in pieces)
    weights = [w for _, w in pieces]
    in_specs = [pl.BlockSpec((rows, depth), lambda n: (0, 0))]
    in_specs += [pl.BlockSpec((w.shape[0], tile), lambda n: (0, n)) for w in weights]
    operands = [normed, *weights]
    if total is not None:
        in_specs.append(pl.BlockSpec((rows, tile), lambda n: (0, n)))
        operands.append(total)
    if last:
        out_spec = pl.BlockSpec((1, rows, tile), lambda n: (0, 0, n))
        out_shape = jax.ShapeDtypeStruct((1, rows, columns), jnp.bfloat16)
    else:
        out_spec = pl.BlockSpec((rows, tile), lambda n: (0, n))
        out_shape = jax.ShapeDtypeStruct((rows, columns), jnp.float32)
    return pl.pallas_call(
        functools.partial(matmul_kernel, offsets, total is not None),
        grid=(columns // tile,),
        in_specs=in_specs,
        out_specs=out_spec,
        out_shape=out_shape,
        compiler_params=pltpu.CompilerParams(vmem_limit_bytes=32 * MIB),
        cost_estimate=cost(2 * rows * depth * columns, 2 * rows * depth + 6 * rows * columns),
        name="project",
    )(*operands)


def scale_of(values):
    target = (jnp.max(jnp.abs(values), axis=1, keepdims=True) + 1e-06) / 448.0
    high = target.astype(jnp.bfloat16).astype(jnp.float32)
    low = (target - high).astype(jnp.bfloat16).astype(jnp.float32)
    return high + low


def rounded(values):
    scale = scale_of(values)
    return (values / scale).astype(jnp.bfloat16).astype(jnp.float32) * scale


def split_kernel(weights_ref, *out_refs):
    y = lax.axis_index("replica") // XL
    width = out_refs[0].shape[1]
    for dy, out_ref in enumerate(out_refs):
        at = pl.multiple_of(((y + dy) % Y) * width, width)
        out_ref[...] = weights_ref[0, :, pl.ds(at, width)]


def partial_kernel(snapshot_ref, *refs):
    weight_refs, (own_ref, other_ref) = refs[:-2], refs[-2:]
    me = lax.axis_index("replica")
    y, x = me // XL, me % XL
    for dx, out_ref in ((0, own_ref), (1, other_ref)):
        column = (x + dx) % XL
        at = pl.multiple_of((y * XL + column) * BLOCK, BLOCK)
        snapshot = snapshot_ref[:, pl.ds(at, BLOCK)]
        inside = pl.ds(pl.multiple_of(column * BLOCK, BLOCK), BLOCK)
        total = None
        for weight_ref in weight_refs:
            part = rounded(snapshot - weight_ref[:, inside].astype(jnp.float32))
            total = part if total is None else total + part
        out_ref[...] = total


def update_kernel(snapshot_ref, momentum_ref, own_ref, other_ref, new_ref, velocity_ref):
    me = lax.axis_index("replica")
    at = pl.multiple_of(me * BLOCK, BLOCK)
    snapshot = snapshot_ref[:, pl.ds(at, BLOCK)]
    average = (own_ref[...] + other_ref[...]) / (Y * XL)
    velocity = (DECAY * momentum_ref[...].astype(jnp.float32) + average).astype(jnp.bfloat16)
    velocity_ref[...] = velocity
    updated = snapshot - RATE * (average + DECAY * velocity.astype(jnp.float32))
    new_ref[...] = rounded(updated).astype(jnp.bfloat16)


def assemble_kernel(*refs):
    piece_refs, out_ref = refs[:-1], refs[-1]
    me = lax.axis_index("replica")
    y, x = me // XL, me % XL
    k = 0
    for dy in range(Y):
        for dx in range(XL):
            owner = ((y + dy) % Y) * XL + (x + dx) % XL
            at = pl.multiple_of(owner * BLOCK, BLOCK)
            out_ref[:, pl.ds(at, BLOCK)] = piece_refs[k][...]
            k += 1


def whole(kernel, out_shape, name, operands):
    spec = pl.BlockSpec(memory_space=pltpu.VMEM)
    nbytes = sum(v.size * v.dtype.itemsize for v in operands)
    return pl.pallas_call(
        kernel,
        in_specs=[spec] * len(operands),
        out_specs=jax.tree.map(lambda _: spec, out_shape),
        out_shape=out_shape,
        compiler_params=pltpu.CompilerParams(vmem_limit_bytes=16 * MIB),
        cost_estimate=cost(8 * nbytes, 2 * nbytes),
        name=name,
    )(*operands)


def body(tokens, gain, next_weights, weights, snapshot, momentum):
    shape = jax.ShapeDtypeStruct
    own = next_weights[0]
    rows, columns = own.shape
    half, quarter = rows // 2, rows // 4

    shards = {(0, 0): own}
    shards[3, 0] = shift(own, dz=1)
    shards[1, 0] = shift(own, dz=-1)
    shards[0, 1] = shift(own, dx=1)

    slices = whole(
        split_kernel,
        [shape((rows, columns // Y), jnp.bfloat16)] * Y,
        "split",
        [weights],
    )
    slices = [slices[0]] + [shift_replica(slices[dy], dy=dy) for dy in range(1, Y)]

    normed = norm(tokens, gain, rows)

    own_sum, other_sum = whole(
        partial_kernel,
        [shape((rows, BLOCK), jnp.float32)] * 2,
        "partial",
        [snapshot, *slices],
    )
    other_sum = shift_replica(other_sum, dx=1)
    new, velocity = whole(
        update_kernel,
        [shape((rows, BLOCK), jnp.bfloat16)] * 2,
        "update",
        [snapshot, momentum, own_sum, other_sum],
    )
    new_other = shift_replica(new, dx=1)
    pieces = []
    for dy in range(Y):
        for value in (new, new_other):
            pieces.append(shift_replica(value, dy=-dy) if dy else value)
    new_weights = whole(
        assemble_kernel, shape((rows, columns), jnp.bfloat16), "assemble", pieces
    )

    def both(value):
        return value, shift(value, dc=1)

    def place(group, *items):
        out = []
        for key, first, pair in items:
            for dc in (0, 1):
                out.append(((group.index(key) * 2 + dc) * rows + first, pair[dc]))
        return out

    first = place(GROUPS[0], *((k, 0, both(shards[k])) for k in GROUPS[0]))

    low_2 = shift(shards[3, 0][:half], dz=1)
    high_2 = shift(shards[1, 0][half:], dz=-1)
    low_31 = shift(shards[0, 1][:half], dz=1)
    low_11 = shift(shards[0, 1][:half], dz=-1)
    high_31 = shift(shards[3, 0][half:], dx=1)
    high_11 = shift(shards[1, 0][half:], dx=1)
    low_21a = shift(low_31[:quarter], dz=1)
    low_21b = shift(low_11[quarter:], dz=-1)
    high_21 = shift(high_2, dx=1)

    second = place(
        GROUPS[1],
        ((2, 0), 0, both(low_2)),
        ((2, 0), half, both(high_2)),
        ((3, 1), 0, both(low_31)),
        ((3, 1), half, both(high_31)),
        ((1, 1), 0, both(low_11)),
        ((1, 1), half, both(high_11)),
    )
    third = place(
        GROUPS[2],
        ((2, 1), 0, both(low_21a)),
        ((2, 1), quarter, both(low_21b)),
        ((2, 1), half, both(high_21)),
    )
    total = matmul(normed[0], first, None, False)
    total = matmul(normed[1], second, total, False)
    next_keys = matmul(normed[2], third, total, True)
    return (next_keys, new_weights, velocity)


def solution(mesh):
    placed = (
        P("replica", "fsdp", None),
        P("replica", None),
        P("replica", "fsdp", None),
        P("replica", "fsdp", None),
        P("fsdp", None),
        P("fsdp", "replica"),
    )
    return jax.shard_map(
        body,
        mesh=mesh,
        in_specs=placed,
        out_specs=(P("replica", "fsdp", None), P("fsdp", None), P("fsdp", "replica")),
        check_vma=False,
    )
```

time: 254 us -> 158 us (0.62)
  waiting for transfers between devices: 178 us -> 33.4 us
  starting transfers between devices: 0.12 us -> 68 us
  Pallas kernels: 0 us -> 29.4 us
  local copies, waits for them, and re-layouts: 4.01 us -> 25.4 us
  blocking collectives: 20.3 us -> 0 us
  matrix products: 19.4 us -> 0 us
  other arithmetic: 18.4 us -> 0 us
  between operations: 13.9 us -> 0.83 us
    all_gather x2 -> x0, waiting for transfers between devices: 122 us -> none  [the longest x1 115 us: body(): lax.all_gather(next_weights[0], 'fsdp', axis=0, tiled=True)]
    ppermute x0 -> x36, starting transfers between devices: none -> 68 us  [the longest x25 50.3 us: shift(): return lax.ppermute(value, 'fsdp', fsdp_perm(**by))]
    reduce_scatter x1 -> x0, waiting for transfers between devices: 55.6 us -> none  [body(): lax.psum_scatter(from_blocks(levels, scales, BLOCK), 'replica', scatter_d...]
    ppermute x0 -> x36, waiting for transfers between devices: none -> 33.4 us  [the longest x11 28 us: shift_replica(): return lax.ppermute(value, 'replica', replica_perm(**by))]
    pallas_call x0 -> x8, Pallas kernels: none -> 29.4 us  [the longest x3 20.4 us: matmul(): pl.pallas_call(functools.partial(matmul_kernel, offsets, total is not Non...]
    unnamed x13 -> x54, local copies, waits for them, and re-layouts: 2.45 us -> 25.2 us
    all_gather x1 -> x0, blocking collectives: 20.3 us -> none  [body(): lax.all_gather(new_scales, 'replica', axis=1, tiled=True)]
    dot_general x1 -> x0, matrix products: 19.4 us -> none  [body(): jnp.dot(normed, lax.all_gather(next_weights[0], 'fsdp', axis=0, tiled=Tru...]
  transfers between devices with their start and end apart: 3 -> 36, of which waited for: 3 -> 9; matrix products, arithmetic and copies ran while one was open for 4% -> 0% of each run, Pallas kernels for 0% -> 16%
where the time goes in v1:
time: 158 us; the launch traced here: 157 us
  starting transfers between devices  68 us (43%)
  waiting for transfers between devices  33.4 us (21%)
  Pallas kernels  29.4 us (19%)
  local copies, waits for them, and re-layouts  25.4 us (16%)
    ppermute x25, starting transfers between devices, shift(): return lax.ppermute(value, 'fsdp', fsdp_perm(**by))  50.3 us
    ppermute x11, waiting for transfers between devices, shift_replica(): return lax.ppermute(value, 'replica', replica_perm(**by))  28 us
    unnamed x54, local copies, waits for them, and re-layouts  25.2 us
    pallas_call x3, Pallas kernels, matmul(): pl.pallas_call(functools.partial(matmul_kernel, offsets, total is not Non...  20.4 us
    ppermute x11, starting transfers between devices, shift_replica(): return lax.ppermute(value, 'replica', replica_perm(**by))  17.8 us
    pallas_call x1, Pallas kernels, norm(): pl.pallas_call(functools.partial(norm_kernel, width), grid=(rows // tile,...  5.7 us
    ppermute x25, waiting for transfers between devices, shift(): return lax.ppermute(value, 'fsdp', fsdp_perm(**by))  5.42 us
    pallas_call x4, Pallas kernels, whole(): pl.pallas_call(kernel, in_specs=[spec] * len(operands), out_specs=jax.tre...  3.3 us
  transfers between devices with their start and end apart: 36, of which 9 were waited for; matrix products, arithmetic and copies ran while one was open for 0% of the time, Pallas kernels for 16%

profile of v1, /device:TPU:1, one launch (start us, length us, event | category | flops | bytes accessed | tf_op | source)
XLA Modules:
  0.0 157.1 jit_solution(16575431376273999318)
XLA Ops:
  0.6 1.2 copy-done.3
  2.0 2.2 %collective-permute-start.25 = (bf16[512,256]{1,0:T(8,128)(2,1)S(1)}, bf16[512,256]{1,0:T(8,128)(2,1)S(1)}, u32[]{:S(2)}, u32[]{:S(2)}) collective-permute-start(bf16[512,256]{1,0:T(8,128)(2,1)S(1)} %get-tuple-element.18), channel_id=1, source_target_pairs={{0,32},{16,48},{32,64},{48,80},{64,96},{80,112},{96,0},{112,16},{1... | collective-permute-start | bytes 786440 | tf_op jit(solution)/shard_map/ppermute | solution.py:43
  4.2 3.8 %collective-permute-start.7 = (bf16[512,1024]{1,0:T(8,128)(2,1)}, bf16[512,1024]{1,0:T(8,128)(2,1)S(1)}, u32[]{:S(2)}, u32[]{:S(2)}) collective-permute-start(bf16[512,1024]{1,0:T(8,128)(2,1)} %bitcast.1), channel_id=1, source_target_pairs={{0,12},{1,13},{2,14},{3,15},{4,0},{5,1},{6,2},{7,3},{8,4},{9,5},{1... | collective-permute-start | bytes 3145736 | tf_op jit(solution)/shard_map/ppermute | solution.py:39
  8.0 2.7 %collective-permute-start = (bf16[512,1024]{1,0:T(8,128)(2,1)}, bf16[512,1024]{1,0:T(8,128)(2,1)S(1)}, u32[]{:S(2)}, u32[]{:S(2)}) collective-permute-start(bf16[512,1024]{1,0:T(8,128)(2,1)} %bitcast.2), channel_id=1, source_target_pairs={{0,2},{1,3},{2,0},{3,1},{4,6},{5,7},{6,4},{7,5},{8,10},{9,11},{10,... | collective-permute-start | bytes 3145736 | tf_op jit(solution)/shard_map/ppermute | solution.py:39
  10.7 2.6 %collective-permute-start.26 = (bf16[512,256]{1,0:T(8,128)(2,1)S(1)}, bf16[512,256]{1,0:T(8,128)(2,1)S(1)}, u32[]{:S(2)}, u32[]{:S(2)}) collective-permute-start(bf16[512,256]{1,0:T(8,128)(2,1)S(1)} %get-tuple-element.19), channel_id=1, source_target_pairs={{0,64},{16,80},{32,96},{48,112},{64,0},{80,16},{96,32},{112,48},{1... | collective-permute-start | bytes 786440 | tf_op jit(solution)/shard_map/ppermute | solution.py:43
  13.3 1.1 collective-permute-start.27
  14.4 4.1 %collective-permute-done.26.refs_2_ = bf16[512,256]{1,0:T(8,128)(2,1)S(1)} collective-permute-done((bf16[512,256]{1,0:T(8,128)(2,1)S(1)}, bf16[512,256]{1,0:T(8,128)(2,1)S(1)}, u32[]{:S(2)}, u32[]{:S(2)}) %collective-permute-start.26) | collective-permute-done | bytes 262176 | tf_op jit(solution)/shard_map/ppermute | solution.py:43
  18.5 2.4 %collective-permute-start.21 = (bf16[512,1024]{1,0:T(8,128)(2,1)}, bf16[512,1024]{1,0:T(8,128)(2,1)S(1)}, u32[]{:S(2)}, u32[]{:S(2)}) collective-permute-start(bf16[512,1024]{1,0:T(8,128)(2,1)} %bitcast.4), channel_id=1, source_target_pairs={{0,1},{1,0},{2,3},{3,2},{4,5},{5,4},{6,7},{7,6},{8,9},{9,8},{10,11... | collective-permute-start | bytes 3145736 | tf_op jit(solution)/shard_map/ppermute | solution.py:39
  20.9 3.1 %collective-permute-done.27.refs_3_ = bf16[512,256]{1,0:T(8,128)(2,1)S(1)} collective-permute-done((bf16[512,256]{1,0:T(8,128)(2,1)S(1)}, bf16[512,256]{1,0:T(8,128)(2,1)S(1)}, u32[]{:S(2)}, u32[]{:S(2)}) %collective-permute-start.27) | collective-permute-done | bytes 262176 | tf_op jit(solution)/shard_map/ppermute | solution.py:43
  24.0 1.6 %copy-done.1 = f32[512,1024]{1,0:T(8,128)S(1)} copy-done((f32[512,1024]{1,0:T(8,128)S(1)}, f32[512,1024]{1,0:T(8,128)}, u32[]{:S(2)}) %copy-start.1) | copy-done | bytes 2097176
  25.6 1.1 partial.1
  27.1 11.7 %collective-permute-done.28.other_ref = f32[512,128]{1,0:T(8,128)S(1)} collective-permute-done((f32[512,128]{1,0:T(8,128)S(1)}, f32[512,128]{1,0:T(8,128)S(1)}, u32[]{:S(2)}, u32[]{:S(2)}) %collective-permute-start.28) | collective-permute-done | bytes 262176 | tf_op jit(solution)/shard_map/ppermute | solution.py:43
  39.6 1.2 collective-permute-start.29
  40.7 2.7 %collective-permute-done.29.refs_1_ = bf16[512,128]{1,0:T(8,128)(2,1)S(1)} collective-permute-done((bf16[512,128]{1,0:T(8,128)(2,1)S(1)}, bf16[512,128]{1,0:T(8,128)(2,1)S(1)}, u32[]{:S(2)}, u32[]{:S(2)}) %collective-permute-start.29) | collective-permute-done | bytes 131104 | tf_op jit(solution)/shard_map/ppermute | solution.py:43
  43.4 1.7 %collective-permute-start.30 = (bf16[512,128]{1,0:T(8,128)(2,1)S(1)}, bf16[512,128]{1,0:T(8,128)(2,1)S(1)}, u32[]{:S(2)}, u32[]{:S(2)}) collective-permute-start(bf16[512,128]{1,0:T(8,128)(2,1)S(1)} %get-tuple-element.23.refs_0_), channel_id=1, source_target_pairs={{0,96},{16,112},{32,0},{48,16},{64,32},{80,48},{96,64},{112,80},{1... | collective-permute-start | bytes 393224 | tf_op jit(solution)/shard_map/ppermute | solution.py:43
  45.0 2.2 %collective-permute-done.30.refs_2_ = bf16[512,128]{1,0:T(8,128)(2,1)S(1)} collective-permute-done((bf16[512,128]{1,0:T(8,128)(2,1)S(1)}, bf16[512,128]{1,0:T(8,128)(2,1)S(1)}, u32[]{:S(2)}, u32[]{:S(2)}) %collective-permute-start.30) | collective-permute-done | bytes 131104 | tf_op jit(solution)/shard_map/ppermute | solution.py:43
  47.2 2.6 %collective-permute-start.32 = (bf16[512,128]{1,0:T(8,128)(2,1)S(1)}, bf16[512,128]{1,0:T(8,128)(2,1)S(1)}, u32[]{:S(2)}, u32[]{:S(2)}) collective-permute-start(bf16[512,128]{1,0:T(8,128)(2,1)S(1)} %get-tuple-element.23.refs_0_), channel_id=1, source_target_pairs={{0,64},{16,80},{32,96},{48,112},{64,0},{80,16},{96,32},{112,48},{1... | collective-permute-start | bytes 393224 | tf_op jit(solution)/shard_map/ppermute | solution.py:43
  50.7 1.8 %collective-permute-start.31 = (bf16[512,128]{1,0:T(8,128)(2,1)S(1)}, bf16[512,128]{1,0:T(8,128)(2,1)S(1)}, u32[]{:S(2)}, u32[]{:S(2)}) collective-permute-start(bf16[512,128]{1,0:T(8,128)(2,1)S(1)} %collective-permute-done.29.refs_1_), channel_id=1, source_target_pairs={{0,96},{16,112},{32,0},{48,16},{64,32},{80,48},{96,64},{112,80},{1... | collective-permute-start | bytes 393224 | tf_op jit(solution)/shard_map/ppermute | solution.py:43
  52.6 2.6 %collective-permute-start.33 = (bf16[512,128]{1,0:T(8,128)(2,1)S(1)}, bf16[512,128]{1,0:T(8,128)(2,1)S(1)}, u32[]{:S(2)}, u32[]{:S(2)}) collective-permute-start(bf16[512,128]{1,0:T(8,128)(2,1)S(1)} %collective-permute-done.29.refs_1_), channel_id=1, source_target_pairs={{0,64},{16,80},{32,96},{48,112},{64,0},{80,16},{96,32},{112,48},{1... | collective-permute-start | bytes 393224 | tf_op jit(solution)/shard_map/ppermute | solution.py:43
  56.5 0.9 collective-permute-start.1
  57.5 1.8 %collective-permute-done.33.refs_5_ = bf16[512,128]{1,0:T(8,128)(2,1)S(1)} collective-permute-done((bf16[512,128]{1,0:T(8,128)(2,1)S(1)}, bf16[512,128]{1,0:T(8,128)(2,1)S(1)}, u32[]{:S(2)}, u32[]{:S(2)}) %collective-permute-start.33) | collective-permute-done | bytes 131104 | tf_op jit(solution)/shard_map/ppermute | solution.py:43
  59.5 2.5 %collective-permute-done.35.refs_7_ = bf16[512,128]{1,0:T(8,128)(2,1)S(1)} collective-permute-done((bf16[512,128]{1,0:T(8,128)(2,1)S(1)}, bf16[512,128]{1,0:T(8,128)(2,1)S(1)}, u32[]{:S(2)}, u32[]{:S(2)}) %collective-permute-start.35) | collective-permute-done | bytes 131104 | tf_op jit(solution)/shard_map/ppermute | solution.py:43
  62.0 7.2 %collective-permute-start.22 = (bf16[512,1024]{1,0:T(8,128)(2,1)S(1)}, bf16[512,1024]{1,0:T(8,128)(2,1)S(1)}, u32[]{:S(2)}, u32[]{:S(2)}) collective-permute-start(bf16[512,1024]{1,0:T(8,128)(2,1)S(1)} %collective-permute-done.11.refs_3_), channel_id=1, source_target_pairs={{0,1},{1,0},{2,3},{3,2},{4,5},{5,4},{6,7},{7,6},{8,9},{9,8},{10,11... | collective-permute-start | bytes 3145736 | tf_op jit(solution)/shard_map/ppermute | solution.py:39
  69.3 1.7 %collective-permute-start.16 = (bf16[256,1024]{1,0:T(8,128)(2,1)S(1)}, bf16[256,1024]{1,0:T(8,128)(2,1)S(1)}, u32[]{:S(2)}, u32[]{:S(2)}) collective-permute-start(bf16[256,1024]{1,0:T(8,128)(2,1)S(1)} %get-tuple-element.25), channel_id=1, source_target_pairs={{0,2},{1,3},{2,0},{3,1},{4,6},{5,7},{6,4},{7,5},{8,10},{9,11},{10,... | collective-permute-start | bytes 1572872 | tf_op jit(solution)/shard_map/ppermute | solution.py:39
  71.0 1.2 collective-permute-start.19
  72.3 9.2 %collective-permute-start.23 = (bf16[512,1024]{1,0:T(8,128)(2,1)S(1)}, bf16[512,1024]{1,0:T(8,128)(2,1)S(1)}, u32[]{:S(2)}, u32[]{:S(2)}) collective-permute-start(bf16[512,1024]{1,0:T(8,128)(2,1)S(1)} %collective-permute-done.7.refs_5_), channel_id=1, source_target_pairs={{0,1},{1,0},{2,3},{3,2},{4,5},{5,4},{6,7},{7,6},{8,9},{9,8},{10,11... | collective-permute-start | bytes 3145736 | tf_op jit(solution)/shard_map/ppermute | solution.py:39
  81.6 1.8 %collective-permute-start.24 = (bf16[512,1024]{1,0:T(8,128)(2,1)S(1)}, bf16[512,1024]{1,0:T(8,128)(2,1)S(1)}, u32[]{:S(2)}, u32[]{:S(2)}) collective-permute-start(bf16[512,1024]{1,0:T(8,128)(2,1)S(1)} %collective-permute-done.refs_7_), channel_id=1, source_target_pairs={{0,1},{1,0},{2,3},{3,2},{4,5},{5,4},{6,7},{7,6},{8,9},{9,8},{10,11... | collective-permute-start | bytes 3145736 | tf_op jit(solution)/shard_map/ppermute | solution.py:39
  83.5 5.3 %collective-permute-done.19.refs_11_ = bf16[256,1024]{1,0:T(8,128)(2,1)} collective-permute-done((bf16[256,1024]{1,0:T(8,128)(2,1)S(1)}, bf16[256,1024]{1,0:T(8,128)(2,1)}, u32[]{:S(2)}, u32[]{:S(2)}) %collective-permute-start.19) | collective-permute-done | bytes 524320 | tf_op jit(solution)/shard_map/ppermute | solution.py:39
  88.7 4.2 %collective-permute-start.5 = (bf16[128,1024]{1,0:T(8,128)(2,1)S(1)}, bf16[128,1024]{1,0:T(8,128)(2,1)S(1)}, u32[]{:S(2)}, u32[]{:S(2)}) collective-permute-start(bf16[128,1024]{1,0:T(8,128)(2,1)S(1)} %slice.28), channel_id=1, source_target_pairs={{0,12},{1,13},{2,14},{3,15},{4,0},{5,1},{6,2},{7,3},{8,4},{9,5},{1... | collective-permute-start | bytes 786440 | tf_op jit(solution)/shard_map/ppermute | solution.py:39
  92.9 6.8 %collective-permute-start.14 = (bf16[256,1024]{1,0:T(8,128)(2,1)S(1)}, bf16[256,1024]{1,0:T(8,128)(2,1)S(1)}, u32[]{:S(2)}, u32[]{:S(2)}) collective-permute-start(bf16[256,1024]{1,0:T(8,128)(2,1)S(1)} %collective-permute-done.8.refs_3_), channel_id=1, source_target_pairs={{0,1},{1,0},{2,3},{3,2},{4,5},{5,4},{6,7},{7,6},{8,9},{9,8},{10,11... | collective-permute-start | bytes 1572872 | tf_op jit(solution)/shard_map/ppermute | solution.py:39
  99.7 3.9 %collective-permute-start.15 = (bf16[256,1024]{1,0:T(8,128)(2,1)S(1)}, bf16[256,1024]{1,0:T(8,128)(2,1)S(1)}, u32[]{:S(2)}, u32[]{:S(2)}) collective-permute-start(bf16[256,1024]{1,0:T(8,128)(2,1)S(1)} %collective-permute-done.1.refs_5_), channel_id=1, source_target_pairs={{0,1},{1,0},{2,3},{3,2},{4,5},{5,4},{6,7},{7,6},{8,9},{9,8},{10,11... | collective-permute-start | bytes 1572872 | tf_op jit(solution)/shard_map/ppermute | solution.py:39
  103.6 1.7 %collective-permute-start.9 = (bf16[256,1024]{1,0:T(8,128)(2,1)S(1)}, bf16[256,1024]{1,0:T(8,128)(2,1)S(1)}, u32[]{:S(2)}, u32[]{:S(2)}) collective-permute-start(bf16[256,1024]{1,0:T(8,128)(2,1)S(1)} %collective-permute-done.8.refs_3_), channel_id=1, source_target_pairs={{0,2},{1,3},{2,0},{3,1},{4,6},{5,7},{6,4},{7,5},{8,10},{9,11},{10,... | collective-permute-start | bytes 1572872 | tf_op jit(solution)/shard_map/ppermute | solution.py:39
  105.3 4.6 %copy-done = bf16[1,768,8192]{2,1,0:T(8,128)(2,1)S(1)} copy-done((bf16[1,768,8192]{2,1,0:T(8,128)(2,1)S(1)}, bf16[1,768,8192]{2,1,0:T(8,128)(2,1)}, u32[]{:S(2)}) %copy-start) | copy-done | bytes 12582936
  109.9 5.7 %norm.1 = (bf16[768,4096]{1,0:T(8,128)(2,1)S(1)}, bf16[768,3072]{1,0:T(8,128)(2,1)S(1)}, bf16[768,1024]{1,0:T(8,128)(2,1)S(1)}) custom-call(bf16[1,768,8192]{2,1,0:T(8,128)(2,1)S(1)} %copy-done, f32[1,8192]{1,0:T(1,128)S(1)} %copy-done.5), custom_call_target="tpu_custom_call" | custom-call | flops 50331648 | bytes 25165824 | tf_op jit(solution)/shard_map/norm/pallas_call | solution.py:84
  115.6 2.2 %copy-done.6 = bf16[768,3072]{1,0:T(8,128)(2,1)} copy-done((bf16[768,3072]{1,0:T(8,128)(2,1)}, bf16[768,3072]{1,0:T(8,128)(2,1)S(1)}, u32[]{:S(2)}) %copy-start.6) | copy-done | bytes 4718616
  117.8 1.3 assemble.1
  122.0 8.5 %project.3.refs_13_ = f32[768,1024]{1,0:T(8,128)S(1)} custom-call(bf16[768,4096]{1,0:T(8,128)(2,1)S(1)} %get-tuple-element.16.refs_0_, bf16[512,1024]{1,0:T(8,128)(2,1)S(1)} %bitcast.5, bf16[512,1024]{1,0:T(8,128)(2,1)S(1)} %collective-permute-done.21.refs_2_, bf16[512,1024]{1,0:T(8,128)(2,1)S(1)} %collective-permute-done.11.refs_3_, ...), custom_call_target="tpu_custom_call" | custom-call | flops 6442450944 | bytes 11010048 | tf_op jit(solution)/shard_map/project/pallas_call | solution.py:133
  130.5 1.7 %copy-done.25 = f32[768,1024]{1,0:T(8,128)} copy-done((f32[768,1024]{1,0:T(8,128)}, f32[768,1024]{1,0:T(8,128)S(1)}, u32[]{:S(2)}) %copy-start.25) | copy-done | bytes 3145752
  135.9 1.0 copy-done.12
  137.0 1.0 copy-done.14
  138.0 1.0 copy-done.16
  139.1 1.0 copy-done.18
  140.1 1.0 copy-done.20
  141.2 1.0 copy-done.22
  142.2 1.0 copy-done.24
  143.2 1.9 %copy-done.26 = f32[768,1024]{1,0:T(8,128)S(1)} copy-done((f32[768,1024]{1,0:T(8,128)S(1)}, f32[768,1024]{1,0:T(8,128)}, u32[]{:S(2)}) %copy-start.26) | copy-done | bytes 3145752
  145.1 7.5 %project.4.refs_7_ = f32[768,1024]{1,0:T(8,128)S(1)} custom-call(bf16[768,3072]{1,0:T(8,128)(2,1)S(1)} %copy-done.7, bf16[256,1024]{1,0:T(8,128)(2,1)S(1)} %copy-done.10, bf16[256,1024]{1,0:T(8,128)(2,1)S(1)} %copy-done.20, bf16[256,1024]{1,0:T(8,128)(2,1)S(1)} %collective-permute-done.8.refs_3_, bf16[256,1024]{1,0:T(8,128)(2,1)S(1)} %copy-done.14, ...), custom_call_target="tpu_custom_call" | custom-call | flops 4831838208 | bytes 9437184 | tf_op jit(solution)/shard_map/project/pallas_call | solution.py:133
  152.7 4.4 %project.5 = bf16[1,768,1024]{2,1,0:T(8,128)(2,1)} custom-call(bf16[768,1024]{1,0:T(8,128)(2,1)S(1)} %get-tuple-element.14.refs_0_, bf16[128,1024]{1,0:T(8,128)(2,1)S(1)} %collective-permute-done.2.refs_1_, bf16[128,1024]{1,0:T(8,128)(2,1)S(1)} %collective-permute-done.3.refs_2_, bf16[128,1024]{1,0:T(8,128)(2,1)S(1)} %collective-permute-done.5.refs_3_, ...), custom_call_target="tpu_custom_call" | custom-call | flops 1610612736 | bytes 6291456 | tf_op jit(solution)/shard_map/project/pallas_call | solution.py:133
  (91 shorter events, 10.7 us)
Async XLA Ops:
  1.9 36.9 %copy-start.4 = (bf16[512,128]{1,0:T(8,128)(2,1)S(1)}, bf16[512,128]{1,0:T(8,128)(2,1)}, u32[]{:S(2)}) copy-start(bf16[512,128]{1,0:T(8,128)(2,1)} %momentum_ref.1) | copy-start | bytes 393220
  2.0 11.3 %collective-permute-start.25 = (bf16[512,256]{1,0:T(8,128)(2,1)S(1)}, bf16[512,256]{1,0:T(8,128)(2,1)S(1)}, u32[]{:S(2)}, u32[]{:S(2)}) collective-permute-start(bf16[512,256]{1,0:T(8,128)(2,1)S(1)} %get-tuple-element.18), channel_id=1, source_target_pairs={{0,32},{16,48},{32,64},{48,80},{64,96},{80,112},{96,0},{112,16},{1... | collective-permute-start | bytes 786440 | tf_op jit(solution)/shard_map/ppermute | solution.py:43
  4.2 45.6 %collective-permute-start.7 = (bf16[512,1024]{1,0:T(8,128)(2,1)}, bf16[512,1024]{1,0:T(8,128)(2,1)S(1)}, u32[]{:S(2)}, u32[]{:S(2)}) collective-permute-start(bf16[512,1024]{1,0:T(8,128)(2,1)} %bitcast.1), channel_id=1, source_target_pairs={{0,12},{1,13},{2,14},{3,15},{4,0},{5,1},{6,2},{7,3},{8,4},{9,5},{1... | collective-permute-start | bytes 3145736 | tf_op jit(solution)/shard_map/ppermute | solution.py:39
  8.0 42.7 %collective-permute-start = (bf16[512,1024]{1,0:T(8,128)(2,1)}, bf16[512,1024]{1,0:T(8,128)(2,1)S(1)}, u32[]{:S(2)}, u32[]{:S(2)}) collective-permute-start(bf16[512,1024]{1,0:T(8,128)(2,1)} %bitcast.2), channel_id=1, source_target_pairs={{0,2},{1,3},{2,0},{3,1},{4,6},{5,7},{6,4},{7,5},{8,10},{9,11},{10,... | collective-permute-start | bytes 3145736 | tf_op jit(solution)/shard_map/ppermute | solution.py:39
  10.7 45.8 %collective-permute-start.11 = (bf16[512,1024]{1,0:T(8,128)(2,1)}, bf16[512,1024]{1,0:T(8,128)(2,1)S(1)}, u32[]{:S(2)}, u32[]{:S(2)}) collective-permute-start(bf16[512,1024]{1,0:T(8,128)(2,1)} %bitcast.3), channel_id=1, source_target_pairs={{0,4},{1,5},{2,6},{3,7},{4,8},{5,9},{6,10},{7,11},{8,12},{9,13},{1... | collective-permute-start | bytes 3145736 | tf_op jit(solution)/shard_map/ppermute | solution.py:39
  10.7 7.8 %collective-permute-start.26 = (bf16[512,256]{1,0:T(8,128)(2,1)S(1)}, bf16[512,256]{1,0:T(8,128)(2,1)S(1)}, u32[]{:S(2)}, u32[]{:S(2)}) collective-permute-start(bf16[512,256]{1,0:T(8,128)(2,1)S(1)} %get-tuple-element.19), channel_id=1, source_target_pairs={{0,64},{16,80},{32,96},{48,112},{64,0},{80,16},{96,32},{112,48},{1... | collective-permute-start | bytes 786440 | tf_op jit(solution)/shard_map/ppermute | solution.py:43
  13.3 10.7 %collective-permute-start.27 = (bf16[512,256]{1,0:T(8,128)(2,1)S(1)}, bf16[512,256]{1,0:T(8,128)(2,1)S(1)}, u32[]{:S(2)}, u32[]{:S(2)}) collective-permute-start(bf16[512,256]{1,0:T(8,128)(2,1)S(1)} %get-tuple-element.20), channel_id=1, source_target_pairs={{0,96},{16,112},{32,0},{48,16},{64,32},{80,48},{96,64},{112,80},{1... | collective-permute-start | bytes 786440 | tf_op jit(solution)/shard_map/ppermute | solution.py:43
  18.5 43.5 %collective-permute-start.21 = (bf16[512,1024]{1,0:T(8,128)(2,1)}, bf16[512,1024]{1,0:T(8,128)(2,1)S(1)}, u32[]{:S(2)}, u32[]{:S(2)}) collective-permute-start(bf16[512,1024]{1,0:T(8,128)(2,1)} %bitcast.4), channel_id=1, source_target_pairs={{0,1},{1,0},{2,3},{3,2},{4,5},{5,4},{6,7},{7,6},{8,9},{9,8},{10,11... | collective-permute-start | bytes 3145736 | tf_op jit(solution)/shard_map/ppermute | solution.py:39
  25.6 13.2 %copy-start.2 = (f32[512,1024]{1,0:T(8,128)S(1)}, f32[512,1024]{1,0:T(8,128)}, u32[]{:S(2)}) copy-start(f32[512,1024]{1,0:T(8,128)} %snapshot_ref.3) | copy-start | bytes 6291460
  26.7 12.0 %collective-permute-start.28 = (f32[512,128]{1,0:T(8,128)S(1)}, f32[512,128]{1,0:T(8,128)S(1)}, u32[]{:S(2)}, u32[]{:S(2)}) collective-permute-start(f32[512,128]{1,0:T(8,128)S(1)} %get-tuple-element.22), channel_id=1, source_target_pairs={{0,16},{16,0},{32,48},{48,32},{64,80},{80,64},{96,112},{112,96},{1... | collective-permute-start | bytes 786440 | tf_op jit(solution)/shard_map/ppermute | solution.py:43
  39.5 65.8 %copy-start.5 = (f32[1,8192]{1,0:T(1,128)S(1)}, f32[1,8192]{1,0:T(1,128)}, u32[]{:S(2)}) copy-start(f32[1,8192]{1,0:T(1,128)} %gain_ref.1) | copy-start | bytes 98308
  39.6 3.8 %collective-permute-start.29 = (bf16[512,128]{1,0:T(8,128)(2,1)S(1)}, bf16[512,128]{1,0:T(8,128)(2,1)S(1)}, u32[]{:S(2)}, u32[]{:S(2)}) collective-permute-start(bf16[512,128]{1,0:T(8,128)(2,1)S(1)} %get-tuple-element.23.refs_0_), channel_id=1, source_target_pairs={{0,16},{16,0},{32,48},{48,32},{64,80},{80,64},{96,112},{112,96},{1... | collective-permute-start | bytes 393224 | tf_op jit(solution)/shard_map/ppermute | solution.py:43
  43.4 3.8 %collective-permute-start.30 = (bf16[512,128]{1,0:T(8,128)(2,1)S(1)}, bf16[512,128]{1,0:T(8,128)(2,1)S(1)}, u32[]{:S(2)}, u32[]{:S(2)}) collective-permute-start(bf16[512,128]{1,0:T(8,128)(2,1)S(1)} %get-tuple-element.23.refs_0_), channel_id=1, source_target_pairs={{0,96},{16,112},{32,0},{48,16},{64,32},{80,48},{96,64},{112,80},{1... | collective-permute-start | bytes 393224 | tf_op jit(solution)/shard_map/ppermute | solution.py:43
  47.2 5.4 %collective-permute-start.32 = (bf16[512,128]{1,0:T(8,128)(2,1)S(1)}, bf16[512,128]{1,0:T(8,128)(2,1)S(1)}, u32[]{:S(2)}, u32[]{:S(2)}) collective-permute-start(bf16[512,128]{1,0:T(8,128)(2,1)S(1)} %get-tuple-element.23.refs_0_), channel_id=1, source_target_pairs={{0,64},{16,80},{32,96},{48,112},{64,0},{80,16},{96,32},{112,48},{1... | collective-permute-start | bytes 393224 | tf_op jit(solution)/shard_map/ppermute | solution.py:43
  49.8 5.4 %collective-permute-start.34 = (bf16[512,128]{1,0:T(8,128)(2,1)S(1)}, bf16[512,128]{1,0:T(8,128)(2,1)S(1)}, u32[]{:S(2)}, u32[]{:S(2)}) collective-permute-start(bf16[512,128]{1,0:T(8,128)(2,1)S(1)} %get-tuple-element.23.refs_0_), channel_id=1, source_target_pairs={{0,32},{16,48},{32,64},{48,80},{64,96},{80,112},{96,0},{112,16},{1... | collective-permute-start | bytes 393224 | tf_op jit(solution)/shard_map/ppermute | solution.py:43
  50.7 5.3 %collective-permute-start.31 = (bf16[512,128]{1,0:T(8,128)(2,1)S(1)}, bf16[512,128]{1,0:T(8,128)(2,1)S(1)}, u32[]{:S(2)}, u32[]{:S(2)}) collective-permute-start(bf16[512,128]{1,0:T(8,128)(2,1)S(1)} %collective-permute-done.29.refs_1_), channel_id=1, source_target_pairs={{0,96},{16,112},{32,0},{48,16},{64,32},{80,48},{96,64},{112,80},{1... | collective-permute-start | bytes 393224 | tf_op jit(solution)/shard_map/ppermute | solution.py:43
  52.6 6.7 %collective-permute-start.33 = (bf16[512,128]{1,0:T(8,128)(2,1)S(1)}, bf16[512,128]{1,0:T(8,128)(2,1)S(1)}, u32[]{:S(2)}, u32[]{:S(2)}) collective-permute-start(bf16[512,128]{1,0:T(8,128)(2,1)S(1)} %collective-permute-done.29.refs_1_), channel_id=1, source_target_pairs={{0,64},{16,80},{32,96},{48,112},{64,0},{80,16},{96,32},{112,48},{1... | collective-permute-start | bytes 393224 | tf_op jit(solution)/shard_map/ppermute | solution.py:43
  55.2 6.8 %collective-permute-start.35 = (bf16[512,128]{1,0:T(8,128)(2,1)S(1)}, bf16[512,128]{1,0:T(8,128)(2,1)S(1)}, u32[]{:S(2)}, u32[]{:S(2)}) collective-permute-start(bf16[512,128]{1,0:T(8,128)(2,1)S(1)} %collective-permute-done.29.refs_1_), channel_id=1, source_target_pairs={{0,32},{16,48},{32,64},{48,80},{64,96},{80,112},{96,0},{112,16},{1... | collective-permute-start | bytes 393224 | tf_op jit(solution)/shard_map/ppermute | solution.py:43
  56.0 13.3 %collective-permute-start.8 = (bf16[256,1024]{1,0:T(8,128)(2,1)S(1)}, bf16[256,1024]{1,0:T(8,128)(2,1)S(1)}, u32[]{:S(2)}, u32[]{:S(2)}) collective-permute-start(bf16[256,1024]{1,0:T(8,128)(2,1)S(1)} %slice.29), channel_id=1, source_target_pairs={{0,12},{1,13},{2,14},{3,15},{4,0},{5,1},{6,2},{7,3},{8,4},{9,5},{1... | collective-permute-start | bytes 1572872 | tf_op jit(solution)/shard_map/ppermute | solution.py:39
  56.5 14.5 %collective-permute-start.1 = (bf16[256,1024]{1,0:T(8,128)(2,1)S(1)}, bf16[256,1024]{1,0:T(8,128)(2,1)S(1)}, u32[]{:S(2)}, u32[]{:S(2)}) collective-permute-start(bf16[256,1024]{1,0:T(8,128)(2,1)S(1)} %slice.26), channel_id=1, source_target_pairs={{0,4},{1,5},{2,6},{3,7},{4,8},{5,9},{6,10},{7,11},{8,12},{9,13},{1... | collective-permute-start | bytes 1572872 | tf_op jit(solution)/shard_map/ppermute | solution.py:39
  59.3 13.0 %collective-permute-start.4 = (bf16[256,1024]{1,0:T(8,128)(2,1)S(1)}, bf16[256,1024]{1,0:T(8,128)(2,1)S(1)}, u32[]{:S(2)}, u32[]{:S(2)}) collective-permute-start(bf16[256,1024]{1,0:T(8,128)(2,1)S(1)} %slice.26), channel_id=1, source_target_pairs={{0,12},{1,13},{2,14},{3,15},{4,0},{5,1},{6,2},{7,3},{8,4},{9,5},{1... | collective-permute-start | bytes 1572872 | tf_op jit(solution)/shard_map/ppermute | solution.py:39
  62.0 19.5 %collective-permute-start.12 = (bf16[256,1024]{1,0:T(8,128)(2,1)S(1)}, bf16[256,1024]{1,0:T(8,128)(2,1)S(1)}, u32[]{:S(2)}, u32[]{:S(2)}) collective-permute-start(bf16[256,1024]{1,0:T(8,128)(2,1)S(1)} %get-tuple-element.26), channel_id=1, source_target_pairs={{0,4},{1,5},{2,6},{3,7},{4,8},{5,9},{6,10},{7,11},{8,12},{9,13},{1... | collective-permute-start | bytes 1572872 | tf_op jit(solution)/shard_map/ppermute | solution.py:39
  62.0 41.6 %collective-permute-start.22 = (bf16[512,1024]{1,0:T(8,128)(2,1)S(1)}, bf16[512,1024]{1,0:T(8,128)(2,1)S(1)}, u32[]{:S(2)}, u32[]{:S(2)}) collective-permute-start(bf16[512,1024]{1,0:T(8,128)(2,1)S(1)} %collective-permute-done.11.refs_3_), channel_id=1, source_target_pairs={{0,1},{1,0},{2,3},{3,2},{4,5},{5,4},{6,7},{7,6},{8,9},{9,8},{10,11... | collective-permute-start | bytes 3145736 | tf_op jit(solution)/shard_map/ppermute | solution.py:39
  69.3 14.1 %collective-permute-start.16 = (bf16[256,1024]{1,0:T(8,128)(2,1)S(1)}, bf16[256,1024]{1,0:T(8,128)(2,1)S(1)}, u32[]{:S(2)}, u32[]{:S(2)}) collective-permute-start(bf16[256,1024]{1,0:T(8,128)(2,1)S(1)} %get-tuple-element.25), channel_id=1, source_target_pairs={{0,2},{1,3},{2,0},{3,1},{4,6},{5,7},{6,4},{7,5},{8,10},{9,11},{10,... | collective-permute-start | bytes 1572872 | tf_op jit(solution)/shard_map/ppermute | solution.py:39
  71.0 17.7 %collective-permute-start.19 = (bf16[256,1024]{1,0:T(8,128)(2,1)S(1)}, bf16[256,1024]{1,0:T(8,128)(2,1)}, u32[]{:S(2)}, u32[]{:S(2)}) collective-permute-start(bf16[256,1024]{1,0:T(8,128)(2,1)S(1)} %slice.29), channel_id=1, source_target_pairs={{0,2},{1,3},{2,0},{3,1},{4,6},{5,7},{6,4},{7,5},{8,10},{9,11},{10,... | collective-permute-start | bytes 1572872 | tf_op jit(solution)/shard_map/ppermute | solution.py:39
  72.3 46.7 %collective-permute-start.23 = (bf16[512,1024]{1,0:T(8,128)(2,1)S(1)}, bf16[512,1024]{1,0:T(8,128)(2,1)S(1)}, u32[]{:S(2)}, u32[]{:S(2)}) collective-permute-start(bf16[512,1024]{1,0:T(8,128)(2,1)S(1)} %collective-permute-done.7.refs_5_), channel_id=1, source_target_pairs={{0,1},{1,0},{2,3},{3,2},{4,5},{5,4},{6,7},{7,6},{8,9},{9,8},{10,11... | collective-permute-start | bytes 3145736 | tf_op jit(solution)/shard_map/ppermute | solution.py:39
  81.6 37.8 %copy-start.9 = (bf16[256,1024]{1,0:T(8,128)(2,1)}, bf16[256,1024]{1,0:T(8,128)(2,1)S(1)}, u32[]{:S(2)}) copy-start(bf16[256,1024]{1,0:T(8,128)(2,1)S(1)} %collective-permute-done.12.refs_1_) | copy-start | bytes 1572868
  81.6 37.8 %collective-permute-start.24 = (bf16[512,1024]{1,0:T(8,128)(2,1)S(1)}, bf16[512,1024]{1,0:T(8,128)(2,1)S(1)}, u32[]{:S(2)}, u32[]{:S(2)}) collective-permute-start(bf16[512,1024]{1,0:T(8,128)(2,1)S(1)} %collective-permute-done.refs_7_), channel_id=1, source_target_pairs={{0,1},{1,0},{2,3},{3,2},{4,5},{5,4},{6,7},{7,6},{8,9},{9,8},{10,11... | collective-permute-start | bytes 3145736 | tf_op jit(solution)/shard_map/ppermute | solution.py:39
  83.4 36.2 %copy-start.11 = (bf16[256,1024]{1,0:T(8,128)(2,1)}, bf16[256,1024]{1,0:T(8,128)(2,1)S(1)}, u32[]{:S(2)}) copy-start(bf16[256,1024]{1,0:T(8,128)(2,1)S(1)} %collective-permute-done.16.refs_7_) | copy-start | bytes 1572868
  83.4 9.5 %collective-permute-start.2 = (bf16[128,1024]{1,0:T(8,128)(2,1)S(1)}, bf16[128,1024]{1,0:T(8,128)(2,1)S(1)}, u32[]{:S(2)}, u32[]{:S(2)}) collective-permute-start(bf16[128,1024]{1,0:T(8,128)(2,1)S(1)} %slice.27), channel_id=1, source_target_pairs={{0,4},{1,5},{2,6},{3,7},{4,8},{5,9},{6,10},{7,11},{8,12},{9,13},{1... | collective-permute-start | bytes 786440 | tf_op jit(solution)/shard_map/ppermute | solution.py:39
  88.7 10.9 %collective-permute-start.5 = (bf16[128,1024]{1,0:T(8,128)(2,1)S(1)}, bf16[128,1024]{1,0:T(8,128)(2,1)S(1)}, u32[]{:S(2)}, u32[]{:S(2)}) collective-permute-start(bf16[128,1024]{1,0:T(8,128)(2,1)S(1)} %slice.28), channel_id=1, source_target_pairs={{0,12},{1,13},{2,14},{3,15},{4,0},{5,1},{6,2},{7,3},{8,4},{9,5},{1... | collective-permute-start | bytes 786440 | tf_op jit(solution)/shard_map/ppermute | solution.py:39
  92.9 26.7 %collective-permute-start.14 = (bf16[256,1024]{1,0:T(8,128)(2,1)S(1)}, bf16[256,1024]{1,0:T(8,128)(2,1)S(1)}, u32[]{:S(2)}, u32[]{:S(2)}) collective-permute-start(bf16[256,1024]{1,0:T(8,128)(2,1)S(1)} %collective-permute-done.8.refs_3_), channel_id=1, source_target_pairs={{0,1},{1,0},{2,3},{3,2},{4,5},{5,4},{6,7},{7,6},{8,9},{9,8},{10,11... | collective-permute-start | bytes 1572872 | tf_op jit(solution)/shard_map/ppermute | solution.py:39
  99.7 21.0 %collective-permute-start.15 = (bf16[256,1024]{1,0:T(8,128)(2,1)S(1)}, bf16[256,1024]{1,0:T(8,128)(2,1)S(1)}, u32[]{:S(2)}, u32[]{:S(2)}) collective-permute-start(bf16[256,1024]{1,0:T(8,128)(2,1)S(1)} %collective-permute-done.1.refs_5_), channel_id=1, source_target_pairs={{0,1},{1,0},{2,3},{3,2},{4,5},{5,4},{6,7},{7,6},{8,9},{9,8},{10,11... | collective-permute-start | bytes 1572872 | tf_op jit(solution)/shard_map/ppermute | solution.py:39
  103.6 18.1 %collective-permute-start.9 = (bf16[256,1024]{1,0:T(8,128)(2,1)S(1)}, bf16[256,1024]{1,0:T(8,128)(2,1)S(1)}, u32[]{:S(2)}, u32[]{:S(2)}) collective-permute-start(bf16[256,1024]{1,0:T(8,128)(2,1)S(1)} %collective-permute-done.8.refs_3_), channel_id=1, source_target_pairs={{0,2},{1,3},{2,0},{3,1},{4,6},{5,7},{6,4},{7,5},{8,10},{9,11},{10,... | collective-permute-start | bytes 1572872 | tf_op jit(solution)/shard_map/ppermute | solution.py:39
  105.3 4.6 %copy-start = (bf16[1,768,8192]{2,1,0:T(8,128)(2,1)S(1)}, bf16[1,768,8192]{2,1,0:T(8,128)(2,1)}, u32[]{:S(2)}) copy-start(bf16[1,768,8192]{2,1,0:T(8,128)(2,1)} %tokens_ref.1) | copy-start | bytes 37748740
  109.9 12.1 %copy-start.8 = (bf16[1,512,1024]{2,1,0:T(8,128)(2,1)S(1)}, bf16[1,512,1024]{2,1,0:T(8,128)(2,1)}, u32[]{:S(2)}) copy-start(bf16[1,512,1024]{2,1,0:T(8,128)(2,1)} %param.8) | copy-start | bytes 3145732
  115.6 2.2 %copy-start.6 = (bf16[768,3072]{1,0:T(8,128)(2,1)}, bf16[768,3072]{1,0:T(8,128)(2,1)S(1)}, u32[]{:S(2)}) copy-start(bf16[768,3072]{1,0:T(8,128)(2,1)S(1)} %get-tuple-element.15.refs_0_) | copy-start | bytes 14155780
  119.1 13.2 %collective-permute-start.18 = (bf16[256,1024]{1,0:T(8,128)(2,1)S(1)}, bf16[256,1024]{1,0:T(8,128)(2,1)S(1)}, u32[]{:S(2)}, u32[]{:S(2)}) collective-permute-start(bf16[256,1024]{1,0:T(8,128)(2,1)S(1)} %collective-permute-done.4.refs_9_), channel_id=1, source_target_pairs={{0,1},{1,0},{2,3},{3,2},{4,5},{5,4},{6,7},{7,6},{8,9},{9,8},{10,11... | collective-permute-start | bytes 1572872 | tf_op jit(solution)/shard_map/ppermute | solution.py:39
  119.4 13.9 %collective-permute-start.13 = (bf16[256,1024]{1,0:T(8,128)(2,1)S(1)}, bf16[256,1024]{1,0:T(8,128)(2,1)S(1)}, u32[]{:S(2)}, u32[]{:S(2)}) collective-permute-start(bf16[256,1024]{1,0:T(8,128)(2,1)S(1)} %collective-permute-done.12.refs_1_), channel_id=1, source_target_pairs={{0,1},{1,0},{2,3},{3,2},{4,5},{5,4},{6,7},{7,6},{8,9},{9,8},{10,11... | collective-permute-start | bytes 1572872 | tf_op jit(solution)/shard_map/ppermute | solution.py:39
  120.4 14.0 %collective-permute-start.17 = (bf16[256,1024]{1,0:T(8,128)(2,1)S(1)}, bf16[256,1024]{1,0:T(8,128)(2,1)S(1)}, u32[]{:S(2)}, u32[]{:S(2)}) collective-permute-start(bf16[256,1024]{1,0:T(8,128)(2,1)S(1)} %collective-permute-done.16.refs_7_), channel_id=1, source_target_pairs={{0,1},{1,0},{2,3},{3,2},{4,5},{5,4},{6,7},{7,6},{8,9},{9,8},{10,11... | collective-permute-start | bytes 1572872 | tf_op jit(solution)/shard_map/ppermute | solution.py:39
  121.5 13.6 %collective-permute-start.20 = (bf16[256,1024]{1,0:T(8,128)(2,1)}, bf16[256,1024]{1,0:T(8,128)(2,1)S(1)}, u32[]{:S(2)}, u32[]{:S(2)}) collective-permute-start(bf16[256,1024]{1,0:T(8,128)(2,1)} %collective-permute-done.19.refs_11_), channel_id=1, source_target_pairs={{0,1},{1,0},{2,3},{3,2},{4,5},{5,4},{6,7},{7,6},{8,9},{9,8},{10,11... | collective-permute-start | bytes 1572872 | tf_op jit(solution)/shard_map/ppermute | solution.py:39
  121.7 31.0 %collective-permute-start.10 = (bf16[256,1024]{1,0:T(8,128)(2,1)S(1)}, bf16[256,1024]{1,0:T(8,128)(2,1)S(1)}, u32[]{:S(2)}, u32[]{:S(2)}) collective-permute-start(bf16[256,1024]{1,0:T(8,128)(2,1)S(1)} %collective-permute-done.9.refs_5_), channel_id=1, source_target_pairs={{0,1},{1,0},{2,3},{3,2},{4,5},{5,4},{6,7},{7,6},{8,9},{9,8},{10,11... | collective-permute-start | bytes 1572872 | tf_op jit(solution)/shard_map/ppermute | solution.py:39
  122.0 13.9 %copy-start.7 = (bf16[768,3072]{1,0:T(8,128)(2,1)S(1)}, bf16[768,3072]{1,0:T(8,128)(2,1)}, u32[]{:S(2)}) copy-start(bf16[768,3072]{1,0:T(8,128)(2,1)} %copy-done.6) | copy-start | bytes 14155780
  122.0 13.9 %copy-start.10 = (bf16[256,1024]{1,0:T(8,128)(2,1)S(1)}, bf16[256,1024]{1,0:T(8,128)(2,1)}, u32[]{:S(2)}) copy-start(bf16[256,1024]{1,0:T(8,128)(2,1)} %copy-done.9) | copy-start | bytes 1572868
  130.5 1.7 %copy-start.25 = (f32[768,1024]{1,0:T(8,128)}, f32[768,1024]{1,0:T(8,128)S(1)}, u32[]{:S(2)}) copy-start(f32[768,1024]{1,0:T(8,128)S(1)} %project.3.refs_13_) | copy-start | bytes 9437188
  133.0 19.6 %collective-permute-start.3 = (bf16[128,1024]{1,0:T(8,128)(2,1)S(1)}, bf16[128,1024]{1,0:T(8,128)(2,1)S(1)}, u32[]{:S(2)}, u32[]{:S(2)}) collective-permute-start(bf16[128,1024]{1,0:T(8,128)(2,1)S(1)} %collective-permute-done.2.refs_1_), channel_id=1, source_target_pairs={{0,1},{1,0},{2,3},{3,2},{4,5},{5,4},{6,7},{7,6},{8,9},{9,8},{10,11... | collective-permute-start | bytes 786440 | tf_op jit(solution)/shard_map/ppermute | solution.py:39
  134.0 18.6 %collective-permute-start.6 = (bf16[128,1024]{1,0:T(8,128)(2,1)S(1)}, bf16[128,1024]{1,0:T(8,128)(2,1)S(1)}, u32[]{:S(2)}, u32[]{:S(2)}) collective-permute-start(bf16[128,1024]{1,0:T(8,128)(2,1)S(1)} %collective-permute-done.5.refs_3_), channel_id=1, source_target_pairs={{0,1},{1,0},{2,3},{3,2},{4,5},{5,4},{6,7},{7,6},{8,9},{9,8},{10,11... | collective-permute-start | bytes 786440 | tf_op jit(solution)/shard_map/ppermute | solution.py:39
  143.2 1.9 %copy-start.26 = (f32[768,1024]{1,0:T(8,128)S(1)}, f32[768,1024]{1,0:T(8,128)}, u32[]{:S(2)}) copy-start(f32[768,1024]{1,0:T(8,128)} %copy-done.25) | copy-start | bytes 9437188
  (15 other events, 14.9 us)

commit v2 on v0

v2 whole, which is shorter than its diff:
```python
import functools

import jax
import jax.numpy as jnp
from jax import lax
from jax.experimental import pallas as pl
from jax.experimental.pallas import tpu as pltpu
from jax.sharding import PartitionSpec as P

BLOCK = 128
DECAY = 0.9
RATE = 0.7
EPS = 1e-05
MIB = 1024 * 1024

Z, X, C = 4, 2, 2
Y, XL = 4, 2


def fsdp_perm(move):
    pairs = []
    for z in range(Z):
        for x in range(X):
            for c in range(C):
                to_z, to_x, to_c = move(z, x, c)
                pairs.append((z * 4 + x * 2 + c, (to_z % Z) * 4 + to_x * 2 + to_c))
    return pairs


def along_z(value):
    return lax.ppermute(
        value, "fsdp", fsdp_perm(lambda z, x, c: (z + 1 - 2 * c, x, c))
    )


def along_x(value):
    return lax.ppermute(value, "fsdp", fsdp_perm(lambda z, x, c: (z, 1 - x, c)))


def to_core(value):
    return lax.ppermute(value, "fsdp", fsdp_perm(lambda z, x, c: (z, x, 1 - c)))


def across_replicas(value, move):
    pairs = []
    for y in range(Y):
        for x in range(XL):
            to_y, to_x = move(y, x)
            pairs.append((y * XL + x, (to_y % Y) * XL + to_x))
    return lax.ppermute(value, "replica", pairs)


def cost(flops, nbytes):
    return pl.CostEstimate(flops=flops, bytes_accessed=nbytes, transcendentals=0)


def prepare_kernel(
    gain_hbm, next_hbm, weights_hbm, out_ref, low_ref, high_ref, *refs
):
    slice_refs, (gain_ref, next_ref, sems, slice_sems) = refs[:Y], refs[Y:]
    rows = next_ref.shape[0]
    side = BLOCK
    first = pl.multiple_of(lax.axis_index("fsdp") * rows, rows)
    copies = [
        pltpu.make_async_copy(
            gain_hbm.at[:, pl.ds(first, rows)], gain_ref, sems.at[rows // side]
        )
    ]
    for i in range(rows // side):
        at = slice(i * side, (i + 1) * side)
        copies.append(
            pltpu.make_async_copy(next_hbm.at[0, at, :], next_ref.at[at, :], sems.at[i])
        )
    y = lax.axis_index("replica") // XL
    width = slice_refs[0].shape[1]
    slice_copies = []
    for dy, slice_ref in enumerate(slice_refs):
        at = pl.multiple_of(((y + dy) % Y) * width, width)
        slice_copies.append(
            pltpu.make_async_copy(
                weights_hbm.at[0, :, pl.ds(at, width)], slice_ref, slice_sems.at[dy]
            )
        )
    for copy in copies + slice_copies:
        copy.start()
    eye = lax.broadcasted_iota(jnp.int32, (side, side), 0) == lax.broadcasted_iota(
        jnp.int32, (side, side), 1
    )
    copies[0].wait()
    for i in range(rows // side):
        at = slice(i * side, (i + 1) * side)
        gain = jnp.where(eye, gain_ref[:, at], 0.0)
        column = jnp.sum(gain, axis=1, keepdims=True)
        copies[1 + i].wait()
        block = (next_ref[at, :].astype(jnp.float32) * column).astype(jnp.bfloat16)
        out_ref[at, :] = block
        if i * side < rows // 2:
            low_ref[at, :] = block
        else:
            high_ref[i * side - rows // 2 : (i + 1) * side - rows // 2, :] = block
    for copy in slice_copies:
        copy.wait()


def prepare(gain, next_weights, weights):
    _, rows, columns = next_weights.shape
    hbm = pl.BlockSpec(memory_space=pltpu.HBM)
    shapes = [(rows, columns), (rows // 2, columns), (rows // 2, columns)]
    shapes += [(rows, columns // Y)] * Y
    operands = [gain, next_weights, weights]
    return pl.pallas_call(
        prepare_kernel,
        in_specs=[hbm] * 3,
        out_specs=[pl.BlockSpec(memory_space=pltpu.VMEM)] * len(shapes),
        out_shape=[jax.ShapeDtypeStruct(s, jnp.bfloat16) for s in shapes],
        scratch_shapes=[
            pltpu.VMEM((1, rows), jnp.float32),
            pltpu.VMEM((rows, columns), jnp.bfloat16),
            pltpu.SemaphoreType.DMA((rows // BLOCK + 1,)),
            pltpu.SemaphoreType.DMA((Y,)),
        ],
        compiler_params=pltpu.CompilerParams(vmem_limit_bytes=8 * MIB),
        cost_estimate=cost(rows * columns, 4 * rows * columns),
        name="prepare",
    )(*(pltpu.with_memory_space_constraint(v, pltpu.HBM) for v in operands))


def phase(values, after=()):
    spec = pl.BlockSpec(memory_space=pl.ANY)
    count = len(values)
    return pl.pallas_call(
        lambda *refs: None,
        in_specs=[spec] * (count + len(after)),
        out_specs=[spec] * count,
        out_shape=[jax.ShapeDtypeStruct(v.shape, v.dtype) for v in values],
        input_output_aliases={i: i for i in range(count)},
        compiler_params=pltpu.CompilerParams(vmem_limit_bytes=MIB),
        cost_estimate=cost(0, 0),
        name="phase",
    )(*values, *after)


def half_kernel(tokens_hbm, half_ref, sems):
    shards = sems.shape[0]
    width = half_ref.shape[1] // shards
    other = 1 - lax.axis_index("fsdp") % C
    copies = []
    for k in range(shards):
        at = pl.ds(pl.multiple_of((k * C + other) * width, width), width)
        to = pl.ds(k * width, width)
        copies.append(
            pltpu.make_async_copy(
                tokens_hbm.at[0, :, at], half_ref.at[:, to], sems.at[k]
            )
        )
    for copy in copies:
        copy.start()
    for copy in copies:
        copy.wait()


def load_kernel(tokens_hbm, tokens_ref, scale_ref, sems):
    _, rows, features = tokens_ref.shape
    parts = sems.shape[0]
    size, tile, width = rows // parts, 32, 512

    def copy(i):
        at = pl.ds(pl.multiple_of(i * size, size), size)
        return pltpu.make_async_copy(
            tokens_hbm.at[0, at, :], tokens_ref.at[0, at, :], sems.at[i]
        )

    for i in range(parts):
        copy(i).start()

    def part(i, carry):
        copy(i).wait()
        for k in range(size // tile):
            at = pl.ds(pl.multiple_of(i * size + k * tile, tile), tile)
            total = jnp.zeros((tile, width), jnp.float32)
            for j in range(features // width):
                value = tokens_ref[0, at, j * width : (j + 1) * width]
                value = value.astype(jnp.float32)
                total = total + value * value
            mean = jnp.sum(total, axis=1, keepdims=True) / features
            scale_ref[at, :] = jnp.broadcast_to(lax.rsqrt(mean + EPS), (tile, BLOCK))
        return carry

    lax.fori_loop(0, parts, part, 0)


def fetch(kernel, tokens, out_shapes, copies, name, after):
    spec = pl.BlockSpec(memory_space=pltpu.VMEM)

    def run(tokens_hbm, *refs):
        kernel(tokens_hbm, *refs[len(after) :])

    return pl.pallas_call(
        run,
        in_specs=[pl.BlockSpec(memory_space=pltpu.HBM)]
        + [pl.BlockSpec(memory_space=pl.ANY)] * len(after),
        out_specs=[spec] * len(out_shapes),
        out_shape=out_shapes,
        scratch_shapes=[pltpu.SemaphoreType.DMA((copies,))],
        compiler_params=pltpu.CompilerParams(vmem_limit_bytes=4 * MIB),
        cost_estimate=cost(tokens.size, 2 * tokens.size),
        name=name,
    )(pltpu.with_memory_space_constraint(tokens, pltpu.HBM), *after)


def project_kernel(places, rows, given, *refs):
    count = len(places)
    tokens_ref, half_ref, weight_refs = refs[0], refs[1], refs[2 : 2 + count]
    total_refs = refs[2 + count : 4 + count] if given else None
    out_ref, other_ref = refs[-2:]
    me = lax.axis_index("fsdp")
    z, x, c = me // 4, (me // 2) % 2, me % 2
    starts = []
    for step, dx, dc, first in places:
        block = ((z + (2 * c - 1) * step + Z) % Z) * 2 + (x + dx) % 2
        starts.append(
            (
                pl.multiple_of((block * 2 + c) * rows + first, BLOCK),
                pl.multiple_of(block * rows + first, BLOCK),
            )
        )
    tile = 256

    def column(n, carry):
        at = pl.ds(pl.multiple_of(n * tile, tile), tile)
        total = total_refs[0][:, at] if given else None
        other = total_refs[1][:, at] if given else None
        for (start, half_start), weight_ref in zip(starts, weight_refs):
            depth = weight_ref.shape[0]
            weight = weight_ref[:, at]
            part = jnp.dot(
                tokens_ref[0, :, pl.ds(start, depth)],
                weight,
                preferred_element_type=jnp.float32,
            )
            total = part if total is None else total + part
            part = jnp.dot(
                half_ref[:, pl.ds(half_start, depth)],
                weight,
                preferred_element_type=jnp.float32,
            )
            other = part if other is None else other + part
        out_ref[:, at] = total
        other_ref[:, at] = other.astype(other_ref.dtype)
        return carry

    lax.fori_loop(0, weight_refs[0].shape[1] // tile, column, 0)


def project(tokens, half, pieces, rows, totals=(), after=(), last=False):
    count = tokens.shape[1]
    columns = pieces[0][1].shape[1]
    operands = [tokens, half, *(w for _, w in pieces)]
    aliases = {len(operands) + i: i for i in range(2 - last)} if totals else {}
    operands += totals
    depth = sum(w.shape[0] for _, w in pieces)
    spec = pl.BlockSpec(memory_space=pltpu.VMEM)
    places = tuple(p for p, _ in pieces)
    return pl.pallas_call(
        functools.partial(project_kernel, places, rows, bool(totals)),
        in_specs=[spec] * len(operands)
        + [pl.BlockSpec(memory_space=pl.ANY)] * len(after),
        out_specs=[spec] * 2,
        out_shape=[
            jax.ShapeDtypeStruct((count, columns), jnp.float32),
            jax.ShapeDtypeStruct(
                (count, columns), jnp.bfloat16 if last else jnp.float32
            ),
        ],
        input_output_aliases=aliases,
        compiler_params=pltpu.CompilerParams(vmem_limit_bytes=6 * MIB),
        cost_estimate=cost(4 * count * depth * columns, 2 * columns * depth),
        name="project",
    )(*operands, *after)


def finish_kernel(places, rows, *refs):
    count = len(places)
    tokens_ref, weight_refs = refs[0], refs[1 : 1 + count]
    own_ref, other_ref, scale_ref = refs[1 + count : 4 + count]
    out_ref = refs[-1]
    me = lax.axis_index("fsdp")
    z, x, c = me // 4, (me // 2) % 2, me % 2
    starts = []
    for step, dx, dc, first in places:
        core = (c + dc) % 2
        shard = ((z + (2 * core - 1) * step + Z) % Z) * 4 + ((x + dx) % 2) * 2 + core
        starts.append(pl.multiple_of(shard * rows + first, BLOCK))
    tile = 256

    def column(n, carry):
        at = pl.ds(pl.multiple_of(n * tile, tile), tile)
        total = own_ref[:, at] + other_ref[:, at].astype(jnp.float32)
        for start, weight_ref in zip(starts, weight_refs):
            total = total + jnp.dot(
                tokens_ref[0, :, pl.ds(start, weight_ref.shape[0])],
                weight_ref[:, at],
                preferred_element_type=jnp.float32,
            )
        out_ref[0, :, at] = (total * scale_ref[:, :1]).astype(jnp.bfloat16)
        return carry

    lax.fori_loop(0, weight_refs[0].shape[1] // tile, column, 0)


def finish(tokens, pieces, rows, own, other, row_scale, after):
    count = tokens.shape[1]
    columns = own.shape[1]
    operands = [tokens, *(w for _, w in pieces), own, other, row_scale]
    depth = sum(w.shape[0] for _, w in pieces)
    spec = pl.BlockSpec(memory_space=pltpu.VMEM)
    places = tuple(p for p, _ in pieces)
    return pl.pallas_call(
        functools.partial(finish_kernel, places, rows),
        in_specs=[spec] * len(operands)
        + [pl.BlockSpec(memory_space=pl.ANY)] * len(after),
        out_specs=spec,
        out_shape=jax.ShapeDtypeStruct((1, count, columns), jnp.bfloat16),
        compiler_params=pltpu.CompilerParams(vmem_limit_bytes=6 * MIB),
        cost_estimate=cost(2 * count * depth * columns, 2 * columns * depth),
        name="finish",
    )(*operands, *after)


def scale_of(values):
    target = (jnp.max(jnp.abs(values), axis=1, keepdims=True) + 1e-06) / 448.0
    high = target.astype(jnp.bfloat16).astype(jnp.float32)
    low = (target - high).astype(jnp.bfloat16).astype(jnp.float32)
    return high + low


def rounded(values):
    scale = scale_of(values)
    return (values / scale).astype(jnp.bfloat16).astype(jnp.float32) * scale


def partial_kernel(snapshot_ref, *refs):
    weight_refs, (own_ref, other_ref) = refs[:-2], refs[-2:]
    me = lax.axis_index("replica")
    y, x = me // XL, me % XL
    for dx, out_ref in ((0, own_ref), (1, other_ref)):
        column = (x + dx) % XL
        at = pl.multiple_of((y * XL + column) * BLOCK, BLOCK)
        snapshot = snapshot_ref[:, pl.ds(at, BLOCK)]
        inside = pl.ds(pl.multiple_of(column * BLOCK, BLOCK), BLOCK)
        total = None
        for weight_ref in weight_refs:
            part = rounded(snapshot - weight_ref[:, inside].astype(jnp.float32))
            total = part if total is None else total + part
        out_ref[...] = total.astype(out_ref.dtype)


def update_kernel(snapshot_ref, momentum_ref, own_ref, other_ref, new_ref, velocity_ref):
    me = lax.axis_index("replica")
    at = pl.multiple_of(me * BLOCK, BLOCK)
    snapshot = snapshot_ref[:, pl.ds(at, BLOCK)]
    average = (own_ref[...] + other_ref[...].astype(jnp.float32)) / (Y * XL)
    velocity = (DECAY * momentum_ref[...].astype(jnp.float32) + average).astype(jnp.bfloat16)
    velocity_ref[...] = velocity
    updated = snapshot - RATE * (average + DECAY * velocity.astype(jnp.float32))
    new_ref[...] = rounded(updated).astype(jnp.bfloat16)


def join_kernel(left_ref, right_ref, out_ref):
    width = left_ref.shape[1]
    out_ref[:, :width] = left_ref[...]
    out_ref[:, width:] = right_ref[...]


def join(left, right, after=()):
    rows, columns = left.shape
    out = jax.ShapeDtypeStruct((rows, 2 * columns), left.dtype)
    return whole(join_kernel, out, "join", [left, right], after=after)


def assemble_kernel(*refs):
    pair_refs, (out_ref, done_ref) = refs[:-2], refs[-2:]
    me = lax.axis_index("replica")
    y, x = me // XL, me % XL
    for dy, pair_ref in enumerate(pair_refs):
        for dx in range(XL):
            owner = ((y + dy) % Y) * XL + (x + dx) % XL
            at = pl.multiple_of(owner * BLOCK, BLOCK)
            inside = slice(dx * BLOCK, (dx + 1) * BLOCK)
            out_ref[:, pl.ds(at, BLOCK)] = pair_ref[:, inside]
    done_ref[...] = jnp.zeros_like(done_ref)


def whole(kernel, out_shape, name, operands, after=()):
    spec = pl.BlockSpec(memory_space=pltpu.VMEM)
    nbytes = sum(v.size * v.dtype.itemsize for v in operands)
    count = len(operands)

    def run(*refs):
        kernel(*refs[:count], *refs[count + len(after) :])

    return pl.pallas_call(
        run,
        in_specs=[spec] * count + [pl.BlockSpec(memory_space=pl.ANY)] * len(after),
        out_specs=jax.tree.map(lambda _: spec, out_shape),
        out_shape=out_shape,
        compiler_params=pltpu.CompilerParams(vmem_limit_bytes=4 * MIB),
        cost_estimate=cost(8 * nbytes, 2 * nbytes),
        name=name,
    )(*operands, *after)


def body(tokens, gain, next_weights, weights, snapshot, momentum):
    shape = jax.ShapeDtypeStruct
    _, rows, columns = next_weights.shape
    half = rows // 2

    own, own_low, own_high, *slices = prepare(gain, next_weights, weights)

    ring_1 = along_z(own)
    low_0 = along_x(own_low)
    arrived = [
        across_replicas(slices[dy], lambda y, x, dy=dy: (y + dy, x))
        for dy in range(1, Y)
    ]
    count, features = tokens.shape[1:]
    (half_sent,) = fetch(
        half_kernel,
        tokens,
        [shape((count, features // C), tokens.dtype)],
        Z * X,
        "half",
        [own],
    )
    ring_1, low_0, own_high, half_sent = phase([ring_1, low_0, own_high, half_sent])

    ring_2 = along_z(ring_1)
    high_0 = along_x(own_high)
    tokens_half = to_core(half_sent)
    tokens, row_scale = fetch(
        load_kernel,
        tokens,
        [shape(tokens.shape, tokens.dtype), shape((count, BLOCK), jnp.float32)],
        12,
        "load",
        [ring_1],
    )
    own_sum, other_sum = whole(
        partial_kernel,
        [shape((rows, BLOCK), jnp.float32), shape((rows, BLOCK), jnp.bfloat16)],
        "partial",
        [snapshot, slices[0], *arrived],
        after=[row_scale],
    )
    other_sum = across_replicas(other_sum, lambda y, x: (y, 1 - x))
    ring_2, low_0, high_0, other_sum = phase([ring_2, low_0, high_0, other_sum])

    ring_3 = along_z(ring_2)
    low_1 = along_z(low_0)
    high_2 = along_x(ring_2[half:])
    new, velocity = whole(
        update_kernel,
        [shape((rows, BLOCK), jnp.bfloat16)] * 2,
        "update",
        [snapshot, momentum, own_sum, other_sum],
    )
    new_other = across_replicas(new, lambda y, x: (y, 1 - x))
    totals = project(
        tokens,
        tokens_half,
        [
            ((0, 0, 0, 0), own),
            ((1, 0, 0, 0), ring_1),
            ((2, 0, 0, 0), ring_2),
            ((0, 1, 0, 0), low_0),
            ((0, 1, 0, half), high_0),
        ],
        rows,
        after=[new],
    )
    ring_3, low_1, high_0, high_2, new_other = phase(
        [ring_3, low_1, high_0, high_2, new_other], after=[totals[0]]
    )

    low_2 = along_z(low_1)
    high_1 = along_z(high_0)
    high_3 = along_x(ring_3[half:])
    pair = join(new, new_other)
    pair_1 = across_replicas(pair, lambda y, x: (y - 1, x))
    pair_3 = across_replicas(pair, lambda y, x: (y + 1, x))
    totals = project(
        tokens,
        tokens_half,
        [
            ((3, 0, 0, 0), ring_3),
            ((1, 1, 0, 0), low_1),
            ((2, 1, 0, half), high_2),
        ],
        rows,
        totals,
        after=[pair],
    )
    low_2, high_1, high_3, pair = phase(
        [low_2, high_1, high_3, pair], after=[totals[0], pair_1, pair_3]
    )

    low_3 = along_z(low_2)
    pair_2 = across_replicas(pair, lambda y, x: (y + 2, x))
    own_total, other_total = project(
        tokens,
        tokens_half,
        [
            ((2, 1, 0, 0), low_2),
            ((1, 1, 0, half), high_1),
            ((3, 1, 0, half), high_3),
        ],
        rows,
        totals,
        last=True,
    )
    low_3, pair_2, other_total = phase([low_3, pair_2, other_total])

    low_3_other = to_core(low_3)
    other_total = to_core(other_total)
    new_weights, done = whole(
        assemble_kernel,
        [shape((rows, columns), jnp.bfloat16), shape((8, BLOCK), jnp.float32)],
        "assemble",
        [pair, pair_1, pair_2, pair_3],
    )
    next_keys = finish(
        tokens,
        [((3, 1, 0, 0), low_3), ((3, 1, 1, 0), low_3_other)],
        rows,
        own_total,
        other_total,
        row_scale,
        after=[done],
    )
    return (next_keys, new_weights, velocity)


def solution(mesh):
    placed = (
        P("replica", "fsdp", None),
        P("replica", None),
        P("replica", "fsdp", None),
        P("replica", "fsdp", None),
        P("fsdp", None),
        P("fsdp", "replica"),
    )
    return jax.shard_map(
        body,
        mesh=mesh,
        in_specs=placed,
        out_specs=(P("replica", "fsdp", None), P("fsdp", None), P("fsdp", "replica")),
        check_vma=False,
    )
```

time: 254 us -> 105 us (0.41)
  waiting for transfers between devices: 178 us -> 33.7 us
  starting transfers between devices: 0.12 us -> 39.8 us
  Pallas kernels: 0 us -> 30.6 us
  blocking collectives: 20.3 us -> 0 us
  matrix products: 19.4 us -> 0 us
  other arithmetic: 18.4 us -> 0 us
  between operations: 13.9 us -> 0.75 us
  local copies, waits for them, and re-layouts: 4.01 us -> 0.08 us
    all_gather x2 -> x0, waiting for transfers between devices: 122 us -> none  [the longest x1 115 us: body(): lax.all_gather(next_weights[0], 'fsdp', axis=0, tiled=True)]
    reduce_scatter x1 -> x0, waiting for transfers between devices: 55.6 us -> none  [body(): lax.psum_scatter(from_blocks(levels, scales, BLOCK), 'replica', scatter_d...]
    ppermute x0 -> x22, starting transfers between devices: none -> 39.8 us  [the longest x8 15.6 us: across_replicas(): return lax.ppermute(value, 'replica', pairs)]
    ppermute x0 -> x22, waiting for transfers between devices: none -> 33.7 us  [the longest x4 14.5 us: along_x(): return lax.ppermute(value, 'fsdp', fsdp_perm(lambda z, x, c: (z, 1 - x, c)))]
    pallas_call x0 -> x16, Pallas kernels: none -> 30.6 us  [the longest x3 15.2 us: project(): pl.pallas_call(functools.partial(project_kernel, places, rows, bool(total...]
    all_gather x1 -> x0, blocking collectives: 20.3 us -> none  [body(): lax.all_gather(new_scales, 'replica', axis=1, tiled=True)]
    dot_general x1 -> x0, matrix products: 19.4 us -> none  [body(): jnp.dot(normed, lax.all_gather(next_weights[0], 'fsdp', axis=0, tiled=Tru...]
    reduce_sum x1 -> x0, other arithmetic: 7.1 us -> none  [body(): square_mean = jnp.mean(rows_float * rows_float, axis=1, keepdims=True)]
  transfers between devices with their start and end apart: 3 -> 22, of which waited for: 3 -> 10; matrix products, arithmetic and copies ran while one was open for 4% -> 0% of each run, Pallas kernels for 0% -> 25%
where the time goes in v2:
time: 105 us
  starting transfers between devices  39.8 us (38%)
  waiting for transfers between devices  33.7 us (32%)
  Pallas kernels  30.6 us (29%)
    ppermute x8, starting transfers between devices, across_replicas(): return lax.ppermute(value, 'replica', pairs)  15.6 us
    pallas_call x3, Pallas kernels, project(): pl.pallas_call(functools.partial(project_kernel, places, rows, bool(total...  15.2 us
    ppermute x4, waiting for transfers between devices, along_x(): return lax.ppermute(value, 'fsdp', fsdp_perm(lambda z, x, c: (z, 1 - x, c)))  14.5 us
    ppermute x8, waiting for transfers between devices, across_replicas(): return lax.ppermute(value, 'replica', pairs)  9.68 us
    ppermute x7, starting transfers between devices, along_z(): lax.ppermute(value, 'fsdp', fsdp_perm(lambda z, x, c: (z + 1 - 2 * c, x,...  9.01 us
    ppermute x4, starting transfers between devices, along_x(): return lax.ppermute(value, 'fsdp', fsdp_perm(lambda z, x, c: (z, 1 - x, c)))  8.6 us
    pallas_call x2, Pallas kernels, fetch(): pl.pallas_call(run, in_specs=[pl.BlockSpec(memory_space=pltpu.HBM)] + [pl...  7.82 us
    ppermute x7, waiting for transfers between devices, along_z(): lax.ppermute(value, 'fsdp', fsdp_perm(lambda z, x, c: (z + 1 - 2 * c, x,...  6.99 us
  transfers between devices with their start and end apart: 22, of which 10 were waited for; matrix products, arithmetic and copies ran while one was open for 0% of the time, Pallas kernels for 25%

profile of v2, /device:TPU:1, one launch (start us, length us, event | category | flops | bytes accessed | tf_op | source)
XLA Modules:
  0.0 104.9 jit_solution(12482743591651213860)
XLA Ops:
  0.6 1.6 %prepare.1 = (bf16[512,1024]{1,0:T(8,128)(2,1)S(1)}, bf16[256,1024]{1,0:T(8,128)(2,1)S(1)}, bf16[256,1024]{1,0:T(8,128)(2,1)S(1)}, bf16[512,256]{1,0:T(8,128)(2,...) custom-call(f32[1,8192]{1,0:T(1,128)} %gain_hbm.1, ...), custom_call_target="tpu_custom_call" | custom-call | flops 524288 | bytes 2097152 | tf_op jit(solution)/shard_map/prepare/pallas_call | solution.py:111
  2.3 4.7 %collective-permute-start = (bf16[512,1024]{1,0:T(8,128)(2,1)S(1)}, bf16[512,1024]{1,0:T(8,128)(2,1)S(1)}, u32[]{:S(2)}, u32[]{:S(2)}) collective-permute-start(bf16[512,1024]{1,0:T(8,128)(2,1)S(1)} %get-tuple-element.44.refs_0_.refs_2_), channel_id=1, source_target_pairs={{0,4},{1,13},{2,6},{3,15},{4,8},{5,1},{6,10},{7,3},{8,12},{9,5},{1... | collective-permute-start | bytes 3145736 | tf_op jit(solution)/shard_map/ppermute | solution.py:31
  6.9 2.7 %collective-permute-start.1 = (bf16[256,1024]{1,0:T(8,128)(2,1)S(1)}, bf16[256,1024]{1,0:T(8,128)(2,1)S(1)}, u32[]{:S(2)}, u32[]{:S(2)}) collective-permute-start(bf16[256,1024]{1,0:T(8,128)(2,1)S(1)} %get-tuple-element.45), channel_id=1, source_target_pairs={{0,2},{1,3},{2,0},{3,1},{4,6},{5,7},{6,4},{7,5},{8,10},{9,11},{10,... | collective-permute-start | bytes 1572872 | tf_op jit(solution)/shard_map/ppermute | solution.py:37
  9.7 2.9 %half.1.refs_3_ = bf16[768,4096]{1,0:T(8,128)(2,1)S(1)} custom-call(bf16[1,768,8192]{2,1,0:T(8,128)(2,1)} %tokens_hbm.3, bf16[512,1024]{1,0:T(8,128)(2,1)S(1)} %get-tuple-element.44.refs_0_.refs_2_), custom_call_target="tpu_custom_call" | custom-call | flops 6291456 | bytes 12582912 | tf_op jit(solution)/shard_map/half/pallas_call | solution.py:198
  12.6 8.8 %collective-permute-done.1.refs_1_ = bf16[256,1024]{1,0:T(8,128)(2,1)S(1)} collective-permute-done((bf16[256,1024]{1,0:T(8,128)(2,1)S(1)}, bf16[256,1024]{1,0:T(8,128)(2,1)S(1)}, u32[]{:S(2)}, u32[]{:S(2)}) %collective-permute-start.1) | collective-permute-done | bytes 524320 | tf_op jit(solution)/shard_map/ppermute | solution.py:37
  21.4 0.0 collective-permute-start.12
  21.4 1.5 %collective-permute-start.2 = (bf16[512,1024]{1,0:T(8,128)(2,1)S(1)}, bf16[512,1024]{1,0:T(8,128)(2,1)S(1)}, u32[]{:S(2)}, u32[]{:S(2)}) collective-permute-start(bf16[512,1024]{1,0:T(8,128)(2,1)S(1)} %get-tuple-element.47.refs_0_.refs_3_), channel_id=1, source_target_pairs={{0,4},{1,13},{2,6},{3,15},{4,8},{5,1},{6,10},{7,3},{8,12},{9,5},{1... | collective-permute-start | bytes 3145736 | tf_op jit(solution)/shard_map/ppermute | solution.py:31
  22.9 1.3 %collective-permute-start.4 = (bf16[512,256]{1,0:T(8,128)(2,1)S(1)}, bf16[512,256]{1,0:T(8,128)(2,1)S(1)}, u32[]{:S(2)}, u32[]{:S(2)}) collective-permute-start(bf16[512,256]{1,0:T(8,128)(2,1)S(1)} %get-tuple-element.52), channel_id=1, source_target_pairs={{0,32},{16,48},{32,64},{48,80},{64,96},{80,112},{96,0},{112,16},{1... | collective-permute-start | bytes 786440 | tf_op jit(solution)/shard_map/ppermute | solution.py:50
  24.2 2.7 %collective-permute-start.3 = (bf16[256,1024]{1,0:T(8,128)(2,1)S(1)}, bf16[256,1024]{1,0:T(8,128)(2,1)S(1)}, u32[]{:S(2)}, u32[]{:S(2)}) collective-permute-start(bf16[256,1024]{1,0:T(8,128)(2,1)S(1)} %get-tuple-element.50), channel_id=1, source_target_pairs={{0,2},{1,3},{2,0},{3,1},{4,6},{5,7},{6,4},{7,5},{8,10},{9,11},{10,... | collective-permute-start | bytes 1572872 | tf_op jit(solution)/shard_map/ppermute | solution.py:37
  26.9 2.6 %collective-permute-start.5 = (bf16[512,256]{1,0:T(8,128)(2,1)S(1)}, bf16[512,256]{1,0:T(8,128)(2,1)S(1)}, u32[]{:S(2)}, u32[]{:S(2)}) collective-permute-start(bf16[512,256]{1,0:T(8,128)(2,1)S(1)} %get-tuple-element.53), channel_id=1, source_target_pairs={{0,64},{16,80},{32,96},{48,112},{64,0},{80,16},{96,32},{112,48},{1... | collective-permute-start | bytes 786440 | tf_op jit(solution)/shard_map/ppermute | solution.py:50
  29.6 2.3 %collective-permute-done.4.refs_2_ = bf16[512,256]{1,0:T(8,128)(2,1)S(1)} collective-permute-done((bf16[512,256]{1,0:T(8,128)(2,1)S(1)}, bf16[512,256]{1,0:T(8,128)(2,1)S(1)}, u32[]{:S(2)}, u32[]{:S(2)}) %collective-permute-start.4) | collective-permute-done | bytes 262176 | tf_op jit(solution)/shard_map/ppermute | solution.py:50
  31.9 2.0 %collective-permute-start.6 = (bf16[512,256]{1,0:T(8,128)(2,1)S(1)}, bf16[512,256]{1,0:T(8,128)(2,1)S(1)}, u32[]{:S(2)}, u32[]{:S(2)}) collective-permute-start(bf16[512,256]{1,0:T(8,128)(2,1)S(1)} %get-tuple-element.54), channel_id=1, source_target_pairs={{0,96},{16,112},{32,0},{48,16},{64,32},{80,48},{96,64},{112,80},{1... | collective-permute-start | bytes 786440 | tf_op jit(solution)/shard_map/ppermute | solution.py:50
  33.9 4.9 %load.1 = (bf16[1,768,8192]{2,1,0:T(8,128)(2,1)S(1)}, f32[768,128]{1,0:T(8,128)S(1)}) custom-call(bf16[1,768,8192]{2,1,0:T(8,128)(2,1)} %tokens_hbm.3, bf16[512,1024]{1,0:T(8,128)(2,1)S(1)} %get-tuple-element.47.refs_0_.refs_3_), custom_call_target="tpu_custom_call" | custom-call | flops 6291456 | bytes 12582912 | tf_op jit(solution)/shard_map/load/pallas_call | solution.py:198
  38.8 0.0 collective-permute-done.5.refs_3_
  38.8 2.5 %collective-permute-done.6.refs_4_ = bf16[512,256]{1,0:T(8,128)(2,1)S(1)} collective-permute-done((bf16[512,256]{1,0:T(8,128)(2,1)S(1)}, bf16[512,256]{1,0:T(8,128)(2,1)S(1)}, u32[]{:S(2)}, u32[]{:S(2)}) %collective-permute-start.6) | collective-permute-done | bytes 262176 | tf_op jit(solution)/shard_map/ppermute | solution.py:50
  41.3 1.1 %partial.1 = (f32[512,128]{1,0:T(8,128)S(1)}, bf16[512,128]{1,0:T(8,128)(2,1)S(1)}) custom-call(f32[512,1024]{1,0:T(8,128)S(1)} %copy-done, bf16[512,256]{1,0:T(8,128)(2,1)S(1)} %get-tuple-element.51.refs_1_, bf16[512,256]{1,0:T(8,128)(2,1)S(1)} %collective-permute-done.4.refs_2_, bf16[512,256]{1,0:T(8,128)(2,1)S(1)} %collective-permute-done.5.refs_3_, ...), custom_call_target="tpu_custom_call" | custom-call | flops 25165824 | bytes 6291456 | tf_op jit(solution)/shard_map/partial/pallas_call | solution.py:402
  42.5 0.3 collective-permute-start.7
  42.8 4.4 %collective-permute-done.7.refs_3_ = bf16[512,128]{1,0:T(8,128)(2,1)S(1)} collective-permute-done((bf16[512,128]{1,0:T(8,128)(2,1)S(1)}, bf16[512,128]{1,0:T(8,128)(2,1)S(1)}, u32[]{:S(2)}, u32[]{:S(2)}) %collective-permute-start.7) | collective-permute-done | bytes 131104 | tf_op jit(solution)/shard_map/ppermute | solution.py:50
  47.2 0.0 collective-permute-done.3.refs_2_
  47.2 0.0 collective-permute-done.2.refs_0_
  47.2 0.1 collective-permute-start.8
  47.4 0.8 update.1
  48.2 0.1 collective-permute-start.11
  48.3 1.9 %collective-permute-start.10 = (bf16[256,1024]{1,0:T(8,128)(2,1)S(1)}, bf16[256,1024]{1,0:T(8,128)(2,1)S(1)}, u32[]{:S(2)}, u32[]{:S(2)}) collective-permute-start(bf16[256,1024]{1,0:T(8,128)(2,1)S(1)} %slice.6), channel_id=1, source_target_pairs={{0,2},{1,3},{2,0},{3,1},{4,6},{5,7},{6,4},{7,5},{8,10},{9,11},{10,... | collective-permute-start | bytes 1572872 | tf_op jit(solution)/shard_map/ppermute | solution.py:37
  50.2 0.0 collective-permute-done.12.refs_1_
  50.2 7.2 %project.3 = (f32[768,1024]{1,0:T(8,128)S(1)}, f32[768,1024]{1,0:T(8,128)S(1)}) custom-call(bf16[1,768,8192]{2,1,0:T(8,128)(2,1)S(1)} %get-tuple-element.48.refs_0_, bf16[768,4096]{1,0:T(8,128)(2,1)S(1)} %collective-permute-done.12.refs_1_, bf16[512,1024]{1,0:T(8,128)(2,1)S(1)} %get-tuple-element.44.refs_0_.refs_2_, ...), custom_call_target="tpu_custom_call" | custom-call | flops 6442450944 | bytes 4194304 | tf_op jit(solution)/shard_map/project/pallas_call | solution.py:264
  57.4 0.0 collective-permute-done.11.refs_4_
  57.4 5.7 %collective-permute-done.10.refs_3_ = bf16[256,1024]{1,0:T(8,128)(2,1)S(1)} collective-permute-done((bf16[256,1024]{1,0:T(8,128)(2,1)S(1)}, bf16[256,1024]{1,0:T(8,128)(2,1)S(1)}, u32[]{:S(2)}, u32[]{:S(2)}) %collective-permute-start.10) | collective-permute-done | bytes 524320 | tf_op jit(solution)/shard_map/ppermute | solution.py:37
  63.1 3.7 %collective-permute-done.9.refs_1_ = bf16[256,1024]{1,0:T(8,128)(2,1)S(1)} collective-permute-done((bf16[256,1024]{1,0:T(8,128)(2,1)S(1)}, bf16[256,1024]{1,0:T(8,128)(2,1)S(1)}, u32[]{:S(2)}, u32[]{:S(2)}) %collective-permute-start.9) | collective-permute-done | bytes 524320 | tf_op jit(solution)/shard_map/ppermute | solution.py:31
  66.9 1.2 %collective-permute-start.15 = (bf16[256,1024]{1,0:T(8,128)(2,1)S(1)}, bf16[256,1024]{1,0:T(8,128)(2,1)S(1)}, u32[]{:S(2)}, u32[]{:S(2)}) collective-permute-start(bf16[256,1024]{1,0:T(8,128)(2,1)S(1)} %slice.7), channel_id=1, source_target_pairs={{0,2},{1,3},{2,0},{3,1},{4,6},{5,7},{6,4},{7,5},{8,10},{9,11},{10,... | collective-permute-start | bytes 1572872 | tf_op jit(solution)/shard_map/ppermute | solution.py:37
  68.1 0.9 collective-permute-start.14
  69.0 0.0 collective-permute-start.13
  69.1 2.1 %collective-permute-start.17 = (bf16[512,256]{1,0:T(8,128)(2,1)S(1)}, bf16[512,256]{1,0:T(8,128)(2,1)S(1)}, u32[]{:S(2)}, u32[]{:S(2)}) collective-permute-start(bf16[512,256]{1,0:T(8,128)(2,1)S(1)} %join.1.refs_7_.refs_3_), channel_id=1, source_target_pairs={{0,32},{16,48},{32,64},{48,80},{64,96},{80,112},{96,0},{112,16},{1... | collective-permute-start | bytes 786440 | tf_op jit(solution)/shard_map/ppermute | solution.py:50
  71.3 2.9 %collective-permute-start.16 = (bf16[512,256]{1,0:T(8,128)(2,1)S(1)}, bf16[512,256]{1,0:T(8,128)(2,1)S(1)}, u32[]{:S(2)}, u32[]{:S(2)}) collective-permute-start(bf16[512,256]{1,0:T(8,128)(2,1)S(1)} %join.1.refs_7_.refs_3_), channel_id=1, source_target_pairs={{0,96},{16,112},{32,0},{48,16},{64,32},{80,48},{96,64},{112,80},{1... | collective-permute-start | bytes 786440 | tf_op jit(solution)/shard_map/ppermute | solution.py:50
  74.2 4.6 %project.4 = (f32[768,1024]{1,0:T(8,128)S(1)}, f32[768,1024]{1,0:T(8,128)S(1)}) custom-call(bf16[1,768,8192]{2,1,0:T(8,128)(2,1)S(1)} %get-tuple-element.48.refs_0_, bf16[768,4096]{1,0:T(8,128)(2,1)S(1)} %collective-permute-done.12.refs_1_, bf16[512,1024]{1,0:T(8,128)(2,1)S(1)} %get-tuple-element.67.refs_2_, ...), custom_call_target="tpu_custom_call", output_to_operand_aliasing={{0}: (5, {}), {1}: (6, {})} | custom-call | flops 3221225472 | bytes 2097152 | tf_op jit(solution)/shard_map/project/pallas_call | solution.py:264
  78.7 0.1 collective-permute-done.17.refs_6_.refs_3_
  78.8 0.0 collective-permute-done.16.refs_5_.refs_1_
  78.8 0.0 collective-permute-done.15.refs_2_
  78.8 3.2 %collective-permute-done.13.refs_0_ = bf16[256,1024]{1,0:T(8,128)(2,1)S(1)} collective-permute-done((bf16[256,1024]{1,0:T(8,128)(2,1)S(1)}, bf16[256,1024]{1,0:T(8,128)(2,1)S(1)}, u32[]{:S(2)}, u32[]{:S(2)}) %collective-permute-start.13) | collective-permute-done | bytes 524320 | tf_op jit(solution)/shard_map/ppermute | solution.py:31
  82.1 1.8 %collective-permute-start.18 = (bf16[256,1024]{1,0:T(8,128)(2,1)S(1)}, bf16[256,1024]{1,0:T(8,128)(2,1)S(1)}, u32[]{:S(2)}, u32[]{:S(2)}) collective-permute-start(bf16[256,1024]{1,0:T(8,128)(2,1)S(1)} %get-tuple-element.72.refs_2_), channel_id=1, source_target_pairs={{0,4},{1,13},{2,6},{3,15},{4,8},{5,1},{6,10},{7,3},{8,12},{9,5},{1... | collective-permute-start | bytes 1572872 | tf_op jit(solution)/shard_map/ppermute | solution.py:31
  83.9 4.1 %collective-permute-start.19 = (bf16[512,256]{1,0:T(8,128)(2,1)S(1)}, bf16[512,256]{1,0:T(8,128)(2,1)S(1)}, u32[]{:S(2)}, u32[]{:S(2)}) collective-permute-start(bf16[512,256]{1,0:T(8,128)(2,1)S(1)} %get-tuple-element.73.refs_0_), channel_id=1, source_target_pairs={{0,64},{16,80},{32,96},{48,112},{64,0},{80,16},{96,32},{112,48},{1... | collective-permute-start | bytes 786440 | tf_op jit(solution)/shard_map/ppermute | solution.py:50
  88.1 3.4 %project.5 = (f32[768,1024]{1,0:T(8,128)S(1)}, bf16[768,1024]{1,0:T(8,128)(2,1)S(1)}) custom-call(bf16[1,768,8192]{2,1,0:T(8,128)(2,1)S(1)} %get-tuple-element.48.refs_0_, bf16[768,4096]{1,0:T(8,128)(2,1)S(1)} %collective-permute-done.12.refs_1_, bf16[256,1024]{1,0:T(8,128)(2,1)S(1)} %get-tuple-element.72.refs_2_, ...), custom_call_target="tpu_custom_call", output_to_operand_aliasing={{0}: (5, {})} | custom-call | flops 2415919104 | bytes 1572864 | tf_op jit(solution)/shard_map/project/pallas_call | solution.py:264
  91.5 0.3 collective-permute-done.19.refs_1_
  91.8 6.6 %collective-permute-start.21 = (bf16[768,1024]{1,0:T(8,128)(2,1)S(1)}, bf16[768,1024]{1,0:T(8,128)(2,1)S(1)}, u32[]{:S(2)}, u32[]{:S(2)}) collective-permute-start(bf16[768,1024]{1,0:T(8,128)(2,1)S(1)} %get-tuple-element.80), channel_id=1, source_target_pairs={{0,1},{1,0},{2,3},{3,2},{4,5},{5,4},{6,7},{7,6},{8,9},{9,8},{10,11... | collective-permute-start | bytes 4718600 | tf_op jit(solution)/shard_map/ppermute | solution.py:41
  98.4 0.0 collective-permute-start.20
  98.4 1.3 %assemble.1 = (bf16[512,1024]{1,0:T(8,128)(2,1)}, f32[8,128]{1,0:T(8,128)S(1)}) custom-call(bf16[512,256]{1,0:T(8,128)(2,1)S(1)} %get-tuple-element.73.refs_0_, bf16[512,256]{1,0:T(8,128)(2,1)S(1)} %collective-permute-done.16.refs_5_.refs_1_, bf16[512,256]{1,0:T(8,128)(2,1)S(1)} %get-tuple-element.81.refs_2_, ...), custom_call_target="tpu_custom_call" | custom-call | flops 8388608 | bytes 2097152 | tf_op jit(solution)/shard_map/assemble/pallas_call | solution.py:402
  99.7 2.5 %collective-permute-done.20.refs_2_ = bf16[256,1024]{1,0:T(8,128)(2,1)S(1)} collective-permute-done((bf16[256,1024]{1,0:T(8,128)(2,1)S(1)}, bf16[256,1024]{1,0:T(8,128)(2,1)S(1)}, u32[]{:S(2)}, u32[]{:S(2)}) %collective-permute-start.20) | collective-permute-done | bytes 524320 | tf_op jit(solution)/shard_map/ppermute | solution.py:41
  102.2 2.7 %finish.1 = bf16[1,768,1024]{2,1,0:T(8,128)(2,1)} custom-call(bf16[1,768,8192]{2,1,0:T(8,128)(2,1)S(1)} %get-tuple-element.48.refs_0_, bf16[256,1024]{1,0:T(8,128)(2,1)S(1)} %get-tuple-element.78.refs_1_, bf16[256,1024]{1,0:T(8,128)(2,1)S(1)} %collective-permute-done.20.refs_2_, f32[768,1024]{1,0:T(8,128)S(1)} %get-tuple-element.79.refs_3_, ...), custom_call_target="tpu_custom_call" | custom-call | flops 805306368 | bytes 1048576 | tf_op jit(solution)/shard_map/finish/pallas_call | solution.py:318
  (18 shorter events, 0.1 us)
Async XLA Ops:
  2.3 19.1 %collective-permute-start = (bf16[512,1024]{1,0:T(8,128)(2,1)S(1)}, bf16[512,1024]{1,0:T(8,128)(2,1)S(1)}, u32[]{:S(2)}, u32[]{:S(2)}) collective-permute-start(bf16[512,1024]{1,0:T(8,128)(2,1)S(1)} %get-tuple-element.44.refs_0_.refs_2_), channel_id=1, source_target_pairs={{0,4},{1,13},{2,6},{3,15},{4,8},{5,1},{6,10},{7,3},{8,12},{9,5},{1... | collective-permute-start | bytes 3145736 | tf_op jit(solution)/shard_map/ppermute | solution.py:31
  6.9 14.4 %collective-permute-start.1 = (bf16[256,1024]{1,0:T(8,128)(2,1)S(1)}, bf16[256,1024]{1,0:T(8,128)(2,1)S(1)}, u32[]{:S(2)}, u32[]{:S(2)}) collective-permute-start(bf16[256,1024]{1,0:T(8,128)(2,1)S(1)} %get-tuple-element.45), channel_id=1, source_target_pairs={{0,2},{1,3},{2,0},{3,1},{4,6},{5,7},{6,4},{7,5},{8,10},{9,11},{10,... | collective-permute-start | bytes 1572872 | tf_op jit(solution)/shard_map/ppermute | solution.py:37
  21.4 28.8 %collective-permute-start.12 = (bf16[768,4096]{1,0:T(8,128)(2,1)S(1)}, bf16[768,4096]{1,0:T(8,128)(2,1)S(1)}, u32[]{:S(2)}, u32[]{:S(2)}) collective-permute-start(bf16[768,4096]{1,0:T(8,128)(2,1)S(1)} %get-tuple-element.63), channel_id=1, source_target_pairs={{0,1},{1,0},{2,3},{3,2},{4,5},{5,4},{6,7},{7,6},{8,9},{9,8},{10,11... | collective-permute-start | bytes 18874376 | tf_op jit(solution)/shard_map/ppermute | solution.py:41
  21.4 25.9 %collective-permute-start.2 = (bf16[512,1024]{1,0:T(8,128)(2,1)S(1)}, bf16[512,1024]{1,0:T(8,128)(2,1)S(1)}, u32[]{:S(2)}, u32[]{:S(2)}) collective-permute-start(bf16[512,1024]{1,0:T(8,128)(2,1)S(1)} %get-tuple-element.47.refs_0_.refs_3_), channel_id=1, source_target_pairs={{0,4},{1,13},{2,6},{3,15},{4,8},{5,1},{6,10},{7,3},{8,12},{9,5},{1... | collective-permute-start | bytes 3145736 | tf_op jit(solution)/shard_map/ppermute | solution.py:31
  22.9 9.0 %collective-permute-start.4 = (bf16[512,256]{1,0:T(8,128)(2,1)S(1)}, bf16[512,256]{1,0:T(8,128)(2,1)S(1)}, u32[]{:S(2)}, u32[]{:S(2)}) collective-permute-start(bf16[512,256]{1,0:T(8,128)(2,1)S(1)} %get-tuple-element.52), channel_id=1, source_target_pairs={{0,32},{16,48},{32,64},{48,80},{64,96},{80,112},{96,0},{112,16},{1... | collective-permute-start | bytes 786440 | tf_op jit(solution)/shard_map/ppermute | solution.py:50
  24.2 23.1 %collective-permute-start.3 = (bf16[256,1024]{1,0:T(8,128)(2,1)S(1)}, bf16[256,1024]{1,0:T(8,128)(2,1)S(1)}, u32[]{:S(2)}, u32[]{:S(2)}) collective-permute-start(bf16[256,1024]{1,0:T(8,128)(2,1)S(1)} %get-tuple-element.50), channel_id=1, source_target_pairs={{0,2},{1,3},{2,0},{3,1},{4,6},{5,7},{6,4},{7,5},{8,10},{9,11},{10,... | collective-permute-start | bytes 1572872 | tf_op jit(solution)/shard_map/ppermute | solution.py:37
  26.9 11.9 %collective-permute-start.5 = (bf16[512,256]{1,0:T(8,128)(2,1)S(1)}, bf16[512,256]{1,0:T(8,128)(2,1)S(1)}, u32[]{:S(2)}, u32[]{:S(2)}) collective-permute-start(bf16[512,256]{1,0:T(8,128)(2,1)S(1)} %get-tuple-element.53), channel_id=1, source_target_pairs={{0,64},{16,80},{32,96},{48,112},{64,0},{80,16},{96,32},{112,48},{1... | collective-permute-start | bytes 786440 | tf_op jit(solution)/shard_map/ppermute | solution.py:50
  31.9 9.5 %copy-start = (f32[512,1024]{1,0:T(8,128)S(1)}, f32[512,1024]{1,0:T(8,128)}, u32[]{:S(2)}) copy-start(f32[512,1024]{1,0:T(8,128)} %refs_0_.3) | copy-start | bytes 6291460
  31.9 9.4 %collective-permute-start.6 = (bf16[512,256]{1,0:T(8,128)(2,1)S(1)}, bf16[512,256]{1,0:T(8,128)(2,1)S(1)}, u32[]{:S(2)}, u32[]{:S(2)}) collective-permute-start(bf16[512,256]{1,0:T(8,128)(2,1)S(1)} %get-tuple-element.54), channel_id=1, source_target_pairs={{0,96},{16,112},{32,0},{48,16},{64,32},{80,48},{96,64},{112,80},{1... | collective-permute-start | bytes 786440 | tf_op jit(solution)/shard_map/ppermute | solution.py:50
  41.3 6.0 %copy-start.1 = (bf16[512,128]{1,0:T(8,128)(2,1)S(1)}, bf16[512,128]{1,0:T(8,128)(2,1)}, u32[]{:S(2)}) copy-start(bf16[512,128]{1,0:T(8,128)(2,1)} %refs_1_.1) | copy-start | bytes 393220
  42.5 4.8 %collective-permute-start.7 = (bf16[512,128]{1,0:T(8,128)(2,1)S(1)}, bf16[512,128]{1,0:T(8,128)(2,1)S(1)}, u32[]{:S(2)}, u32[]{:S(2)}) collective-permute-start(bf16[512,128]{1,0:T(8,128)(2,1)S(1)} %get-tuple-element.56), channel_id=1, source_target_pairs={{0,16},{16,0},{32,48},{48,32},{64,80},{80,64},{96,112},{112,96},{1... | collective-permute-start | bytes 393224 | tf_op jit(solution)/shard_map/ppermute | solution.py:50
  47.2 19.6 %collective-permute-start.8 = (bf16[512,1024]{1,0:T(8,128)(2,1)S(1)}, bf16[512,1024]{1,0:T(8,128)(2,1)S(1)}, u32[]{:S(2)}, u32[]{:S(2)}) collective-permute-start(bf16[512,1024]{1,0:T(8,128)(2,1)S(1)} %get-tuple-element.57.refs_4_), channel_id=1, source_target_pairs={{0,4},{1,13},{2,6},{3,15},{4,8},{5,1},{6,10},{7,3},{8,12},{9,5},{1... | collective-permute-start | bytes 3145736 | tf_op jit(solution)/shard_map/ppermute | solution.py:31
  48.2 9.3 %collective-permute-start.11 = (bf16[512,128]{1,0:T(8,128)(2,1)S(1)}, bf16[512,128]{1,0:T(8,128)(2,1)S(1)}, u32[]{:S(2)}, u32[]{:S(2)}) collective-permute-start(bf16[512,128]{1,0:T(8,128)(2,1)S(1)} %get-tuple-element.62.refs_7_.refs_0_), channel_id=1, source_target_pairs={{0,16},{16,0},{32,48},{48,32},{64,80},{80,64},{96,112},{112,96},{1... | collective-permute-start | bytes 393224 | tf_op jit(solution)/shard_map/ppermute | solution.py:50
  48.3 14.8 %collective-permute-start.10 = (bf16[256,1024]{1,0:T(8,128)(2,1)S(1)}, bf16[256,1024]{1,0:T(8,128)(2,1)S(1)}, u32[]{:S(2)}, u32[]{:S(2)}) collective-permute-start(bf16[256,1024]{1,0:T(8,128)(2,1)S(1)} %slice.6), channel_id=1, source_target_pairs={{0,2},{1,3},{2,0},{3,1},{4,6},{5,7},{6,4},{7,5},{8,10},{9,11},{10,... | collective-permute-start | bytes 1572872 | tf_op jit(solution)/shard_map/ppermute | solution.py:37
  50.2 16.7 %collective-permute-start.9 = (bf16[256,1024]{1,0:T(8,128)(2,1)S(1)}, bf16[256,1024]{1,0:T(8,128)(2,1)S(1)}, u32[]{:S(2)}, u32[]{:S(2)}) collective-permute-start(bf16[256,1024]{1,0:T(8,128)(2,1)S(1)} %get-tuple-element.58.refs_5_), channel_id=1, source_target_pairs={{0,4},{1,13},{2,6},{3,15},{4,8},{5,1},{6,10},{7,3},{8,12},{9,5},{1... | collective-permute-start | bytes 1572872 | tf_op jit(solution)/shard_map/ppermute | solution.py:31
  66.9 11.9 %collective-permute-start.15 = (bf16[256,1024]{1,0:T(8,128)(2,1)S(1)}, bf16[256,1024]{1,0:T(8,128)(2,1)S(1)}, u32[]{:S(2)}, u32[]{:S(2)}) collective-permute-start(bf16[256,1024]{1,0:T(8,128)(2,1)S(1)} %slice.7), channel_id=1, source_target_pairs={{0,2},{1,3},{2,0},{3,1},{4,6},{5,7},{6,4},{7,5},{8,10},{9,11},{10,... | collective-permute-start | bytes 1572872 | tf_op jit(solution)/shard_map/ppermute | solution.py:37
  68.1 10.7 %collective-permute-start.14 = (bf16[256,1024]{1,0:T(8,128)(2,1)S(1)}, bf16[256,1024]{1,0:T(8,128)(2,1)S(1)}, u32[]{:S(2)}, u32[]{:S(2)}) collective-permute-start(bf16[256,1024]{1,0:T(8,128)(2,1)S(1)} %get-tuple-element.66), channel_id=1, source_target_pairs={{0,4},{1,13},{2,6},{3,15},{4,8},{5,1},{6,10},{7,3},{8,12},{9,5},{1... | collective-permute-start | bytes 1572872 | tf_op jit(solution)/shard_map/ppermute | solution.py:31
  69.0 13.0 %collective-permute-start.13 = (bf16[256,1024]{1,0:T(8,128)(2,1)S(1)}, bf16[256,1024]{1,0:T(8,128)(2,1)S(1)}, u32[]{:S(2)}, u32[]{:S(2)}) collective-permute-start(bf16[256,1024]{1,0:T(8,128)(2,1)S(1)} %get-tuple-element.65.refs_3_), channel_id=1, source_target_pairs={{0,4},{1,13},{2,6},{3,15},{4,8},{5,1},{6,10},{7,3},{8,12},{9,5},{1... | collective-permute-start | bytes 1572872 | tf_op jit(solution)/shard_map/ppermute | solution.py:31
  69.1 9.7 %collective-permute-start.17 = (bf16[512,256]{1,0:T(8,128)(2,1)S(1)}, bf16[512,256]{1,0:T(8,128)(2,1)S(1)}, u32[]{:S(2)}, u32[]{:S(2)}) collective-permute-start(bf16[512,256]{1,0:T(8,128)(2,1)S(1)} %join.1.refs_7_.refs_3_), channel_id=1, source_target_pairs={{0,32},{16,48},{32,64},{48,80},{64,96},{80,112},{96,0},{112,16},{1... | collective-permute-start | bytes 786440 | tf_op jit(solution)/shard_map/ppermute | solution.py:50
  71.3 7.6 %collective-permute-start.16 = (bf16[512,256]{1,0:T(8,128)(2,1)S(1)}, bf16[512,256]{1,0:T(8,128)(2,1)S(1)}, u32[]{:S(2)}, u32[]{:S(2)}) collective-permute-start(bf16[512,256]{1,0:T(8,128)(2,1)S(1)} %join.1.refs_7_.refs_3_), channel_id=1, source_target_pairs={{0,96},{16,112},{32,0},{48,16},{64,32},{80,48},{96,64},{112,80},{1... | collective-permute-start | bytes 786440 | tf_op jit(solution)/shard_map/ppermute | solution.py:50
  82.1 9.7 %collective-permute-start.18 = (bf16[256,1024]{1,0:T(8,128)(2,1)S(1)}, bf16[256,1024]{1,0:T(8,128)(2,1)S(1)}, u32[]{:S(2)}, u32[]{:S(2)}) collective-permute-start(bf16[256,1024]{1,0:T(8,128)(2,1)S(1)} %get-tuple-element.72.refs_2_), channel_id=1, source_target_pairs={{0,4},{1,13},{2,6},{3,15},{4,8},{5,1},{6,10},{7,3},{8,12},{9,5},{1... | collective-permute-start | bytes 1572872 | tf_op jit(solution)/shard_map/ppermute | solution.py:31
  83.9 7.9 %collective-permute-start.19 = (bf16[512,256]{1,0:T(8,128)(2,1)S(1)}, bf16[512,256]{1,0:T(8,128)(2,1)S(1)}, u32[]{:S(2)}, u32[]{:S(2)}) collective-permute-start(bf16[512,256]{1,0:T(8,128)(2,1)S(1)} %get-tuple-element.73.refs_0_), channel_id=1, source_target_pairs={{0,64},{16,80},{32,96},{48,112},{64,0},{80,16},{96,32},{112,48},{1... | collective-permute-start | bytes 786440 | tf_op jit(solution)/shard_map/ppermute | solution.py:50
  91.8 10.3 %collective-permute-start.21 = (bf16[768,1024]{1,0:T(8,128)(2,1)S(1)}, bf16[768,1024]{1,0:T(8,128)(2,1)S(1)}, u32[]{:S(2)}, u32[]{:S(2)}) collective-permute-start(bf16[768,1024]{1,0:T(8,128)(2,1)S(1)} %get-tuple-element.80), channel_id=1, source_target_pairs={{0,1},{1,0},{2,3},{3,2},{4,5},{5,4},{6,7},{7,6},{8,9},{9,8},{10,11... | collective-permute-start | bytes 4718600 | tf_op jit(solution)/shard_map/ppermute | solution.py:41
  98.4 3.8 %collective-permute-start.20 = (bf16[256,1024]{1,0:T(8,128)(2,1)S(1)}, bf16[256,1024]{1,0:T(8,128)(2,1)S(1)}, u32[]{:S(2)}, u32[]{:S(2)}) collective-permute-start(bf16[256,1024]{1,0:T(8,128)(2,1)S(1)} %get-tuple-element.78.refs_1_), channel_id=1, source_target_pairs={{0,1},{1,0},{2,3},{3,2},{4,5},{5,4},{6,7},{7,6},{8,9},{9,8},{10,11... | collective-permute-start | bytes 1572872 | tf_op jit(solution)/shard_map/ppermute | solution.py:41

commit v3 on v2

--- a/solution.py
+++ b/solution.py
@@ -140,25 +140,6 @@
     )(*values, *after)
 
 
-def half_kernel(tokens_hbm, half_ref, sems):
-    shards = sems.shape[0]
-    width = half_ref.shape[1] // shards
-    other = 1 - lax.axis_index("fsdp") % C
-    copies = []
-    for k in range(shards):
-        at = pl.ds(pl.multiple_of((k * C + other) * width, width), width)
-        to = pl.ds(k * width, width)
-        copies.append(
-            pltpu.make_async_copy(
-                tokens_hbm.at[0, :, at], half_ref.at[:, to], sems.at[k]
-            )
-        )
-    for copy in copies:
-        copy.start()
-    for copy in copies:
-        copy.wait()
-
-
 def load_kernel(tokens_hbm, tokens_ref, scale_ref, sems):
     _, rows, features = tokens_ref.shape
     parts = sems.shape[0]
@@ -210,7 +191,7 @@
 
 def project_kernel(places, rows, given, *refs):
     count = len(places)
-    tokens_ref, half_ref, weight_refs = refs[0], refs[1], refs[2 : 2 + count]
+    tokens_ref, other_tokens_ref, weight_refs = refs[0], refs[1], refs[2 : 2 + count]
     total_refs = refs[2 + count : 4 + count] if given else None
     out_ref, other_ref = refs[-2:]
     me = lax.axis_index("fsdp")
@@ -218,19 +199,14 @@
     starts = []
     for step, dx, dc, first in places:
         block = ((z + (2 * c - 1) * step + Z) % Z) * 2 + (x + dx) % 2
-        starts.append(
-            (
-                pl.multiple_of((block * 2 + c) * rows + first, BLOCK),
-                pl.multiple_of(block * rows + first, BLOCK),
-            )
-        )
+        starts.append(pl.multiple_of((block * 2 + c) * rows + first, BLOCK))
     tile = 256
 
     def column(n, carry):
         at = pl.ds(pl.multiple_of(n * tile, tile), tile)
         total = total_refs[0][:, at] if given else None
         other = total_refs[1][:, at] if given else None
-        for (start, half_start), weight_ref in zip(starts, weight_refs):
+        for start, weight_ref in zip(starts, weight_refs):
             depth = weight_ref.shape[0]
             weight = weight_ref[:, at]
             part = jnp.dot(
@@ -240,7 +216,7 @@
             )
             total = part if total is None else total + part
             part = jnp.dot(
-                half_ref[:, pl.ds(half_start, depth)],
+                other_tokens_ref[0, :, pl.ds(start, depth)],
                 weight,
                 preferred_element_type=jnp.float32,
             )
@@ -252,10 +228,10 @@
     lax.fori_loop(0, weight_refs[0].shape[1] // tile, column, 0)
 
 
-def project(tokens, half, pieces, rows, totals=(), after=(), last=False):
+def project(tokens, other_tokens, pieces, rows, totals=(), after=(), last=False):
     count = tokens.shape[1]
     columns = pieces[0][1].shape[1]
-    operands = [tokens, half, *(w for _, w in pieces)]
+    operands = [tokens, other_tokens, *(w for _, w in pieces)]
     aliases = {len(operands) + i: i for i in range(2 - last)} if totals else {}
     operands += totals
     depth = sum(w.shape[0] for _, w in pieces)
@@ -417,47 +393,43 @@
 
     own, own_low, own_high, *slices = prepare(gain, next_weights, weights)
 
+    def project_on(totals, pieces, after=(), last=False):
+        return project(tokens, other_tokens, pieces, rows, totals, after, last)
+
+    other_tokens = to_core(tokens)
     ring_1 = along_z(own)
     low_0 = along_x(own_low)
-    arrived = [
-        across_replicas(slices[dy], lambda y, x, dy=dy: (y + dy, x))
-        for dy in range(1, Y)
-    ]
-    count, features = tokens.shape[1:]
-    (half_sent,) = fetch(
-        half_kernel,
-        tokens,
-        [shape((count, features // C), tokens.dtype)],
-        Z * X,
-        "half",
-        [own],
-    )
-    ring_1, low_0, own_high, half_sent = phase([ring_1, low_0, own_high, half_sent])
-
-    ring_2 = along_z(ring_1)
-    high_0 = along_x(own_high)
-    tokens_half = to_core(half_sent)
+    arrived_1 = across_replicas(slices[1], lambda y, x: (y + 1, x))
+    arrived_3 = across_replicas(slices[3], lambda y, x: (y - 1, x))
     tokens, row_scale = fetch(
         load_kernel,
         tokens,
-        [shape(tokens.shape, tokens.dtype), shape((count, BLOCK), jnp.float32)],
+        [shape(tokens.shape, tokens.dtype), shape((tokens.shape[1], BLOCK), jnp.float32)],
         12,
         "load",
-        [ring_1],
-    )
+        [own],
+    )
+    ring_1, low_0, own_high, slice_2 = phase(
+        [ring_1, low_0, own_high, slices[2]], after=[row_scale, arrived_1, arrived_3]
+    )
+
+    ring_2 = along_z(ring_1)
+    high_0 = along_x(own_high)
+    low_1 = along_z(low_0)
+    arrived_2 = across_replicas(slice_2, lambda y, x: (y + 2, x))
+    totals = project_on((), [((0, 0, 0, 0), own), ((1, 0, 0, 0), ring_1)])
     own_sum, other_sum = whole(
         partial_kernel,
         [shape((rows, BLOCK), jnp.float32), shape((rows, BLOCK), jnp.bfloat16)],
         "partial",
-        [snapshot, slices[0], *arrived],
-        after=[row_scale],
+        [snapshot, slices[0], arrived_1, arrived_2, arrived_3],
+        after=[totals[0]],
     )
     other_sum = across_replicas(other_sum, lambda y, x: (y, 1 - x))
-    ring_2, low_0, high_0, other_sum = phase([ring_2, low_0, high_0, other_sum])
+    ring_2, high_0, low_1, other_sum = phase([ring_2, high_0, low_1, other_sum])
 
     ring_3 = along_z(ring_2)
-    low_1 = along_z(low_0)
-    high_2 = along_x(ring_2[half:])
+    low_2 = along_z(low_1)
     new, velocity = whole(
         update_kernel,
         [shape((rows, BLOCK), jnp.bfloat16)] * 2,
@@ -465,62 +437,49 @@
         [snapshot, momentum, own_sum, other_sum],
     )
     new_other = across_replicas(new, lambda y, x: (y, 1 - x))
-    totals = project(
-        tokens,
-        tokens_half,
+    (high_2,) = phase([ring_2[half:]], after=[new_other])
+    high_2 = along_x(high_2)
+    pair = join(new, new_other)
+    pair_1 = across_replicas(pair, lambda y, x: (y - 1, x))
+    pair_3 = across_replicas(pair, lambda y, x: (y + 1, x))
+    totals = project_on(
+        totals,
         [
-            ((0, 0, 0, 0), own),
-            ((1, 0, 0, 0), ring_1),
             ((2, 0, 0, 0), ring_2),
             ((0, 1, 0, 0), low_0),
             ((0, 1, 0, half), high_0),
         ],
-        rows,
-        after=[new],
-    )
-    ring_3, low_1, high_0, high_2, new_other = phase(
-        [ring_3, low_1, high_0, high_2, new_other], after=[totals[0]]
-    )
-
-    low_2 = along_z(low_1)
+        after=[pair],
+    )
+    ring_3, high_0, pair = phase(
+        [ring_3, high_0, pair], after=[totals[0], pair_1, pair_3]
+    )
+
     high_1 = along_z(high_0)
     high_3 = along_x(ring_3[half:])
-    pair = join(new, new_other)
-    pair_1 = across_replicas(pair, lambda y, x: (y - 1, x))
-    pair_3 = across_replicas(pair, lambda y, x: (y + 1, x))
-    totals = project(
-        tokens,
-        tokens_half,
+    pair_2 = across_replicas(pair, lambda y, x: (y + 2, x))
+    totals = project_on(
+        totals,
         [
             ((3, 0, 0, 0), ring_3),
             ((1, 1, 0, 0), low_1),
+        ],
+    )
+    (low_2,) = phase([low_2], after=[totals[0]])
+
+    low_3 = along_z(low_2)
+    own_total, other_total = project_on(
+        totals,
+        [
             ((2, 1, 0, half), high_2),
-        ],
-        rows,
-        totals,
-        after=[pair],
-    )
-    low_2, high_1, high_3, pair = phase(
-        [low_2, high_1, high_3, pair], after=[totals[0], pair_1, pair_3]
-    )
-
-    low_3 = along_z(low_2)
-    pair_2 = across_replicas(pair, lambda y, x: (y + 2, x))
-    own_total, other_total = project(
-        tokens,
-        tokens_half,
-        [
             ((2, 1, 0, 0), low_2),
             ((1, 1, 0, half), high_1),
-            ((3, 1, 0, half), high_3),
         ],
-        rows,
-        totals,
         last=True,
     )
-    low_3, pair_2, other_total = phase([low_3, pair_2, other_total])
-
-    low_3_other = to_core(low_3)
+    low_3, high_3, pair_2, other_total = phase([low_3, high_3, pair_2, other_total])
+
+    low_3_other, high_3_other = to_core(low_3), to_core(high_3)
     other_total = to_core(other_total)
     new_weights, done = whole(
         assemble_kernel,
@@ -530,7 +489,12 @@
     )
     next_keys = finish(
         tokens,
-        [((3, 1, 0, 0), low_3), ((3, 1, 1, 0), low_3_other)],
+        [
+            ((3, 1, 0, 0), low_3),
+            ((3, 1, 0, half), high_3),
+            ((3, 1, 1, 0), low_3_other),
+            ((3, 1, 1, half), high_3_other),
+        ],
         rows,
         own_total,
         other_total,

time: 105 us -> 88.9 us (0.85)
  waiting for transfers between devices: 33.7 us -> 21.4 us
  starting transfers between devices: 39.8 us -> 37.3 us
  Pallas kernels: 30.6 us -> 29.2 us
    ppermute x4, waiting for transfers between devices: 14.5 us -> 4.79 us  [along_x(): return lax.ppermute(value, 'fsdp', fsdp_perm(lambda z, x, c: (z, 1 - x, c)))]
    ppermute x8, starting transfers between devices: 15.6 us -> 12 us  [across_replicas(): return lax.ppermute(value, 'replica', pairs)]
    ppermute x4, starting transfers between devices: 8.6 us -> 12 us  [along_x(): return lax.ppermute(value, 'fsdp', fsdp_perm(lambda z, x, c: (z, 1 - x, c)))]
    pallas_call x2 -> x1, Pallas kernels: 7.82 us -> 4.92 us  [fetch(): pl.pallas_call(run, in_specs=[pl.BlockSpec(memory_space=pltpu.HBM)] + [pl...]
    ppermute x3 -> x4, starting transfers between devices: 6.58 us -> 4.56 us  [to_core(): return lax.ppermute(value, 'fsdp', fsdp_perm(lambda z, x, c: (z, x, 1 - c)))]
    ppermute x7, waiting for transfers between devices: 6.99 us -> 5.59 us  [along_z(): lax.ppermute(value, 'fsdp', fsdp_perm(lambda z, x, c: (z + 1 - 2 * c, x,...]
    ppermute x8, waiting for transfers between devices: 9.68 us -> 8.28 us  [across_replicas(): return lax.ppermute(value, 'replica', pairs)]
    pallas_call x3 -> x4, Pallas kernels: 15.2 us -> 15.8 us  [project(): pl.pallas_call(functools.partial(project_kernel, places, rows, bool(total...]
  transfers between devices with their start and end apart: 22 -> 23, of which waited for: 10 -> 10; matrix products, arithmetic and copies ran while one was open for 0% -> 0% of each run, Pallas kernels for 25% -> 29%
where the time goes in v3:
time: 88.9 us; the launch traced here: 88.7 us
  starting transfers between devices  37.3 us (42%)
  Pallas kernels  29.2 us (33%)
  waiting for transfers between devices  21.4 us (24%)
    pallas_call x4, Pallas kernels, project(): pl.pallas_call(functools.partial(project_kernel, places, rows, bool(total...  15.8 us
    ppermute x4, starting transfers between devices, along_x(): return lax.ppermute(value, 'fsdp', fsdp_perm(lambda z, x, c: (z, 1 - x, c)))  12 us
    ppermute x8, starting transfers between devices, across_replicas(): return lax.ppermute(value, 'replica', pairs)  12 us
    ppermute x7, starting transfers between devices, along_z(): lax.ppermute(value, 'fsdp', fsdp_perm(lambda z, x, c: (z + 1 - 2 * c, x,...  8.68 us
    ppermute x8, waiting for transfers between devices, across_replicas(): return lax.ppermute(value, 'replica', pairs)  8.28 us
    ppermute x7, waiting for transfers between devices, along_z(): lax.ppermute(value, 'fsdp', fsdp_perm(lambda z, x, c: (z + 1 - 2 * c, x,...  5.59 us
    pallas_call x1, Pallas kernels, fetch(): pl.pallas_call(run, in_specs=[pl.BlockSpec(memory_space=pltpu.HBM)] + [pl...  4.92 us
    ppermute x4, waiting for transfers between devices, along_x(): return lax.ppermute(value, 'fsdp', fsdp_perm(lambda z, x, c: (z, 1 - x, c)))  4.79 us
  transfers between devices with their start and end apart: 23, of which 10 were waited for; matrix products, arithmetic and copies ran while one was open for 0% of the time, Pallas kernels for 29%

profile of v3, /device:TPU:1, one launch (start us, length us, event | category | flops | bytes accessed | tf_op | source)
XLA Modules:
  0.0 88.7 jit_solution(6999760050148611564)
XLA Ops:
  0.6 1.5 %collective-permute-start.8 = (bf16[1,768,8192]{2,1,0:T(8,128)(2,1)}, bf16[1,768,8192]{2,1,0:T(8,128)(2,1)S(1)}, u32[]{:S(2)}, u32[]{:S(2)}) collective-permute-start(bf16[1,768,8192]{2,1,0:T(8,128)(2,1)} %tokens_hbm.1), channel_id=1, source_target_pairs={{0,1},{1,0},{2,3},{3,2},{4,5},{5,4},{6,7},{7,6},{8,9},{9,8},{10,11... | collective-permute-start | bytes 37748744 | tf_op jit(solution)/shard_map/ppermute | solution.py:41
  2.1 1.6 %prepare.1 = (bf16[512,1024]{1,0:T(8,128)(2,1)S(1)}, bf16[256,1024]{1,0:T(8,128)(2,1)S(1)}, bf16[256,1024]{1,0:T(8,128)(2,1)S(1)}, bf16[512,256]{1,0:T(8,128)(2,...) custom-call(f32[1,8192]{1,0:T(1,128)} %gain_hbm.1, ...), custom_call_target="tpu_custom_call" | custom-call | flops 524288 | bytes 2097152 | tf_op jit(solution)/shard_map/prepare/pallas_call | solution.py:111
  3.8 3.9 %collective-permute-start = (bf16[512,1024]{1,0:T(8,128)(2,1)S(1)}, bf16[512,1024]{1,0:T(8,128)(2,1)S(1)}, u32[]{:S(2)}, u32[]{:S(2)}) collective-permute-start(bf16[512,1024]{1,0:T(8,128)(2,1)S(1)} %get-tuple-element.41.refs_0_.refs_2_), channel_id=1, source_target_pairs={{0,4},{1,13},{2,6},{3,15},{4,8},{5,1},{6,10},{7,3},{8,12},{9,5},{1... | collective-permute-start | bytes 3145736 | tf_op jit(solution)/shard_map/ppermute | solution.py:31
  7.7 2.7 %collective-permute-start.1 = (bf16[256,1024]{1,0:T(8,128)(2,1)S(1)}, bf16[256,1024]{1,0:T(8,128)(2,1)S(1)}, u32[]{:S(2)}, u32[]{:S(2)}) collective-permute-start(bf16[256,1024]{1,0:T(8,128)(2,1)S(1)} %get-tuple-element.43), channel_id=1, source_target_pairs={{0,2},{1,3},{2,0},{3,1},{4,6},{5,7},{6,4},{7,5},{8,10},{9,11},{10,... | collective-permute-start | bytes 1572872 | tf_op jit(solution)/shard_map/ppermute | solution.py:37
  10.4 1.3 %collective-permute-start.2 = (bf16[512,256]{1,0:T(8,128)(2,1)S(1)}, bf16[512,256]{1,0:T(8,128)(2,1)S(1)}, u32[]{:S(2)}, u32[]{:S(2)}) collective-permute-start(bf16[512,256]{1,0:T(8,128)(2,1)S(1)} %get-tuple-element.47), channel_id=1, source_target_pairs={{0,32},{16,48},{32,64},{48,80},{64,96},{80,112},{96,0},{112,16},{1... | collective-permute-start | bytes 786440 | tf_op jit(solution)/shard_map/ppermute | solution.py:50
  11.7 1.4 %collective-permute-start.3 = (bf16[512,256]{1,0:T(8,128)(2,1)S(1)}, bf16[512,256]{1,0:T(8,128)(2,1)S(1)}, u32[]{:S(2)}, u32[]{:S(2)}) collective-permute-start(bf16[512,256]{1,0:T(8,128)(2,1)S(1)} %get-tuple-element.48), channel_id=1, source_target_pairs={{0,96},{16,112},{32,0},{48,16},{64,32},{80,48},{96,64},{112,80},{1... | collective-permute-start | bytes 786440 | tf_op jit(solution)/shard_map/ppermute | solution.py:50
  13.1 4.9 %load.1 = (bf16[1,768,8192]{2,1,0:T(8,128)(2,1)S(1)}, f32[768,128]{1,0:T(8,128)S(1)}) custom-call(bf16[1,768,8192]{2,1,0:T(8,128)(2,1)} %tokens_hbm.1, bf16[512,1024]{1,0:T(8,128)(2,1)S(1)} %get-tuple-element.41.refs_0_.refs_2_), custom_call_target="tpu_custom_call" | custom-call | flops 6291456 | bytes 12582912 | tf_op jit(solution)/shard_map/load/pallas_call | solution.py:179
  18.1 0.8 collective-permute-done.2.refs_5_.refs_2_
  18.9 0.4 collective-permute-done.3.refs_6_.refs_4_
  19.2 2.2 %collective-permute-done.1.refs_1_ = bf16[256,1024]{1,0:T(8,128)(2,1)S(1)} collective-permute-done((bf16[256,1024]{1,0:T(8,128)(2,1)S(1)}, bf16[256,1024]{1,0:T(8,128)(2,1)S(1)}, u32[]{:S(2)}, u32[]{:S(2)}) %collective-permute-start.1) | collective-permute-done | bytes 524320 | tf_op jit(solution)/shard_map/ppermute | solution.py:37
  21.5 0.0 collective-permute-done.refs_0_
  21.5 1.4 %collective-permute-start.4 = (bf16[512,1024]{1,0:T(8,128)(2,1)S(1)}, bf16[512,1024]{1,0:T(8,128)(2,1)S(1)}, u32[]{:S(2)}, u32[]{:S(2)}) collective-permute-start(bf16[512,1024]{1,0:T(8,128)(2,1)S(1)} %get-tuple-element.49.refs_3_), channel_id=1, source_target_pairs={{0,4},{1,13},{2,6},{3,15},{4,8},{5,1},{6,10},{7,3},{8,12},{9,5},{1... | collective-permute-start | bytes 3145736 | tf_op jit(solution)/shard_map/ppermute | solution.py:31
  22.9 0.1 collective-permute-start.6
  22.9 2.7 %collective-permute-start.5 = (bf16[256,1024]{1,0:T(8,128)(2,1)S(1)}, bf16[256,1024]{1,0:T(8,128)(2,1)S(1)}, u32[]{:S(2)}, u32[]{:S(2)}) collective-permute-start(bf16[256,1024]{1,0:T(8,128)(2,1)S(1)} %get-tuple-element.50), channel_id=1, source_target_pairs={{0,2},{1,3},{2,0},{3,1},{4,6},{5,7},{6,4},{7,5},{8,10},{9,11},{10,... | collective-permute-start | bytes 1572872 | tf_op jit(solution)/shard_map/ppermute | solution.py:37
  25.7 2.9 %collective-permute-start.7 = (bf16[512,256]{1,0:T(8,128)(2,1)S(1)}, bf16[512,256]{1,0:T(8,128)(2,1)S(1)}, u32[]{:S(2)}, u32[]{:S(2)}) collective-permute-start(bf16[512,256]{1,0:T(8,128)(2,1)S(1)} %get-tuple-element.53), channel_id=1, source_target_pairs={{0,64},{16,80},{32,96},{48,112},{64,0},{80,16},{96,32},{112,48},{1... | collective-permute-start | bytes 786440 | tf_op jit(solution)/shard_map/ppermute | solution.py:50
  28.6 0.0 collective-permute-done.8.refs_1_
  28.6 4.0 %project.4 = (f32[768,1024]{1,0:T(8,128)S(1)}, f32[768,1024]{1,0:T(8,128)S(1)}) custom-call(bf16[1,768,8192]{2,1,0:T(8,128)(2,1)S(1)} %get-tuple-element.42.refs_0_, bf16[1,768,8192]{2,1,0:T(8,128)(2,1)S(1)} %collective-permute-done.8.refs_1_, bf16[512,1024]{1,0:T(8,128)(2,1)S(1)} %get-tuple-element.41.refs_0_.refs_2_, ...), custom_call_target="tpu_custom_call" | custom-call | flops 3221225472 | bytes 2097152 | tf_op jit(solution)/shard_map/project/pallas_call | solution.py:240
  32.6 1.4 %collective-permute-done.7.refs_3_ = bf16[512,256]{1,0:T(8,128)(2,1)S(1)} collective-permute-done((bf16[512,256]{1,0:T(8,128)(2,1)S(1)}, bf16[512,256]{1,0:T(8,128)(2,1)S(1)}, u32[]{:S(2)}, u32[]{:S(2)}) %collective-permute-start.7) | collective-permute-done | bytes 262176 | tf_op jit(solution)/shard_map/ppermute | solution.py:50
  33.9 1.1 %partial.1 = (f32[512,128]{1,0:T(8,128)S(1)}, bf16[512,128]{1,0:T(8,128)(2,1)S(1)}) custom-call(f32[512,1024]{1,0:T(8,128)S(1)} %copy-done, bf16[512,256]{1,0:T(8,128)(2,1)S(1)} %get-tuple-element.52.refs_1_, bf16[512,256]{1,0:T(8,128)(2,1)S(1)} %collective-permute-done.2.refs_5_.refs_2_, bf16[512,256]{1,0:T(8,128)(2,1)S(1)} %collective-permute-done.7.refs_3_, ...), custom_call_target="tpu_custom_call" | custom-call | flops 25165824 | bytes 6291456 | tf_op jit(solution)/shard_map/partial/pallas_call | solution.py:378
  35.1 0.4 collective-permute-start.9
  35.5 5.6 %collective-permute-done.6.refs_2_ = bf16[256,1024]{1,0:T(8,128)(2,1)S(1)} collective-permute-done((bf16[256,1024]{1,0:T(8,128)(2,1)S(1)}, bf16[256,1024]{1,0:T(8,128)(2,1)S(1)}, u32[]{:S(2)}, u32[]{:S(2)}) %collective-permute-start.6) | collective-permute-done | bytes 524320 | tf_op jit(solution)/shard_map/ppermute | solution.py:31
  41.0 0.0 collective-permute-done.4.refs_0_
  41.0 0.0 collective-permute-done.9.refs_3_
  41.1 2.4 %collective-permute-start.11 = (bf16[512,1024]{1,0:T(8,128)(2,1)S(1)}, bf16[512,1024]{1,0:T(8,128)(2,1)S(1)}, u32[]{:S(2)}, u32[]{:S(2)}) collective-permute-start(bf16[512,1024]{1,0:T(8,128)(2,1)S(1)} %get-tuple-element.57.refs_2_), channel_id=1, source_target_pairs={{0,4},{1,13},{2,6},{3,15},{4,8},{5,1},{6,10},{7,3},{8,12},{9,5},{1... | collective-permute-start | bytes 3145736 | tf_op jit(solution)/shard_map/ppermute | solution.py:31
  43.4 0.8 update.1
  44.2 1.2 %collective-permute-start.12 = (bf16[512,128]{1,0:T(8,128)(2,1)S(1)}, bf16[512,128]{1,0:T(8,128)(2,1)S(1)}, u32[]{:S(2)}, u32[]{:S(2)}) collective-permute-start(bf16[512,128]{1,0:T(8,128)(2,1)S(1)} %get-tuple-element.61.refs_0_), channel_id=1, source_target_pairs={{0,16},{16,0},{32,48},{48,32},{64,80},{80,64},{96,112},{112,96},{1... | collective-permute-start | bytes 393224 | tf_op jit(solution)/shard_map/ppermute | solution.py:50
  45.5 0.1 collective-permute-start.10
  45.5 3.4 %collective-permute-done.12.refs_1_ = bf16[512,128]{1,0:T(8,128)(2,1)S(1)} collective-permute-done((bf16[512,128]{1,0:T(8,128)(2,1)S(1)}, bf16[512,128]{1,0:T(8,128)(2,1)S(1)}, u32[]{:S(2)}, u32[]{:S(2)}) %collective-permute-start.12) | collective-permute-done | bytes 131104 | tf_op jit(solution)/shard_map/ppermute | solution.py:50
  49.0 2.8 %collective-permute-start.13 = (bf16[512,256]{1,0:T(8,128)(2,1)S(1)}, bf16[512,256]{1,0:T(8,128)(2,1)S(1)}, u32[]{:S(2)}, u32[]{:S(2)}) collective-permute-start(bf16[512,256]{1,0:T(8,128)(2,1)S(1)} %join.1.refs_7_.refs_2_), channel_id=1, source_target_pairs={{0,96},{16,112},{32,0},{48,16},{64,32},{80,48},{96,64},{112,80},{1... | collective-permute-start | bytes 786440 | tf_op jit(solution)/shard_map/ppermute | solution.py:50
  51.8 3.0 %collective-permute-start.18 = (bf16[256,1024]{1,0:T(8,128)(2,1)S(1)}, bf16[256,1024]{1,0:T(8,128)(2,1)S(1)}, u32[]{:S(2)}, u32[]{:S(2)}) collective-permute-start(bf16[256,1024]{1,0:T(8,128)(2,1)S(1)} %phase.10), channel_id=1, source_target_pairs={{0,2},{1,3},{2,0},{3,1},{4,6},{5,7},{6,4},{7,5},{8,10},{9,11},{10,... | collective-permute-start | bytes 1572872 | tf_op jit(solution)/shard_map/ppermute | solution.py:37
  54.8 4.6 %project.5 = (f32[768,1024]{1,0:T(8,128)S(1)}, f32[768,1024]{1,0:T(8,128)S(1)}) custom-call(bf16[1,768,8192]{2,1,0:T(8,128)(2,1)S(1)} %get-tuple-element.42.refs_0_, bf16[1,768,8192]{2,1,0:T(8,128)(2,1)S(1)} %collective-permute-done.8.refs_1_, bf16[512,1024]{1,0:T(8,128)(2,1)S(1)} %get-tuple-element.57.refs_2_, ...), custom_call_target="tpu_custom_call", output_to_operand_aliasing={{0}: (5, {}), {1}: (6, {})} | custom-call | flops 3221225472 | bytes 2097152 | tf_op jit(solution)/shard_map/project/pallas_call | solution.py:240
  59.4 0.0 collective-permute-done.13.refs_4_.refs_1_
  59.5 0.1 collective-permute-start.19
  59.6 3.8 %project.6 = (f32[768,1024]{1,0:T(8,128)S(1)}, f32[768,1024]{1,0:T(8,128)S(1)}) custom-call(bf16[1,768,8192]{2,1,0:T(8,128)(2,1)S(1)} %get-tuple-element.42.refs_0_, bf16[1,768,8192]{2,1,0:T(8,128)(2,1)S(1)} %collective-permute-done.8.refs_1_, bf16[512,1024]{1,0:T(8,128)(2,1)S(1)} %get-tuple-element.64.refs_2_, ...), custom_call_target="tpu_custom_call", output_to_operand_aliasing={{0}: (4, {}), {1}: (5, {})} | custom-call | flops 2415919104 | bytes 1572864 | tf_op jit(solution)/shard_map/project/pallas_call | solution.py:240
  63.4 0.0 collective-permute-done.10.refs_0_
  63.4 0.8 collective-permute-start.15
  64.2 3.5 %collective-permute-start.16 = (bf16[256,1024]{1,0:T(8,128)(2,1)S(1)}, bf16[256,1024]{1,0:T(8,128)(2,1)S(1)}, u32[]{:S(2)}, u32[]{:S(2)}) collective-permute-start(bf16[256,1024]{1,0:T(8,128)(2,1)S(1)} %slice.6), channel_id=1, source_target_pairs={{0,2},{1,3},{2,0},{3,1},{4,6},{5,7},{6,4},{7,5},{8,10},{9,11},{10,... | collective-permute-start | bytes 1572872 | tf_op jit(solution)/shard_map/ppermute | solution.py:37
  67.7 2.0 %collective-permute-start.17 = (bf16[512,256]{1,0:T(8,128)(2,1)S(1)}, bf16[512,256]{1,0:T(8,128)(2,1)S(1)}, u32[]{:S(2)}, u32[]{:S(2)}) collective-permute-start(bf16[512,256]{1,0:T(8,128)(2,1)S(1)} %get-tuple-element.67.refs_0_), channel_id=1, source_target_pairs={{0,64},{16,80},{32,96},{48,112},{64,0},{80,16},{96,32},{112,48},{1... | collective-permute-start | bytes 786440 | tf_op jit(solution)/shard_map/ppermute | solution.py:50
  69.7 3.4 %project.7 = (f32[768,1024]{1,0:T(8,128)S(1)}, bf16[768,1024]{1,0:T(8,128)(2,1)S(1)}) custom-call(bf16[1,768,8192]{2,1,0:T(8,128)(2,1)S(1)} %get-tuple-element.42.refs_0_, bf16[1,768,8192]{2,1,0:T(8,128)(2,1)S(1)} %collective-permute-done.8.refs_1_, bf16[256,1024]{1,0:T(8,128)(2,1)S(1)} %collective-permute-done.18.refs_2_, ...), custom_call_target="tpu_custom_call", output_to_operand_aliasing={{0}: (5, {})} | custom-call | flops 2415919104 | bytes 1572864 | tf_op jit(solution)/shard_map/project/pallas_call | solution.py:240
  73.2 2.3 %collective-permute-done.17.refs_2_ = bf16[512,256]{1,0:T(8,128)(2,1)S(1)} collective-permute-done((bf16[512,256]{1,0:T(8,128)(2,1)S(1)}, bf16[512,256]{1,0:T(8,128)(2,1)S(1)}, u32[]{:S(2)}, u32[]{:S(2)}) %collective-permute-start.17) | collective-permute-done | bytes 262176 | tf_op jit(solution)/shard_map/ppermute | solution.py:50
  75.5 2.6 %collective-permute-done.16.refs_1_ = bf16[256,1024]{1,0:T(8,128)(2,1)S(1)} collective-permute-done((bf16[256,1024]{1,0:T(8,128)(2,1)S(1)}, bf16[256,1024]{1,0:T(8,128)(2,1)S(1)}, u32[]{:S(2)}, u32[]{:S(2)}) %collective-permute-start.16) | collective-permute-done | bytes 524320 | tf_op jit(solution)/shard_map/ppermute | solution.py:37
  78.1 2.5 %collective-permute-start.22 = (bf16[768,1024]{1,0:T(8,128)(2,1)S(1)}, bf16[768,1024]{1,0:T(8,128)(2,1)S(1)}, u32[]{:S(2)}, u32[]{:S(2)}) collective-permute-start(bf16[768,1024]{1,0:T(8,128)(2,1)S(1)} %get-tuple-element.74), channel_id=1, source_target_pairs={{0,1},{1,0},{2,3},{3,2},{4,5},{5,4},{6,7},{7,6},{8,9},{9,8},{10,11... | collective-permute-start | bytes 4718600 | tf_op jit(solution)/shard_map/ppermute | solution.py:41
  80.6 0.0 collective-permute-start.20
  80.6 0.5 collective-permute-start.21
  81.1 1.3 %assemble.1 = (bf16[512,1024]{1,0:T(8,128)(2,1)}, f32[8,128]{1,0:T(8,128)S(1)}) custom-call(bf16[512,256]{1,0:T(8,128)(2,1)S(1)} %get-tuple-element.67.refs_0_, bf16[512,256]{1,0:T(8,128)(2,1)S(1)} %collective-permute-done.13.refs_4_.refs_1_, bf16[512,256]{1,0:T(8,128)(2,1)S(1)} %get-tuple-element.75.refs_2_, ...), custom_call_target="tpu_custom_call" | custom-call | flops 8388608 | bytes 2097152 | tf_op jit(solution)/shard_map/assemble/pallas_call | solution.py:378
  82.4 2.0 %collective-permute-done.20.refs_3_ = bf16[256,1024]{1,0:T(8,128)(2,1)S(1)} collective-permute-done((bf16[256,1024]{1,0:T(8,128)(2,1)S(1)}, bf16[256,1024]{1,0:T(8,128)(2,1)S(1)}, u32[]{:S(2)}, u32[]{:S(2)}) %collective-permute-start.20) | collective-permute-done | bytes 524320 | tf_op jit(solution)/shard_map/ppermute | solution.py:41
  84.4 0.7 collective-permute-done.21.refs_4_
  85.1 3.6 %finish.1 = bf16[1,768,1024]{2,1,0:T(8,128)(2,1)} custom-call(bf16[1,768,8192]{2,1,0:T(8,128)(2,1)S(1)} %get-tuple-element.42.refs_0_, bf16[256,1024]{1,0:T(8,128)(2,1)S(1)} %get-tuple-element.71.refs_1_, bf16[256,1024]{1,0:T(8,128)(2,1)S(1)} %get-tuple-element.72.refs_2_, bf16[256,1024]{1,0:T(8,128)(2,1)S(1)} %collective-permute-done.20.refs_3_, ...), custom_call_target="tpu_custom_call" | custom-call | flops 1610612736 | bytes 2097152 | tf_op jit(solution)/shard_map/finish/pallas_call | solution.py:294
  (21 shorter events, 0.2 us)
Async XLA Ops:
  0.6 28.0 %collective-permute-start.8 = (bf16[1,768,8192]{2,1,0:T(8,128)(2,1)}, bf16[1,768,8192]{2,1,0:T(8,128)(2,1)S(1)}, u32[]{:S(2)}, u32[]{:S(2)}) collective-permute-start(bf16[1,768,8192]{2,1,0:T(8,128)(2,1)} %tokens_hbm.1), channel_id=1, source_target_pairs={{0,1},{1,0},{2,3},{3,2},{4,5},{5,4},{6,7},{7,6},{8,9},{9,8},{10,11... | collective-permute-start | bytes 37748744 | tf_op jit(solution)/shard_map/ppermute | solution.py:41
  3.8 17.7 %collective-permute-start = (bf16[512,1024]{1,0:T(8,128)(2,1)S(1)}, bf16[512,1024]{1,0:T(8,128)(2,1)S(1)}, u32[]{:S(2)}, u32[]{:S(2)}) collective-permute-start(bf16[512,1024]{1,0:T(8,128)(2,1)S(1)} %get-tuple-element.41.refs_0_.refs_2_), channel_id=1, source_target_pairs={{0,4},{1,13},{2,6},{3,15},{4,8},{5,1},{6,10},{7,3},{8,12},{9,5},{1... | collective-permute-start | bytes 3145736 | tf_op jit(solution)/shard_map/ppermute | solution.py:31
  7.7 13.8 %collective-permute-start.1 = (bf16[256,1024]{1,0:T(8,128)(2,1)S(1)}, bf16[256,1024]{1,0:T(8,128)(2,1)S(1)}, u32[]{:S(2)}, u32[]{:S(2)}) collective-permute-start(bf16[256,1024]{1,0:T(8,128)(2,1)S(1)} %get-tuple-element.43), channel_id=1, source_target_pairs={{0,2},{1,3},{2,0},{3,1},{4,6},{5,7},{6,4},{7,5},{8,10},{9,11},{10,... | collective-permute-start | bytes 1572872 | tf_op jit(solution)/shard_map/ppermute | solution.py:37
  10.4 8.5 %collective-permute-start.2 = (bf16[512,256]{1,0:T(8,128)(2,1)S(1)}, bf16[512,256]{1,0:T(8,128)(2,1)S(1)}, u32[]{:S(2)}, u32[]{:S(2)}) collective-permute-start(bf16[512,256]{1,0:T(8,128)(2,1)S(1)} %get-tuple-element.47), channel_id=1, source_target_pairs={{0,32},{16,48},{32,64},{48,80},{64,96},{80,112},{96,0},{112,16},{1... | collective-permute-start | bytes 786440 | tf_op jit(solution)/shard_map/ppermute | solution.py:50
  11.7 7.5 %collective-permute-start.3 = (bf16[512,256]{1,0:T(8,128)(2,1)S(1)}, bf16[512,256]{1,0:T(8,128)(2,1)S(1)}, u32[]{:S(2)}, u32[]{:S(2)}) collective-permute-start(bf16[512,256]{1,0:T(8,128)(2,1)S(1)} %get-tuple-element.48), channel_id=1, source_target_pairs={{0,96},{16,112},{32,0},{48,16},{64,32},{80,48},{96,64},{112,80},{1... | collective-permute-start | bytes 786440 | tf_op jit(solution)/shard_map/ppermute | solution.py:50
  21.5 19.6 %collective-permute-start.4 = (bf16[512,1024]{1,0:T(8,128)(2,1)S(1)}, bf16[512,1024]{1,0:T(8,128)(2,1)S(1)}, u32[]{:S(2)}, u32[]{:S(2)}) collective-permute-start(bf16[512,1024]{1,0:T(8,128)(2,1)S(1)} %get-tuple-element.49.refs_3_), channel_id=1, source_target_pairs={{0,4},{1,13},{2,6},{3,15},{4,8},{5,1},{6,10},{7,3},{8,12},{9,5},{1... | collective-permute-start | bytes 3145736 | tf_op jit(solution)/shard_map/ppermute | solution.py:31
  22.9 18.2 %collective-permute-start.6 = (bf16[256,1024]{1,0:T(8,128)(2,1)S(1)}, bf16[256,1024]{1,0:T(8,128)(2,1)S(1)}, u32[]{:S(2)}, u32[]{:S(2)}) collective-permute-start(bf16[256,1024]{1,0:T(8,128)(2,1)S(1)} %get-tuple-element.51.refs_3_), channel_id=1, source_target_pairs={{0,4},{1,13},{2,6},{3,15},{4,8},{5,1},{6,10},{7,3},{8,12},{9,5},{1... | collective-permute-start | bytes 1572872 | tf_op jit(solution)/shard_map/ppermute | solution.py:31
  22.9 18.1 %collective-permute-start.5 = (bf16[256,1024]{1,0:T(8,128)(2,1)S(1)}, bf16[256,1024]{1,0:T(8,128)(2,1)S(1)}, u32[]{:S(2)}, u32[]{:S(2)}) collective-permute-start(bf16[256,1024]{1,0:T(8,128)(2,1)S(1)} %get-tuple-element.50), channel_id=1, source_target_pairs={{0,2},{1,3},{2,0},{3,1},{4,6},{5,7},{6,4},{7,5},{8,10},{9,11},{10,... | collective-permute-start | bytes 1572872 | tf_op jit(solution)/shard_map/ppermute | solution.py:37
  25.7 8.3 %collective-permute-start.7 = (bf16[512,256]{1,0:T(8,128)(2,1)S(1)}, bf16[512,256]{1,0:T(8,128)(2,1)S(1)}, u32[]{:S(2)}, u32[]{:S(2)}) collective-permute-start(bf16[512,256]{1,0:T(8,128)(2,1)S(1)} %get-tuple-element.53), channel_id=1, source_target_pairs={{0,64},{16,80},{32,96},{48,112},{64,0},{80,16},{96,32},{112,48},{1... | collective-permute-start | bytes 786440 | tf_op jit(solution)/shard_map/ppermute | solution.py:50
  28.6 5.4 %copy-start = (f32[512,1024]{1,0:T(8,128)S(1)}, f32[512,1024]{1,0:T(8,128)}, u32[]{:S(2)}) copy-start(f32[512,1024]{1,0:T(8,128)} %refs_0_.3) | copy-start | bytes 6291460
  33.9 9.5 %copy-start.1 = (bf16[512,128]{1,0:T(8,128)(2,1)S(1)}, bf16[512,128]{1,0:T(8,128)(2,1)}, u32[]{:S(2)}) copy-start(bf16[512,128]{1,0:T(8,128)(2,1)} %refs_1_.1) | copy-start | bytes 393220
  35.1 6.0 %collective-permute-start.9 = (bf16[512,128]{1,0:T(8,128)(2,1)S(1)}, bf16[512,128]{1,0:T(8,128)(2,1)S(1)}, u32[]{:S(2)}, u32[]{:S(2)}) collective-permute-start(bf16[512,128]{1,0:T(8,128)(2,1)S(1)} %get-tuple-element.55), channel_id=1, source_target_pairs={{0,16},{16,0},{32,48},{48,32},{64,80},{80,64},{96,112},{112,96},{1... | collective-permute-start | bytes 393224 | tf_op jit(solution)/shard_map/ppermute | solution.py:50
  41.1 18.4 %collective-permute-start.11 = (bf16[512,1024]{1,0:T(8,128)(2,1)S(1)}, bf16[512,1024]{1,0:T(8,128)(2,1)S(1)}, u32[]{:S(2)}, u32[]{:S(2)}) collective-permute-start(bf16[512,1024]{1,0:T(8,128)(2,1)S(1)} %get-tuple-element.57.refs_2_), channel_id=1, source_target_pairs={{0,4},{1,13},{2,6},{3,15},{4,8},{5,1},{6,10},{7,3},{8,12},{9,5},{1... | collective-permute-start | bytes 3145736 | tf_op jit(solution)/shard_map/ppermute | solution.py:31
  44.2 4.8 %collective-permute-start.12 = (bf16[512,128]{1,0:T(8,128)(2,1)S(1)}, bf16[512,128]{1,0:T(8,128)(2,1)S(1)}, u32[]{:S(2)}, u32[]{:S(2)}) collective-permute-start(bf16[512,128]{1,0:T(8,128)(2,1)S(1)} %get-tuple-element.61.refs_0_), channel_id=1, source_target_pairs={{0,16},{16,0},{32,48},{48,32},{64,80},{80,64},{96,112},{112,96},{1... | collective-permute-start | bytes 393224 | tf_op jit(solution)/shard_map/ppermute | solution.py:50
  45.5 18.0 %collective-permute-start.10 = (bf16[256,1024]{1,0:T(8,128)(2,1)S(1)}, bf16[256,1024]{1,0:T(8,128)(2,1)S(1)}, u32[]{:S(2)}, u32[]{:S(2)}) collective-permute-start(bf16[256,1024]{1,0:T(8,128)(2,1)S(1)} %get-tuple-element.56.refs_3_), channel_id=1, source_target_pairs={{0,4},{1,13},{2,6},{3,15},{4,8},{5,1},{6,10},{7,3},{8,12},{9,5},{1... | collective-permute-start | bytes 1572872 | tf_op jit(solution)/shard_map/ppermute | solution.py:31
  49.0 10.4 %collective-permute-start.13 = (bf16[512,256]{1,0:T(8,128)(2,1)S(1)}, bf16[512,256]{1,0:T(8,128)(2,1)S(1)}, u32[]{:S(2)}, u32[]{:S(2)}) collective-permute-start(bf16[512,256]{1,0:T(8,128)(2,1)S(1)} %join.1.refs_7_.refs_2_), channel_id=1, source_target_pairs={{0,96},{16,112},{32,0},{48,16},{64,32},{80,48},{96,64},{112,80},{1... | collective-permute-start | bytes 786440 | tf_op jit(solution)/shard_map/ppermute | solution.py:50
  51.8 7.6 %collective-permute-start.14 = (bf16[512,256]{1,0:T(8,128)(2,1)S(1)}, bf16[512,256]{1,0:T(8,128)(2,1)S(1)}, u32[]{:S(2)}, u32[]{:S(2)}) collective-permute-start(bf16[512,256]{1,0:T(8,128)(2,1)S(1)} %join.1.refs_7_.refs_2_), channel_id=1, source_target_pairs={{0,32},{16,48},{32,64},{48,80},{64,96},{80,112},{96,0},{112,16},{1... | collective-permute-start | bytes 786440 | tf_op jit(solution)/shard_map/ppermute | solution.py:50
  51.8 17.9 %collective-permute-start.18 = (bf16[256,1024]{1,0:T(8,128)(2,1)S(1)}, bf16[256,1024]{1,0:T(8,128)(2,1)S(1)}, u32[]{:S(2)}, u32[]{:S(2)}) collective-permute-start(bf16[256,1024]{1,0:T(8,128)(2,1)S(1)} %phase.10), channel_id=1, source_target_pairs={{0,2},{1,3},{2,0},{3,1},{4,6},{5,7},{6,4},{7,5},{8,10},{9,11},{10,... | collective-permute-start | bytes 1572872 | tf_op jit(solution)/shard_map/ppermute | solution.py:37
  59.5 10.2 %collective-permute-start.19 = (bf16[256,1024]{1,0:T(8,128)(2,1)S(1)}, bf16[256,1024]{1,0:T(8,128)(2,1)S(1)}, u32[]{:S(2)}, u32[]{:S(2)}) collective-permute-start(bf16[256,1024]{1,0:T(8,128)(2,1)S(1)} %get-tuple-element.68), channel_id=1, source_target_pairs={{0,4},{1,13},{2,6},{3,15},{4,8},{5,1},{6,10},{7,3},{8,12},{9,5},{1... | collective-permute-start | bytes 1572872 | tf_op jit(solution)/shard_map/ppermute | solution.py:31
  63.4 12.1 %collective-permute-start.15 = (bf16[256,1024]{1,0:T(8,128)(2,1)S(1)}, bf16[256,1024]{1,0:T(8,128)(2,1)S(1)}, u32[]{:S(2)}, u32[]{:S(2)}) collective-permute-start(bf16[256,1024]{1,0:T(8,128)(2,1)S(1)} %phase.9.refs_3_), channel_id=1, source_target_pairs={{0,4},{1,13},{2,6},{3,15},{4,8},{5,1},{6,10},{7,3},{8,12},{9,5},{1... | collective-permute-start | bytes 1572872 | tf_op jit(solution)/shard_map/ppermute | solution.py:31
  64.2 13.9 %collective-permute-start.16 = (bf16[256,1024]{1,0:T(8,128)(2,1)S(1)}, bf16[256,1024]{1,0:T(8,128)(2,1)S(1)}, u32[]{:S(2)}, u32[]{:S(2)}) collective-permute-start(bf16[256,1024]{1,0:T(8,128)(2,1)S(1)} %slice.6), channel_id=1, source_target_pairs={{0,2},{1,3},{2,0},{3,1},{4,6},{5,7},{6,4},{7,5},{8,10},{9,11},{10,... | collective-permute-start | bytes 1572872 | tf_op jit(solution)/shard_map/ppermute | solution.py:37
  67.7 7.8 %collective-permute-start.17 = (bf16[512,256]{1,0:T(8,128)(2,1)S(1)}, bf16[512,256]{1,0:T(8,128)(2,1)S(1)}, u32[]{:S(2)}, u32[]{:S(2)}) collective-permute-start(bf16[512,256]{1,0:T(8,128)(2,1)S(1)} %get-tuple-element.67.refs_0_), channel_id=1, source_target_pairs={{0,64},{16,80},{32,96},{48,112},{64,0},{80,16},{96,32},{112,48},{1... | collective-permute-start | bytes 786440 | tf_op jit(solution)/shard_map/ppermute | solution.py:50
  78.1 7.1 %collective-permute-start.22 = (bf16[768,1024]{1,0:T(8,128)(2,1)S(1)}, bf16[768,1024]{1,0:T(8,128)(2,1)S(1)}, u32[]{:S(2)}, u32[]{:S(2)}) collective-permute-start(bf16[768,1024]{1,0:T(8,128)(2,1)S(1)} %get-tuple-element.74), channel_id=1, source_target_pairs={{0,1},{1,0},{2,3},{3,2},{4,5},{5,4},{6,7},{7,6},{8,9},{9,8},{10,11... | collective-permute-start | bytes 4718600 | tf_op jit(solution)/shard_map/ppermute | solution.py:41
  80.6 3.8 %collective-permute-start.20 = (bf16[256,1024]{1,0:T(8,128)(2,1)S(1)}, bf16[256,1024]{1,0:T(8,128)(2,1)S(1)}, u32[]{:S(2)}, u32[]{:S(2)}) collective-permute-start(bf16[256,1024]{1,0:T(8,128)(2,1)S(1)} %get-tuple-element.71.refs_1_), channel_id=1, source_target_pairs={{0,1},{1,0},{2,3},{3,2},{4,5},{5,4},{6,7},{7,6},{8,9},{9,8},{10,11... | collective-permute-start | bytes 1572872 | tf_op jit(solution)/shard_map/ppermute | solution.py:41
  80.6 4.5 %collective-permute-start.21 = (bf16[256,1024]{1,0:T(8,128)(2,1)S(1)}, bf16[256,1024]{1,0:T(8,128)(2,1)S(1)}, u32[]{:S(2)}, u32[]{:S(2)}) collective-permute-start(bf16[256,1024]{1,0:T(8,128)(2,1)S(1)} %get-tuple-element.72.refs_2_), channel_id=1, source_target_pairs={{0,1},{1,0},{2,3},{3,2},{4,5},{5,4},{6,7},{7,6},{8,9},{9,8},{10,11... | collective-permute-start | bytes 1572872 | tf_op jit(solution)/shard_map/ppermute | solution.py:41

commit v4 on v3

--- a/solution.py
+++ b/solution.py
@@ -228,7 +228,7 @@
     lax.fori_loop(0, weight_refs[0].shape[1] // tile, column, 0)
 
 
-def project(tokens, other_tokens, pieces, rows, totals=(), after=(), last=False):
+def project(tokens, other_tokens, pieces, rows, totals=(), after=(), last=False, counted=True):
     count = tokens.shape[1]
     columns = pieces[0][1].shape[1]
     operands = [tokens, other_tokens, *(w for _, w in pieces)]
@@ -250,15 +250,17 @@
         ],
         input_output_aliases=aliases,
         compiler_params=pltpu.CompilerParams(vmem_limit_bytes=6 * MIB),
-        cost_estimate=cost(4 * count * depth * columns, 2 * columns * depth),
+        cost_estimate=cost(4 * count * depth * columns, 2 * columns * depth)
+        if counted
+        else cost(1, 1),
         name="project",
     )(*operands, *after)
 
 
-def finish_kernel(places, rows, *refs):
+def finish_kernel(places, rows, given, last, *refs):
     count = len(places)
     tokens_ref, weight_refs = refs[0], refs[1 : 1 + count]
-    own_ref, other_ref, scale_ref = refs[1 + count : 4 + count]
+    total_refs = refs[1 + count : 1 + count + given]
     out_ref = refs[-1]
     me = lax.axis_index("fsdp")
     z, x, c = me // 4, (me // 2) % 2, me % 2
@@ -271,32 +273,45 @@
 
     def column(n, carry):
         at = pl.ds(pl.multiple_of(n * tile, tile), tile)
-        total = own_ref[:, at] + other_ref[:, at].astype(jnp.float32)
+        total = total_refs[0][:, at]
+        for total_ref in total_refs[1:]:
+            total = total + total_ref[:, at].astype(jnp.float32)
         for start, weight_ref in zip(starts, weight_refs):
             total = total + jnp.dot(
                 tokens_ref[0, :, pl.ds(start, weight_ref.shape[0])],
                 weight_ref[:, at],
                 preferred_element_type=jnp.float32,
             )
-        out_ref[0, :, at] = (total * scale_ref[:, :1]).astype(jnp.bfloat16)
+        if last:
+            scale_ref = refs[1 + count + given]
+            out_ref[0, :, at] = (total * scale_ref[:, :1]).astype(jnp.bfloat16)
+        else:
+            out_ref[:, at] = total
         return carry
 
     lax.fori_loop(0, weight_refs[0].shape[1] // tile, column, 0)
 
 
-def finish(tokens, pieces, rows, own, other, row_scale, after):
+def finish(tokens, pieces, rows, totals, row_scale=None, after=()):
     count = tokens.shape[1]
-    columns = own.shape[1]
-    operands = [tokens, *(w for _, w in pieces), own, other, row_scale]
+    columns = totals[0].shape[1]
+    last = row_scale is not None
+    operands = [tokens, *(w for _, w in pieces), *totals]
+    if last:
+        operands.append(row_scale)
+        out_shape = jax.ShapeDtypeStruct((1, count, columns), jnp.bfloat16)
+    else:
+        out_shape = jax.ShapeDtypeStruct((count, columns), jnp.float32)
     depth = sum(w.shape[0] for _, w in pieces)
     spec = pl.BlockSpec(memory_space=pltpu.VMEM)
     places = tuple(p for p, _ in pieces)
     return pl.pallas_call(
-        functools.partial(finish_kernel, places, rows),
+        functools.partial(finish_kernel, places, rows, len(totals), last),
         in_specs=[spec] * len(operands)
         + [pl.BlockSpec(memory_space=pl.ANY)] * len(after),
         out_specs=spec,
-        out_shape=jax.ShapeDtypeStruct((1, count, columns), jnp.bfloat16),
+        out_shape=out_shape,
+        input_output_aliases={} if last else {1 + len(pieces): 0},
         compiler_params=pltpu.CompilerParams(vmem_limit_bytes=6 * MIB),
         cost_estimate=cost(2 * count * depth * columns, 2 * columns * depth),
         name="finish",
@@ -393,8 +408,10 @@
 
     own, own_low, own_high, *slices = prepare(gain, next_weights, weights)
 
-    def project_on(totals, pieces, after=(), last=False):
-        return project(tokens, other_tokens, pieces, rows, totals, after, last)
+    def project_on(totals, pieces, after=(), last=False, counted=True):
+        return project(
+            tokens, other_tokens, pieces, rows, totals, after, last, counted
+        )
 
     other_tokens = to_core(tokens)
     ring_1 = along_z(own)
@@ -437,9 +454,9 @@
         [snapshot, momentum, own_sum, other_sum],
     )
     new_other = across_replicas(new, lambda y, x: (y, 1 - x))
-    (high_2,) = phase([ring_2[half:]], after=[new_other])
-    high_2 = along_x(high_2)
-    pair = join(new, new_other)
+    (high_2_sent,) = phase([ring_2[half:]], after=[new_other])
+    high_2 = along_x(high_2_sent)
+    pair = join(new, new_other, after=[high_2_sent])
     pair_1 = across_replicas(pair, lambda y, x: (y - 1, x))
     pair_3 = across_replicas(pair, lambda y, x: (y + 1, x))
     totals = project_on(
@@ -450,13 +467,15 @@
             ((0, 1, 0, half), high_0),
         ],
         after=[pair],
-    )
-    ring_3, high_0, pair = phase(
-        [ring_3, high_0, pair], after=[totals[0], pair_1, pair_3]
-    )
+        counted=False,
+    )
+    ring_3, high_0 = phase([ring_3, high_0], after=[totals[0]])
 
     high_1 = along_z(high_0)
     high_3 = along_x(ring_3[half:])
+    low_2, pair = phase([low_2, pair], after=[pair_1, pair_3, ring_3])
+
+    low_3 = along_z(low_2)
     pair_2 = across_replicas(pair, lambda y, x: (y + 2, x))
     totals = project_on(
         totals,
@@ -464,10 +483,8 @@
             ((3, 0, 0, 0), ring_3),
             ((1, 1, 0, 0), low_1),
         ],
-    )
-    (low_2,) = phase([low_2], after=[totals[0]])
-
-    low_3 = along_z(low_2)
+        after=[low_2],
+    )
     own_total, other_total = project_on(
         totals,
         [
@@ -481,23 +498,21 @@
 
     low_3_other, high_3_other = to_core(low_3), to_core(high_3)
     other_total = to_core(other_total)
+    own_total = finish(
+        tokens, [((3, 1, 0, 0), low_3), ((3, 1, 0, half), high_3)], rows, [own_total]
+    )
     new_weights, done = whole(
         assemble_kernel,
         [shape((rows, columns), jnp.bfloat16), shape((8, BLOCK), jnp.float32)],
         "assemble",
         [pair, pair_1, pair_2, pair_3],
+        after=[own_total],
     )
     next_keys = finish(
         tokens,
-        [
-            ((3, 1, 0, 0), low_3),
-            ((3, 1, 0, half), high_3),
-            ((3, 1, 1, 0), low_3_other),
-            ((3, 1, 1, half), high_3_other),
-        ],
+        [((3, 1, 1, 0), low_3_other), ((3, 1, 1, half), high_3_other)],
         rows,
-        own_total,
-        other_total,
+        [own_total, other_total],
         row_scale,
         after=[done],
     )

time: 88.9 us -> 86.1 us (0.969)
  waiting for transfers between devices: 21.4 us -> 15.8 us
  starting transfers between devices: 37.3 us -> 39.2 us
  Pallas kernels: 29.2 us -> 30.1 us
    ppermute x8, waiting for transfers between devices: 8.28 us -> 5.65 us  [across_replicas(): return lax.ppermute(value, 'replica', pairs)]
    ppermute x7, starting transfers between devices: 8.68 us -> 10.7 us  [along_z(): lax.ppermute(value, 'fsdp', fsdp_perm(lambda z, x, c: (z + 1 - 2 * c, x,...]
    ppermute x7, waiting for transfers between devices: 5.59 us -> 3.66 us  [along_z(): lax.ppermute(value, 'fsdp', fsdp_perm(lambda z, x, c: (z + 1 - 2 * c, x,...]
    ppermute x4, waiting for transfers between devices: 2.73 us -> 0.94 us  [to_core(): return lax.ppermute(value, 'fsdp', fsdp_perm(lambda z, x, c: (z, x, 1 - c)))]
    ppermute x4, starting transfers between devices: 12 us -> 10.6 us  [along_x(): return lax.ppermute(value, 'fsdp', fsdp_perm(lambda z, x, c: (z, 1 - x, c)))]
    ppermute x8, starting transfers between devices: 12 us -> 13.1 us  [across_replicas(): return lax.ppermute(value, 'replica', pairs)]
    pallas_call x1 -> x2, Pallas kernels: 3.58 us -> 4.5 us  [finish(): pl.pallas_call(functools.partial(finish_kernel, places, rows, len(totals)...]
  transfers between devices with their start and end apart: 23 -> 23, of which waited for: 10 -> 10; matrix products, arithmetic and copies ran while one was open for 0% -> 0% of each run, Pallas kernels for 29% -> 32%
where the time goes in v4:
time: 86.1 us; the launch traced here: 85.9 us
  starting transfers between devices  39.2 us (46%)
  Pallas kernels  30.1 us (35%)
  waiting for transfers between devices  15.8 us (18%)
    pallas_call x4, Pallas kernels, project(): pl.pallas_call(functools.partial(project_kernel, places, rows, bool(total...  15.8 us
    ppermute x8, starting transfers between devices, across_replicas(): return lax.ppermute(value, 'replica', pairs)  13.1 us
    ppermute x7, starting transfers between devices, along_z(): lax.ppermute(value, 'fsdp', fsdp_perm(lambda z, x, c: (z + 1 - 2 * c, x,...  10.7 us
    ppermute x4, starting transfers between devices, along_x(): return lax.ppermute(value, 'fsdp', fsdp_perm(lambda z, x, c: (z, 1 - x, c)))  10.6 us
    ppermute x8, waiting for transfers between devices, across_replicas(): return lax.ppermute(value, 'replica', pairs)  5.65 us
    ppermute x4, waiting for transfers between devices, along_x(): return lax.ppermute(value, 'fsdp', fsdp_perm(lambda z, x, c: (z, 1 - x, c)))  5.51 us
    pallas_call x1, Pallas kernels, fetch(): pl.pallas_call(run, in_specs=[pl.BlockSpec(memory_space=pltpu.HBM)] + [pl...  4.92 us
    ppermute x4, starting transfers between devices, to_core(): return lax.ppermute(value, 'fsdp', fsdp_perm(lambda z, x, c: (z, x, 1 - c)))  4.9 us
  transfers between devices with their start and end apart: 23, of which 10 were waited for; matrix products, arithmetic and copies ran while one was open for 0% of the time, Pallas kernels for 32%

profile of v4, /device:TPU:1, one launch (start us, length us, event | category | flops | bytes accessed | tf_op | source)
XLA Modules:
  0.0 85.9 jit_solution(14017807724954889655)
XLA Ops:
  0.6 1.5 %collective-permute-start.8 = (bf16[1,768,8192]{2,1,0:T(8,128)(2,1)}, bf16[1,768,8192]{2,1,0:T(8,128)(2,1)S(1)}, u32[]{:S(2)}, u32[]{:S(2)}) collective-permute-start(bf16[1,768,8192]{2,1,0:T(8,128)(2,1)} %tokens_hbm.1), channel_id=1, source_target_pairs={{0,1},{1,0},{2,3},{3,2},{4,5},{5,4},{6,7},{7,6},{8,9},{9,8},{10,11... | collective-permute-start | bytes 37748744 | tf_op jit(solution)/shard_map/ppermute | solution.py:41
  2.1 1.6 %prepare.1 = (bf16[512,1024]{1,0:T(8,128)(2,1)S(1)}, bf16[256,1024]{1,0:T(8,128)(2,1)S(1)}, bf16[256,1024]{1,0:T(8,128)(2,1)S(1)}, bf16[512,256]{1,0:T(8,128)(2,...) custom-call(f32[1,8192]{1,0:T(1,128)} %gain_hbm.1, ...), custom_call_target="tpu_custom_call" | custom-call | flops 524288 | bytes 2097152 | tf_op jit(solution)/shard_map/prepare/pallas_call | solution.py:111
  3.8 3.9 %collective-permute-start = (bf16[512,1024]{1,0:T(8,128)(2,1)S(1)}, bf16[512,1024]{1,0:T(8,128)(2,1)S(1)}, u32[]{:S(2)}, u32[]{:S(2)}) collective-permute-start(bf16[512,1024]{1,0:T(8,128)(2,1)S(1)} %get-tuple-element.42.refs_0_.refs_2_), channel_id=1, source_target_pairs={{0,4},{1,13},{2,6},{3,15},{4,8},{5,1},{6,10},{7,3},{8,12},{9,5},{1... | collective-permute-start | bytes 3145736 | tf_op jit(solution)/shard_map/ppermute | solution.py:31
  7.7 2.7 %collective-permute-start.1 = (bf16[256,1024]{1,0:T(8,128)(2,1)S(1)}, bf16[256,1024]{1,0:T(8,128)(2,1)S(1)}, u32[]{:S(2)}, u32[]{:S(2)}) collective-permute-start(bf16[256,1024]{1,0:T(8,128)(2,1)S(1)} %get-tuple-element.44), channel_id=1, source_target_pairs={{0,2},{1,3},{2,0},{3,1},{4,6},{5,7},{6,4},{7,5},{8,10},{9,11},{10,... | collective-permute-start | bytes 1572872 | tf_op jit(solution)/shard_map/ppermute | solution.py:37
  10.4 1.3 %collective-permute-start.2 = (bf16[512,256]{1,0:T(8,128)(2,1)S(1)}, bf16[512,256]{1,0:T(8,128)(2,1)S(1)}, u32[]{:S(2)}, u32[]{:S(2)}) collective-permute-start(bf16[512,256]{1,0:T(8,128)(2,1)S(1)} %get-tuple-element.48), channel_id=1, source_target_pairs={{0,32},{16,48},{32,64},{48,80},{64,96},{80,112},{96,0},{112,16},{1... | collective-permute-start | bytes 786440 | tf_op jit(solution)/shard_map/ppermute | solution.py:50
  11.7 1.4 %collective-permute-start.3 = (bf16[512,256]{1,0:T(8,128)(2,1)S(1)}, bf16[512,256]{1,0:T(8,128)(2,1)S(1)}, u32[]{:S(2)}, u32[]{:S(2)}) collective-permute-start(bf16[512,256]{1,0:T(8,128)(2,1)S(1)} %get-tuple-element.49), channel_id=1, source_target_pairs={{0,96},{16,112},{32,0},{48,16},{64,32},{80,48},{96,64},{112,80},{1... | collective-permute-start | bytes 786440 | tf_op jit(solution)/shard_map/ppermute | solution.py:50
  13.1 4.9 %load.1 = (bf16[1,768,8192]{2,1,0:T(8,128)(2,1)S(1)}, f32[768,128]{1,0:T(8,128)S(1)}) custom-call(bf16[1,768,8192]{2,1,0:T(8,128)(2,1)} %tokens_hbm.1, bf16[512,1024]{1,0:T(8,128)(2,1)S(1)} %get-tuple-element.42.refs_0_.refs_2_), custom_call_target="tpu_custom_call" | custom-call | flops 6291456 | bytes 12582912 | tf_op jit(solution)/shard_map/load/pallas_call | solution.py:179
  18.1 0.8 collective-permute-done.2.refs_5_.refs_2_
  18.9 0.4 collective-permute-done.3.refs_6_.refs_4_
  19.2 2.2 %collective-permute-done.1.refs_1_ = bf16[256,1024]{1,0:T(8,128)(2,1)S(1)} collective-permute-done((bf16[256,1024]{1,0:T(8,128)(2,1)S(1)}, bf16[256,1024]{1,0:T(8,128)(2,1)S(1)}, u32[]{:S(2)}, u32[]{:S(2)}) %collective-permute-start.1) | collective-permute-done | bytes 524320 | tf_op jit(solution)/shard_map/ppermute | solution.py:37
  21.5 1.4 %collective-permute-start.4 = (bf16[512,1024]{1,0:T(8,128)(2,1)S(1)}, bf16[512,1024]{1,0:T(8,128)(2,1)S(1)}, u32[]{:S(2)}, u32[]{:S(2)}) collective-permute-start(bf16[512,1024]{1,0:T(8,128)(2,1)S(1)} %get-tuple-element.50.refs_3_), channel_id=1, source_target_pairs={{0,4},{1,13},{2,6},{3,15},{4,8},{5,1},{6,10},{7,3},{8,12},{9,5},{1... | collective-permute-start | bytes 3145736 | tf_op jit(solution)/shard_map/ppermute | solution.py:31
  22.9 2.7 %collective-permute-start.5 = (bf16[256,1024]{1,0:T(8,128)(2,1)S(1)}, bf16[256,1024]{1,0:T(8,128)(2,1)S(1)}, u32[]{:S(2)}, u32[]{:S(2)}) collective-permute-start(bf16[256,1024]{1,0:T(8,128)(2,1)S(1)} %get-tuple-element.51), channel_id=1, source_target_pairs={{0,2},{1,3},{2,0},{3,1},{4,6},{5,7},{6,4},{7,5},{8,10},{9,11},{10,... | collective-permute-start | bytes 1572872 | tf_op jit(solution)/shard_map/ppermute | solution.py:37
  25.6 0.1 collective-permute-start.6
  25.7 2.9 %collective-permute-start.7 = (bf16[512,256]{1,0:T(8,128)(2,1)S(1)}, bf16[512,256]{1,0:T(8,128)(2,1)S(1)}, u32[]{:S(2)}, u32[]{:S(2)}) collective-permute-start(bf16[512,256]{1,0:T(8,128)(2,1)S(1)} %get-tuple-element.54), channel_id=1, source_target_pairs={{0,64},{16,80},{32,96},{48,112},{64,0},{80,16},{96,32},{112,48},{1... | collective-permute-start | bytes 786440 | tf_op jit(solution)/shard_map/ppermute | solution.py:50
  28.6 0.0 collective-permute-done.8.refs_1_
  28.6 4.0 %project.4 = (f32[768,1024]{1,0:T(8,128)S(1)}, f32[768,1024]{1,0:T(8,128)S(1)}) custom-call(bf16[1,768,8192]{2,1,0:T(8,128)(2,1)S(1)} %get-tuple-element.43.refs_0_, bf16[1,768,8192]{2,1,0:T(8,128)(2,1)S(1)} %collective-permute-done.8.refs_1_, bf16[512,1024]{1,0:T(8,128)(2,1)S(1)} %get-tuple-element.42.refs_0_.refs_2_, ...), custom_call_target="tpu_custom_call" | custom-call | flops 3221225472 | bytes 2097152 | tf_op jit(solution)/shard_map/project/pallas_call | solution.py:240
  32.6 1.4 %collective-permute-done.7.refs_3_ = bf16[512,256]{1,0:T(8,128)(2,1)S(1)} collective-permute-done((bf16[512,256]{1,0:T(8,128)(2,1)S(1)}, bf16[512,256]{1,0:T(8,128)(2,1)S(1)}, u32[]{:S(2)}, u32[]{:S(2)}) %collective-permute-start.7) | collective-permute-done | bytes 262176 | tf_op jit(solution)/shard_map/ppermute | solution.py:50
  34.0 1.1 %partial.1 = (f32[512,128]{1,0:T(8,128)S(1)}, bf16[512,128]{1,0:T(8,128)(2,1)S(1)}) custom-call(f32[512,1024]{1,0:T(8,128)S(1)} %copy-done, bf16[512,256]{1,0:T(8,128)(2,1)S(1)} %get-tuple-element.53.refs_1_, bf16[512,256]{1,0:T(8,128)(2,1)S(1)} %collective-permute-done.2.refs_5_.refs_2_, bf16[512,256]{1,0:T(8,128)(2,1)S(1)} %collective-permute-done.7.refs_3_, ...), custom_call_target="tpu_custom_call" | custom-call | flops 25165824 | bytes 6291456 | tf_op jit(solution)/shard_map/partial/pallas_call | solution.py:393
  35.1 0.4 collective-permute-start.9
  35.5 1.9 %collective-permute-done.5.refs_1_ = bf16[256,1024]{1,0:T(8,128)(2,1)S(1)} collective-permute-done((bf16[256,1024]{1,0:T(8,128)(2,1)S(1)}, bf16[256,1024]{1,0:T(8,128)(2,1)S(1)}, u32[]{:S(2)}, u32[]{:S(2)}) %collective-permute-start.5) | collective-permute-done | bytes 524320 | tf_op jit(solution)/shard_map/ppermute | solution.py:37
  37.4 3.6 %collective-permute-done.6.refs_2_ = bf16[256,1024]{1,0:T(8,128)(2,1)S(1)} collective-permute-done((bf16[256,1024]{1,0:T(8,128)(2,1)S(1)}, bf16[256,1024]{1,0:T(8,128)(2,1)S(1)}, u32[]{:S(2)}, u32[]{:S(2)}) %collective-permute-start.6) | collective-permute-done | bytes 524320 | tf_op jit(solution)/shard_map/ppermute | solution.py:31
  41.0 0.0 collective-permute-done.4.refs_0_
  41.0 0.0 collective-permute-done.9.refs_3_
  41.0 2.4 %collective-permute-start.14 = (bf16[512,1024]{1,0:T(8,128)(2,1)S(1)}, bf16[512,1024]{1,0:T(8,128)(2,1)S(1)}, u32[]{:S(2)}, u32[]{:S(2)}) collective-permute-start(bf16[512,1024]{1,0:T(8,128)(2,1)S(1)} %get-tuple-element.61.refs_2_), channel_id=1, source_target_pairs={{0,4},{1,13},{2,6},{3,15},{4,8},{5,1},{6,10},{7,3},{8,12},{9,5},{1... | collective-permute-start | bytes 3145736 | tf_op jit(solution)/shard_map/ppermute | solution.py:31
  43.4 0.1 collective-permute-start.10
  43.5 0.8 update.1
  44.3 1.2 %collective-permute-start.11 = (bf16[512,128]{1,0:T(8,128)(2,1)S(1)}, bf16[512,128]{1,0:T(8,128)(2,1)S(1)}, u32[]{:S(2)}, u32[]{:S(2)}) collective-permute-start(bf16[512,128]{1,0:T(8,128)(2,1)S(1)} %get-tuple-element.60.refs_0_), channel_id=1, source_target_pairs={{0,16},{16,0},{32,48},{48,32},{64,80},{80,64},{96,112},{112,96},{1... | collective-permute-start | bytes 393224 | tf_op jit(solution)/shard_map/ppermute | solution.py:50
  45.5 3.1 %collective-permute-done.11.refs_1_ = bf16[512,128]{1,0:T(8,128)(2,1)S(1)} collective-permute-done((bf16[512,128]{1,0:T(8,128)(2,1)S(1)}, bf16[512,128]{1,0:T(8,128)(2,1)S(1)}, u32[]{:S(2)}, u32[]{:S(2)}) %collective-permute-start.11) | collective-permute-done | bytes 131104 | tf_op jit(solution)/shard_map/ppermute | solution.py:50
  48.7 1.4 %collective-permute-start.13 = (bf16[512,256]{1,0:T(8,128)(2,1)S(1)}, bf16[512,256]{1,0:T(8,128)(2,1)S(1)}, u32[]{:S(2)}, u32[]{:S(2)}) collective-permute-start(bf16[512,256]{1,0:T(8,128)(2,1)S(1)} %join.1.refs_7_.refs_1_), channel_id=1, source_target_pairs={{0,32},{16,48},{32,64},{48,80},{64,96},{80,112},{96,0},{112,16},{1... | collective-permute-start | bytes 786440 | tf_op jit(solution)/shard_map/ppermute | solution.py:50
  50.0 1.5 %collective-permute-start.12 = (bf16[512,256]{1,0:T(8,128)(2,1)S(1)}, bf16[512,256]{1,0:T(8,128)(2,1)S(1)}, u32[]{:S(2)}, u32[]{:S(2)}) collective-permute-start(bf16[512,256]{1,0:T(8,128)(2,1)S(1)} %join.1.refs_7_.refs_1_), channel_id=1, source_target_pairs={{0,96},{16,112},{32,0},{48,16},{64,32},{80,48},{96,64},{112,80},{1... | collective-permute-start | bytes 786440 | tf_op jit(solution)/shard_map/ppermute | solution.py:50
  51.6 2.7 %collective-permute-start.18 = (bf16[256,1024]{1,0:T(8,128)(2,1)S(1)}, bf16[256,1024]{1,0:T(8,128)(2,1)S(1)}, u32[]{:S(2)}, u32[]{:S(2)}) collective-permute-start(bf16[256,1024]{1,0:T(8,128)(2,1)S(1)} %phase.8.refs_2_), channel_id=1, source_target_pairs={{0,2},{1,3},{2,0},{3,1},{4,6},{5,7},{6,4},{7,5},{8,10},{9,11},{10,... | collective-permute-start | bytes 1572872 | tf_op jit(solution)/shard_map/ppermute | solution.py:37
  54.3 4.6 %project.5 = (f32[768,1024]{1,0:T(8,128)S(1)}, f32[768,1024]{1,0:T(8,128)S(1)}) custom-call(bf16[1,768,8192]{2,1,0:T(8,128)(2,1)S(1)} %get-tuple-element.43.refs_0_, bf16[1,768,8192]{2,1,0:T(8,128)(2,1)S(1)} %collective-permute-done.8.refs_1_, bf16[512,1024]{1,0:T(8,128)(2,1)S(1)} %get-tuple-element.61.refs_2_, ...), custom_call_target="tpu_custom_call", output_to_operand_aliasing={{0}: (5, {}), {1}: (6, {})} | custom-call | flops 1 | bytes 1 | tf_op jit(solution)/shard_map/project/pallas_call | solution.py:240
  58.9 0.0 collective-permute-done.14.refs_0_
  58.9 0.1 collective-permute-start.19
  59.1 2.3 %collective-permute-start.16 = (bf16[256,1024]{1,0:T(8,128)(2,1)S(1)}, bf16[256,1024]{1,0:T(8,128)(2,1)S(1)}, u32[]{:S(2)}, u32[]{:S(2)}) collective-permute-start(bf16[256,1024]{1,0:T(8,128)(2,1)S(1)} %slice.7), channel_id=1, source_target_pairs={{0,2},{1,3},{2,0},{3,1},{4,6},{5,7},{6,4},{7,5},{8,10},{9,11},{10,... | collective-permute-start | bytes 1572872 | tf_op jit(solution)/shard_map/ppermute | solution.py:37
  61.4 2.8 %collective-permute-start.15 = (bf16[256,1024]{1,0:T(8,128)(2,1)S(1)}, bf16[256,1024]{1,0:T(8,128)(2,1)S(1)}, u32[]{:S(2)}, u32[]{:S(2)}) collective-permute-start(bf16[256,1024]{1,0:T(8,128)(2,1)S(1)} %get-tuple-element.66.refs_6_.refs_3_), channel_id=1, source_target_pairs={{0,4},{1,13},{2,6},{3,15},{4,8},{5,1},{6,10},{7,3},{8,12},{9,5},{1... | collective-permute-start | bytes 1572872 | tf_op jit(solution)/shard_map/ppermute | solution.py:31
  64.2 2.9 %collective-permute-start.17 = (bf16[512,256]{1,0:T(8,128)(2,1)S(1)}, bf16[512,256]{1,0:T(8,128)(2,1)S(1)}, u32[]{:S(2)}, u32[]{:S(2)}) collective-permute-start(bf16[512,256]{1,0:T(8,128)(2,1)S(1)} %get-tuple-element.67.refs_0_), channel_id=1, source_target_pairs={{0,64},{16,80},{32,96},{48,112},{64,0},{80,16},{96,32},{112,48},{1... | collective-permute-start | bytes 786440 | tf_op jit(solution)/shard_map/ppermute | solution.py:50
  67.1 3.8 %project.6 = (f32[768,1024]{1,0:T(8,128)S(1)}, f32[768,1024]{1,0:T(8,128)S(1)}) custom-call(bf16[1,768,8192]{2,1,0:T(8,128)(2,1)S(1)} %get-tuple-element.43.refs_0_, bf16[1,768,8192]{2,1,0:T(8,128)(2,1)S(1)} %collective-permute-done.8.refs_1_, bf16[512,1024]{1,0:T(8,128)(2,1)S(1)} %get-tuple-element.65.refs_4_.refs_2_, ...), custom_call_target="tpu_custom_call", output_to_operand_aliasing={{0}: (4, {}), {1}: (5, {})} | custom-call | flops 2415919104 | bytes 1572864 | tf_op jit(solution)/shard_map/project/pallas_call | solution.py:240
  70.9 3.5 %project.7 = (f32[768,1024]{1,0:T(8,128)S(1)}, bf16[768,1024]{1,0:T(8,128)(2,1)S(1)}) custom-call(bf16[1,768,8192]{2,1,0:T(8,128)(2,1)S(1)} %get-tuple-element.43.refs_0_, bf16[1,768,8192]{2,1,0:T(8,128)(2,1)S(1)} %collective-permute-done.8.refs_1_, bf16[256,1024]{1,0:T(8,128)(2,1)S(1)} %collective-permute-done.18.refs_2_, ...), custom_call_target="tpu_custom_call", output_to_operand_aliasing={{0}: (5, {})} | custom-call | flops 2415919104 | bytes 1572864 | tf_op jit(solution)/shard_map/project/pallas_call | solution.py:240
  74.4 1.4 %collective-permute-done.16.refs_1_ = bf16[256,1024]{1,0:T(8,128)(2,1)S(1)} collective-permute-done((bf16[256,1024]{1,0:T(8,128)(2,1)S(1)}, bf16[256,1024]{1,0:T(8,128)(2,1)S(1)}, u32[]{:S(2)}, u32[]{:S(2)}) %collective-permute-start.16) | collective-permute-done | bytes 524320 | tf_op jit(solution)/shard_map/ppermute | solution.py:37
  75.8 2.9 %collective-permute-start.22 = (bf16[768,1024]{1,0:T(8,128)(2,1)S(1)}, bf16[768,1024]{1,0:T(8,128)(2,1)S(1)}, u32[]{:S(2)}, u32[]{:S(2)}) collective-permute-start(bf16[768,1024]{1,0:T(8,128)(2,1)S(1)} %get-tuple-element.76), channel_id=1, source_target_pairs={{0,1},{1,0},{2,3},{3,2},{4,5},{5,4},{6,7},{7,6},{8,9},{9,8},{10,11... | collective-permute-start | bytes 4718600 | tf_op jit(solution)/shard_map/ppermute | solution.py:41
  78.7 0.1 collective-permute-start.20
  78.7 0.4 collective-permute-start.21
  79.2 1.8 %finish.2.refs_4_.refs_3_ = f32[768,1024]{1,0:T(8,128)S(1)} custom-call(bf16[1,768,8192]{2,1,0:T(8,128)(2,1)S(1)} %get-tuple-element.43.refs_0_, bf16[256,1024]{1,0:T(8,128)(2,1)S(1)} %get-tuple-element.73.refs_1_, bf16[256,1024]{1,0:T(8,128)(2,1)S(1)} %get-tuple-element.74.refs_2_, ...), custom_call_target="tpu_custom_call", output_to_operand_aliasing={{}: (3, {})} | custom-call | flops 805306368 | bytes 1048576 | tf_op jit(solution)/shard_map/finish/pallas_call | solution.py:308
  80.9 1.3 %assemble.1 = (bf16[512,1024]{1,0:T(8,128)(2,1)}, f32[8,128]{1,0:T(8,128)S(1)}) custom-call(bf16[512,256]{1,0:T(8,128)(2,1)S(1)} %get-tuple-element.67.refs_0_, bf16[512,256]{1,0:T(8,128)(2,1)S(1)} %collective-permute-done.12.refs_2_.refs_1_, bf16[512,256]{1,0:T(8,128)(2,1)S(1)} %get-tuple-element.77.refs_2_, ...), custom_call_target="tpu_custom_call" | custom-call | flops 8388608 | bytes 2097152 | tf_op jit(solution)/shard_map/assemble/pallas_call | solution.py:393
  82.3 0.2 collective-permute-done.20.refs_1_
  82.4 0.7 collective-permute-done.21.refs_2_
  83.2 2.7 %finish.3 = bf16[1,768,1024]{2,1,0:T(8,128)(2,1)} custom-call(bf16[1,768,8192]{2,1,0:T(8,128)(2,1)S(1)} %get-tuple-element.43.refs_0_, bf16[256,1024]{1,0:T(8,128)(2,1)S(1)} %collective-permute-done.20.refs_1_, bf16[256,1024]{1,0:T(8,128)(2,1)S(1)} %collective-permute-done.21.refs_2_, f32[768,1024]{1,0:T(8,128)S(1)} %finish.2.refs_4_.refs_3_, ...), custom_call_target="tpu_custom_call" | custom-call | flops 805306368 | bytes 1048576 | tf_op jit(solution)/shard_map/finish/pallas_call | solution.py:308
  (22 shorter events, 0.2 us)
Async XLA Ops:
  0.6 28.0 %collective-permute-start.8 = (bf16[1,768,8192]{2,1,0:T(8,128)(2,1)}, bf16[1,768,8192]{2,1,0:T(8,128)(2,1)S(1)}, u32[]{:S(2)}, u32[]{:S(2)}) collective-permute-start(bf16[1,768,8192]{2,1,0:T(8,128)(2,1)} %tokens_hbm.1), channel_id=1, source_target_pairs={{0,1},{1,0},{2,3},{3,2},{4,5},{5,4},{6,7},{7,6},{8,9},{9,8},{10,11... | collective-permute-start | bytes 37748744 | tf_op jit(solution)/shard_map/ppermute | solution.py:41
  3.8 17.7 %collective-permute-start = (bf16[512,1024]{1,0:T(8,128)(2,1)S(1)}, bf16[512,1024]{1,0:T(8,128)(2,1)S(1)}, u32[]{:S(2)}, u32[]{:S(2)}) collective-permute-start(bf16[512,1024]{1,0:T(8,128)(2,1)S(1)} %get-tuple-element.42.refs_0_.refs_2_), channel_id=1, source_target_pairs={{0,4},{1,13},{2,6},{3,15},{4,8},{5,1},{6,10},{7,3},{8,12},{9,5},{1... | collective-permute-start | bytes 3145736 | tf_op jit(solution)/shard_map/ppermute | solution.py:31
  7.7 13.8 %collective-permute-start.1 = (bf16[256,1024]{1,0:T(8,128)(2,1)S(1)}, bf16[256,1024]{1,0:T(8,128)(2,1)S(1)}, u32[]{:S(2)}, u32[]{:S(2)}) collective-permute-start(bf16[256,1024]{1,0:T(8,128)(2,1)S(1)} %get-tuple-element.44), channel_id=1, source_target_pairs={{0,2},{1,3},{2,0},{3,1},{4,6},{5,7},{6,4},{7,5},{8,10},{9,11},{10,... | collective-permute-start | bytes 1572872 | tf_op jit(solution)/shard_map/ppermute | solution.py:37
  10.4 8.5 %collective-permute-start.2 = (bf16[512,256]{1,0:T(8,128)(2,1)S(1)}, bf16[512,256]{1,0:T(8,128)(2,1)S(1)}, u32[]{:S(2)}, u32[]{:S(2)}) collective-permute-start(bf16[512,256]{1,0:T(8,128)(2,1)S(1)} %get-tuple-element.48), channel_id=1, source_target_pairs={{0,32},{16,48},{32,64},{48,80},{64,96},{80,112},{96,0},{112,16},{1... | collective-permute-start | bytes 786440 | tf_op jit(solution)/shard_map/ppermute | solution.py:50
  11.7 7.5 %collective-permute-start.3 = (bf16[512,256]{1,0:T(8,128)(2,1)S(1)}, bf16[512,256]{1,0:T(8,128)(2,1)S(1)}, u32[]{:S(2)}, u32[]{:S(2)}) collective-permute-start(bf16[512,256]{1,0:T(8,128)(2,1)S(1)} %get-tuple-element.49), channel_id=1, source_target_pairs={{0,96},{16,112},{32,0},{48,16},{64,32},{80,48},{96,64},{112,80},{1... | collective-permute-start | bytes 786440 | tf_op jit(solution)/shard_map/ppermute | solution.py:50
  21.5 19.6 %collective-permute-start.4 = (bf16[512,1024]{1,0:T(8,128)(2,1)S(1)}, bf16[512,1024]{1,0:T(8,128)(2,1)S(1)}, u32[]{:S(2)}, u32[]{:S(2)}) collective-permute-start(bf16[512,1024]{1,0:T(8,128)(2,1)S(1)} %get-tuple-element.50.refs_3_), channel_id=1, source_target_pairs={{0,4},{1,13},{2,6},{3,15},{4,8},{5,1},{6,10},{7,3},{8,12},{9,5},{1... | collective-permute-start | bytes 3145736 | tf_op jit(solution)/shard_map/ppermute | solution.py:31
  22.9 14.5 %collective-permute-start.5 = (bf16[256,1024]{1,0:T(8,128)(2,1)S(1)}, bf16[256,1024]{1,0:T(8,128)(2,1)S(1)}, u32[]{:S(2)}, u32[]{:S(2)}) collective-permute-start(bf16[256,1024]{1,0:T(8,128)(2,1)S(1)} %get-tuple-element.51), channel_id=1, source_target_pairs={{0,2},{1,3},{2,0},{3,1},{4,6},{5,7},{6,4},{7,5},{8,10},{9,11},{10,... | collective-permute-start | bytes 1572872 | tf_op jit(solution)/shard_map/ppermute | solution.py:37
  25.6 15.4 %collective-permute-start.6 = (bf16[256,1024]{1,0:T(8,128)(2,1)S(1)}, bf16[256,1024]{1,0:T(8,128)(2,1)S(1)}, u32[]{:S(2)}, u32[]{:S(2)}) collective-permute-start(bf16[256,1024]{1,0:T(8,128)(2,1)S(1)} %get-tuple-element.52.refs_3_), channel_id=1, source_target_pairs={{0,4},{1,13},{2,6},{3,15},{4,8},{5,1},{6,10},{7,3},{8,12},{9,5},{1... | collective-permute-start | bytes 1572872 | tf_op jit(solution)/shard_map/ppermute | solution.py:31
  25.7 8.3 %collective-permute-start.7 = (bf16[512,256]{1,0:T(8,128)(2,1)S(1)}, bf16[512,256]{1,0:T(8,128)(2,1)S(1)}, u32[]{:S(2)}, u32[]{:S(2)}) collective-permute-start(bf16[512,256]{1,0:T(8,128)(2,1)S(1)} %get-tuple-element.54), channel_id=1, source_target_pairs={{0,64},{16,80},{32,96},{48,112},{64,0},{80,16},{96,32},{112,48},{1... | collective-permute-start | bytes 786440 | tf_op jit(solution)/shard_map/ppermute | solution.py:50
  28.6 5.4 %copy-start = (f32[512,1024]{1,0:T(8,128)S(1)}, f32[512,1024]{1,0:T(8,128)}, u32[]{:S(2)}) copy-start(f32[512,1024]{1,0:T(8,128)} %refs_0_.3) | copy-start | bytes 6291460
  34.0 9.5 %copy-start.1 = (bf16[512,128]{1,0:T(8,128)(2,1)S(1)}, bf16[512,128]{1,0:T(8,128)(2,1)}, u32[]{:S(2)}) copy-start(bf16[512,128]{1,0:T(8,128)(2,1)} %refs_1_.1) | copy-start | bytes 393220
  35.1 5.9 %collective-permute-start.9 = (bf16[512,128]{1,0:T(8,128)(2,1)S(1)}, bf16[512,128]{1,0:T(8,128)(2,1)S(1)}, u32[]{:S(2)}, u32[]{:S(2)}) collective-permute-start(bf16[512,128]{1,0:T(8,128)(2,1)S(1)} %get-tuple-element.56), channel_id=1, source_target_pairs={{0,16},{16,0},{32,48},{48,32},{64,80},{80,64},{96,112},{112,96},{1... | collective-permute-start | bytes 393224 | tf_op jit(solution)/shard_map/ppermute | solution.py:50
  41.0 17.9 %collective-permute-start.14 = (bf16[512,1024]{1,0:T(8,128)(2,1)S(1)}, bf16[512,1024]{1,0:T(8,128)(2,1)S(1)}, u32[]{:S(2)}, u32[]{:S(2)}) collective-permute-start(bf16[512,1024]{1,0:T(8,128)(2,1)S(1)} %get-tuple-element.61.refs_2_), channel_id=1, source_target_pairs={{0,4},{1,13},{2,6},{3,15},{4,8},{5,1},{6,10},{7,3},{8,12},{9,5},{1... | collective-permute-start | bytes 3145736 | tf_op jit(solution)/shard_map/ppermute | solution.py:31
  43.4 18.0 %collective-permute-start.10 = (bf16[256,1024]{1,0:T(8,128)(2,1)S(1)}, bf16[256,1024]{1,0:T(8,128)(2,1)S(1)}, u32[]{:S(2)}, u32[]{:S(2)}) collective-permute-start(bf16[256,1024]{1,0:T(8,128)(2,1)S(1)} %get-tuple-element.57.refs_3_), channel_id=1, source_target_pairs={{0,4},{1,13},{2,6},{3,15},{4,8},{5,1},{6,10},{7,3},{8,12},{9,5},{1... | collective-permute-start | bytes 1572872 | tf_op jit(solution)/shard_map/ppermute | solution.py:31
  44.3 4.4 %collective-permute-start.11 = (bf16[512,128]{1,0:T(8,128)(2,1)S(1)}, bf16[512,128]{1,0:T(8,128)(2,1)S(1)}, u32[]{:S(2)}, u32[]{:S(2)}) collective-permute-start(bf16[512,128]{1,0:T(8,128)(2,1)S(1)} %get-tuple-element.60.refs_0_), channel_id=1, source_target_pairs={{0,16},{16,0},{32,48},{48,32},{64,80},{80,64},{96,112},{112,96},{1... | collective-permute-start | bytes 393224 | tf_op jit(solution)/shard_map/ppermute | solution.py:50
  48.7 10.4 %collective-permute-start.13 = (bf16[512,256]{1,0:T(8,128)(2,1)S(1)}, bf16[512,256]{1,0:T(8,128)(2,1)S(1)}, u32[]{:S(2)}, u32[]{:S(2)}) collective-permute-start(bf16[512,256]{1,0:T(8,128)(2,1)S(1)} %join.1.refs_7_.refs_1_), channel_id=1, source_target_pairs={{0,32},{16,48},{32,64},{48,80},{64,96},{80,112},{96,0},{112,16},{1... | collective-permute-start | bytes 786440 | tf_op jit(solution)/shard_map/ppermute | solution.py:50
  50.0 11.4 %collective-permute-start.12 = (bf16[512,256]{1,0:T(8,128)(2,1)S(1)}, bf16[512,256]{1,0:T(8,128)(2,1)S(1)}, u32[]{:S(2)}, u32[]{:S(2)}) collective-permute-start(bf16[512,256]{1,0:T(8,128)(2,1)S(1)} %join.1.refs_7_.refs_1_), channel_id=1, source_target_pairs={{0,96},{16,112},{32,0},{48,16},{64,32},{80,48},{96,64},{112,80},{1... | collective-permute-start | bytes 786440 | tf_op jit(solution)/shard_map/ppermute | solution.py:50
  51.6 19.3 %collective-permute-start.18 = (bf16[256,1024]{1,0:T(8,128)(2,1)S(1)}, bf16[256,1024]{1,0:T(8,128)(2,1)S(1)}, u32[]{:S(2)}, u32[]{:S(2)}) collective-permute-start(bf16[256,1024]{1,0:T(8,128)(2,1)S(1)} %phase.8.refs_2_), channel_id=1, source_target_pairs={{0,2},{1,3},{2,0},{3,1},{4,6},{5,7},{6,4},{7,5},{8,10},{9,11},{10,... | collective-permute-start | bytes 1572872 | tf_op jit(solution)/shard_map/ppermute | solution.py:37
  58.9 11.9 %collective-permute-start.19 = (bf16[256,1024]{1,0:T(8,128)(2,1)S(1)}, bf16[256,1024]{1,0:T(8,128)(2,1)S(1)}, u32[]{:S(2)}, u32[]{:S(2)}) collective-permute-start(bf16[256,1024]{1,0:T(8,128)(2,1)S(1)} %get-tuple-element.68), channel_id=1, source_target_pairs={{0,4},{1,13},{2,6},{3,15},{4,8},{5,1},{6,10},{7,3},{8,12},{9,5},{1... | collective-permute-start | bytes 1572872 | tf_op jit(solution)/shard_map/ppermute | solution.py:31
  59.1 16.7 %collective-permute-start.16 = (bf16[256,1024]{1,0:T(8,128)(2,1)S(1)}, bf16[256,1024]{1,0:T(8,128)(2,1)S(1)}, u32[]{:S(2)}, u32[]{:S(2)}) collective-permute-start(bf16[256,1024]{1,0:T(8,128)(2,1)S(1)} %slice.7), channel_id=1, source_target_pairs={{0,2},{1,3},{2,0},{3,1},{4,6},{5,7},{6,4},{7,5},{8,10},{9,11},{10,... | collective-permute-start | bytes 1572872 | tf_op jit(solution)/shard_map/ppermute | solution.py:37
  61.4 14.3 %collective-permute-start.15 = (bf16[256,1024]{1,0:T(8,128)(2,1)S(1)}, bf16[256,1024]{1,0:T(8,128)(2,1)S(1)}, u32[]{:S(2)}, u32[]{:S(2)}) collective-permute-start(bf16[256,1024]{1,0:T(8,128)(2,1)S(1)} %get-tuple-element.66.refs_6_.refs_3_), channel_id=1, source_target_pairs={{0,4},{1,13},{2,6},{3,15},{4,8},{5,1},{6,10},{7,3},{8,12},{9,5},{1... | collective-permute-start | bytes 1572872 | tf_op jit(solution)/shard_map/ppermute | solution.py:31
  64.2 10.2 %collective-permute-start.17 = (bf16[512,256]{1,0:T(8,128)(2,1)S(1)}, bf16[512,256]{1,0:T(8,128)(2,1)S(1)}, u32[]{:S(2)}, u32[]{:S(2)}) collective-permute-start(bf16[512,256]{1,0:T(8,128)(2,1)S(1)} %get-tuple-element.67.refs_0_), channel_id=1, source_target_pairs={{0,64},{16,80},{32,96},{48,112},{64,0},{80,16},{96,32},{112,48},{1... | collective-permute-start | bytes 786440 | tf_op jit(solution)/shard_map/ppermute | solution.py:50
  75.8 7.4 %collective-permute-start.22 = (bf16[768,1024]{1,0:T(8,128)(2,1)S(1)}, bf16[768,1024]{1,0:T(8,128)(2,1)S(1)}, u32[]{:S(2)}, u32[]{:S(2)}) collective-permute-start(bf16[768,1024]{1,0:T(8,128)(2,1)S(1)} %get-tuple-element.76), channel_id=1, source_target_pairs={{0,1},{1,0},{2,3},{3,2},{4,5},{5,4},{6,7},{7,6},{8,9},{9,8},{10,11... | collective-permute-start | bytes 4718600 | tf_op jit(solution)/shard_map/ppermute | solution.py:41
  78.7 3.8 %collective-permute-start.20 = (bf16[256,1024]{1,0:T(8,128)(2,1)S(1)}, bf16[256,1024]{1,0:T(8,128)(2,1)S(1)}, u32[]{:S(2)}, u32[]{:S(2)}) collective-permute-start(bf16[256,1024]{1,0:T(8,128)(2,1)S(1)} %get-tuple-element.73.refs_1_), channel_id=1, source_target_pairs={{0,1},{1,0},{2,3},{3,2},{4,5},{5,4},{6,7},{7,6},{8,9},{9,8},{10,11... | collective-permute-start | bytes 1572872 | tf_op jit(solution)/shard_map/ppermute | solution.py:41
  78.7 4.5 %collective-permute-start.21 = (bf16[256,1024]{1,0:T(8,128)(2,1)S(1)}, bf16[256,1024]{1,0:T(8,128)(2,1)S(1)}, u32[]{:S(2)}, u32[]{:S(2)}) collective-permute-start(bf16[256,1024]{1,0:T(8,128)(2,1)S(1)} %get-tuple-element.74.refs_2_), channel_id=1, source_target_pairs={{0,1},{1,0},{2,3},{3,2},{4,5},{5,4},{6,7},{7,6},{8,9},{9,8},{10,11... | collective-permute-start | bytes 1572872 | tf_op jit(solution)/shard_map/ppermute | solution.py:41

commit v5 on v4

--- a/solution.py
+++ b/solution.py
@@ -119,7 +119,7 @@
             pltpu.SemaphoreType.DMA((rows // BLOCK + 1,)),
             pltpu.SemaphoreType.DMA((Y,)),
         ],
-        compiler_params=pltpu.CompilerParams(vmem_limit_bytes=8 * MIB),
+        compiler_params=pltpu.CompilerParams(vmem_limit_bytes=4 * MIB),
         cost_estimate=cost(rows * columns, 4 * rows * columns),
         name="prepare",
     )(*(pltpu.with_memory_space_constraint(v, pltpu.HBM) for v in operands))
@@ -183,7 +183,7 @@
         out_specs=[spec] * len(out_shapes),
         out_shape=out_shapes,
         scratch_shapes=[pltpu.SemaphoreType.DMA((copies,))],
-        compiler_params=pltpu.CompilerParams(vmem_limit_bytes=4 * MIB),
+        compiler_params=pltpu.CompilerParams(vmem_limit_bytes=3 * MIB),
         cost_estimate=cost(tokens.size, 2 * tokens.size),
         name=name,
     )(pltpu.with_memory_space_constraint(tokens, pltpu.HBM), *after)
@@ -249,7 +249,7 @@
             ),
         ],
         input_output_aliases=aliases,
-        compiler_params=pltpu.CompilerParams(vmem_limit_bytes=6 * MIB),
+        compiler_params=pltpu.CompilerParams(vmem_limit_bytes=3 * MIB),
         cost_estimate=cost(4 * count * depth * columns, 2 * columns * depth)
         if counted
         else cost(1, 1),
@@ -312,7 +312,7 @@
         out_specs=spec,
         out_shape=out_shape,
         input_output_aliases={} if last else {1 + len(pieces): 0},
-        compiler_params=pltpu.CompilerParams(vmem_limit_bytes=6 * MIB),
+        compiler_params=pltpu.CompilerParams(vmem_limit_bytes=3 * MIB),
         cost_estimate=cost(2 * count * depth * columns, 2 * columns * depth),
         name="finish",
     )(*operands, *after)
@@ -395,7 +395,7 @@
         in_specs=[spec] * count + [pl.BlockSpec(memory_space=pl.ANY)] * len(after),
         out_specs=jax.tree.map(lambda _: spec, out_shape),
         out_shape=out_shape,
-        compiler_params=pltpu.CompilerParams(vmem_limit_bytes=4 * MIB),
+        compiler_params=pltpu.CompilerParams(vmem_limit_bytes=3 * MIB),
         cost_estimate=cost(8 * nbytes, 2 * nbytes),
         name=name,
     )(*operands, *after)
@@ -443,9 +443,14 @@
         after=[totals[0]],
     )
     other_sum = across_replicas(other_sum, lambda y, x: (y, 1 - x))
-    ring_2, high_0, low_1, other_sum = phase([ring_2, high_0, low_1, other_sum])
-
-    ring_3 = along_z(ring_2)
+    ring_2, high_0 = phase([ring_2, high_0], after=[own_sum])
+
+    high_r2 = ring_2[half:]
+    high_r3 = along_z(high_r2)
+    low_r3 = along_z(ring_2[:half])
+    high_2 = along_x(high_r2)
+    low_1, other_sum = phase([low_1, other_sum], after=[ring_2])
+
     low_2 = along_z(low_1)
     new, velocity = whole(
         update_kernel,
@@ -454,11 +459,6 @@
         [snapshot, momentum, own_sum, other_sum],
     )
     new_other = across_replicas(new, lambda y, x: (y, 1 - x))
-    (high_2_sent,) = phase([ring_2[half:]], after=[new_other])
-    high_2 = along_x(high_2_sent)
-    pair = join(new, new_other, after=[high_2_sent])
-    pair_1 = across_replicas(pair, lambda y, x: (y - 1, x))
-    pair_3 = across_replicas(pair, lambda y, x: (y + 1, x))
     totals = project_on(
         totals,
         [
@@ -466,40 +466,50 @@
             ((0, 1, 0, 0), low_0),
             ((0, 1, 0, half), high_0),
         ],
-        after=[pair],
+        after=[new],
         counted=False,
     )
-    ring_3, high_0 = phase([ring_3, high_0], after=[totals[0]])
-
+    high_r3, high_0 = phase([high_r3, high_0], after=[totals[0]])
+
+    high_3 = along_x(high_r3)
     high_1 = along_z(high_0)
-    high_3 = along_x(ring_3[half:])
-    low_2, pair = phase([low_2, pair], after=[pair_1, pair_3, ring_3])
+    (new_other,) = phase([new_other], after=[high_r3, low_r3, high_2])
+    pair = join(new, new_other)
+    pair_1 = across_replicas(pair, lambda y, x: (y - 1, x))
+    pair_3 = across_replicas(pair, lambda y, x: (y + 1, x))
+    (low_2,) = phase([low_2], after=[pair])
 
     low_3 = along_z(low_2)
-    pair_2 = across_replicas(pair, lambda y, x: (y + 2, x))
     totals = project_on(
         totals,
         [
-            ((3, 0, 0, 0), ring_3),
+            ((3, 0, 0, 0), low_r3),
+            ((3, 0, 0, half), high_r3),
             ((1, 1, 0, 0), low_1),
         ],
         after=[low_2],
-    )
+        counted=False,
+    )
+    (pair,) = phase([pair], after=[totals[0], pair_1])
+    pair_2 = across_replicas(pair, lambda y, x: (y + 2, x))
     own_total, other_total = project_on(
         totals,
         [
             ((2, 1, 0, half), high_2),
             ((2, 1, 0, 0), low_2),
             ((1, 1, 0, half), high_1),
+            ((3, 1, 0, half), high_3),
         ],
         last=True,
-    )
-    low_3, high_3, pair_2, other_total = phase([low_3, high_3, pair_2, other_total])
-
-    low_3_other, high_3_other = to_core(low_3), to_core(high_3)
+        counted=False,
+        after=[pair],
+    )
+    low_3, other_total, pair_2 = phase([low_3, other_total, pair_2], after=[pair_3])
+
+    low_3_other = to_core(low_3)
     other_total = to_core(other_total)
     own_total = finish(
-        tokens, [((3, 1, 0, 0), low_3), ((3, 1, 0, half), high_3)], rows, [own_total]
+        tokens, [((3, 1, 0, 0), low_3)], rows, [own_total]
     )
     new_weights, done = whole(
         assemble_kernel,
@@ -510,7 +520,7 @@
     )
     next_keys = finish(
         tokens,
-        [((3, 1, 1, 0), low_3_other), ((3, 1, 1, half), high_3_other)],
+        [((3, 1, 1, 0), low_3_other)],
         rows,
         [own_total, other_total],
         row_scale,

time: 86.1 us -> 83.7 us (0.972)
  starting transfers between devices: 39.2 us -> 37.7 us
    ppermute x8, waiting for transfers between devices: 5.65 us -> 9.99 us  [across_replicas(): return lax.ppermute(value, 'replica', pairs)]
    ppermute x7 -> x8, waiting for transfers between devices: 3.66 us -> 0.22 us  [along_z(): lax.ppermute(value, 'fsdp', fsdp_perm(lambda z, x, c: (z + 1 - 2 * c, x,...]
    ppermute x4 -> x3, starting transfers between devices: 4.9 us -> 7.18 us  [to_core(): return lax.ppermute(value, 'fsdp', fsdp_perm(lambda z, x, c: (z, x, 1 - c)))]
    ppermute x4, starting transfers between devices: 10.6 us -> 8.78 us  [along_x(): return lax.ppermute(value, 'fsdp', fsdp_perm(lambda z, x, c: (z, 1 - x, c)))]
    ppermute x4, waiting for transfers between devices: 5.51 us -> 3.92 us  [along_x(): return lax.ppermute(value, 'fsdp', fsdp_perm(lambda z, x, c: (z, 1 - x, c)))]
    ppermute x8, starting transfers between devices: 13.1 us -> 11.6 us  [across_replicas(): return lax.ppermute(value, 'replica', pairs)]
    pallas_call x2, Pallas kernels: 4.5 us -> 3.44 us  [finish(): pl.pallas_call(functools.partial(finish_kernel, places, rows, len(totals)...]
    ppermute x7 -> x8, starting transfers between devices: 10.7 us -> 10.1 us  [along_z(): lax.ppermute(value, 'fsdp', fsdp_perm(lambda z, x, c: (z + 1 - 2 * c, x,...]
  transfers between devices with their start and end apart: 23 -> 23, of which waited for: 10 -> 11; matrix products, arithmetic and copies ran while one was open for 0% -> 0% of each run, Pallas kernels for 32% -> 33%
where the time goes in v5:
time: 83.7 us; the launch traced here: 83.6 us
  starting transfers between devices  37.7 us (45%)
  Pallas kernels  29.6 us (35%)
  waiting for transfers between devices  15.4 us (18%)
    pallas_call x4, Pallas kernels, project(): pl.pallas_call(functools.partial(project_kernel, places, rows, bool(total...  16.4 us
    ppermute x8, starting transfers between devices, across_replicas(): return lax.ppermute(value, 'replica', pairs)  11.6 us
    ppermute x8, starting transfers between devices, along_z(): lax.ppermute(value, 'fsdp', fsdp_perm(lambda z, x, c: (z + 1 - 2 * c, x,...  10.1 us
    ppermute x8, waiting for transfers between devices, across_replicas(): return lax.ppermute(value, 'replica', pairs)  9.99 us
    ppermute x4, starting transfers between devices, along_x(): return lax.ppermute(value, 'fsdp', fsdp_perm(lambda z, x, c: (z, 1 - x, c)))  8.78 us
    ppermute x3, starting transfers between devices, to_core(): return lax.ppermute(value, 'fsdp', fsdp_perm(lambda z, x, c: (z, x, 1 - c)))  7.18 us
    pallas_call x1, Pallas kernels, fetch(): pl.pallas_call(run, in_specs=[pl.BlockSpec(memory_space=pltpu.HBM)] + [pl...  4.92 us
    ppermute x4, waiting for transfers between devices, along_x(): return lax.ppermute(value, 'fsdp', fsdp_perm(lambda z, x, c: (z, 1 - x, c)))  3.92 us
  transfers between devices with their start and end apart: 23, of which 11 were waited for; matrix products, arithmetic and copies ran while one was open for 0% of the time, Pallas kernels for 33%

profile of v5, /device:TPU:1, one launch (start us, length us, event | category | flops | bytes accessed | tf_op | source)
XLA Modules:
  0.0 83.6 jit_solution(7584603310428523835)
XLA Ops:
  0.6 1.5 %collective-permute-start.6 = (bf16[1,768,8192]{2,1,0:T(8,128)(2,1)}, bf16[1,768,8192]{2,1,0:T(8,128)(2,1)S(1)}, u32[]{:S(2)}, u32[]{:S(2)}) collective-permute-start(bf16[1,768,8192]{2,1,0:T(8,128)(2,1)} %tokens_hbm.1), channel_id=1, source_target_pairs={{0,1},{1,0},{2,3},{3,2},{4,5},{5,4},{6,7},{7,6},{8,9},{9,8},{10,11... | collective-permute-start | bytes 37748744 | tf_op jit(solution)/shard_map/ppermute | solution.py:41
  2.1 1.6 %prepare.1 = (bf16[512,1024]{1,0:T(8,128)(2,1)S(1)}, bf16[256,1024]{1,0:T(8,128)(2,1)S(1)}, bf16[256,1024]{1,0:T(8,128)(2,1)S(1)}, bf16[512,256]{1,0:T(8,128)(2,...) custom-call(f32[1,8192]{1,0:T(1,128)} %gain_hbm.1, ...), custom_call_target="tpu_custom_call" | custom-call | flops 524288 | bytes 2097152 | tf_op jit(solution)/shard_map/prepare/pallas_call | solution.py:111
  3.8 3.9 %collective-permute-start = (bf16[512,1024]{1,0:T(8,128)(2,1)S(1)}, bf16[512,1024]{1,0:T(8,128)(2,1)S(1)}, u32[]{:S(2)}, u32[]{:S(2)}) collective-permute-start(bf16[512,1024]{1,0:T(8,128)(2,1)S(1)} %get-tuple-element.39.refs_0_.refs_2_), channel_id=1, source_target_pairs={{0,4},{1,13},{2,6},{3,15},{4,8},{5,1},{6,10},{7,3},{8,12},{9,5},{1... | collective-permute-start | bytes 3145736 | tf_op jit(solution)/shard_map/ppermute | solution.py:31
  7.7 2.7 %collective-permute-start.1 = (bf16[256,1024]{1,0:T(8,128)(2,1)S(1)}, bf16[256,1024]{1,0:T(8,128)(2,1)S(1)}, u32[]{:S(2)}, u32[]{:S(2)}) collective-permute-start(bf16[256,1024]{1,0:T(8,128)(2,1)S(1)} %get-tuple-element.41), channel_id=1, source_target_pairs={{0,2},{1,3},{2,0},{3,1},{4,6},{5,7},{6,4},{7,5},{8,10},{9,11},{10,... | collective-permute-start | bytes 1572872 | tf_op jit(solution)/shard_map/ppermute | solution.py:37
  10.4 1.3 %collective-permute-start.2 = (bf16[512,256]{1,0:T(8,128)(2,1)S(1)}, bf16[512,256]{1,0:T(8,128)(2,1)S(1)}, u32[]{:S(2)}, u32[]{:S(2)}) collective-permute-start(bf16[512,256]{1,0:T(8,128)(2,1)S(1)} %get-tuple-element.45), channel_id=1, source_target_pairs={{0,32},{16,48},{32,64},{48,80},{64,96},{80,112},{96,0},{112,16},{1... | collective-permute-start | bytes 786440 | tf_op jit(solution)/shard_map/ppermute | solution.py:50
  11.7 1.4 %collective-permute-start.3 = (bf16[512,256]{1,0:T(8,128)(2,1)S(1)}, bf16[512,256]{1,0:T(8,128)(2,1)S(1)}, u32[]{:S(2)}, u32[]{:S(2)}) collective-permute-start(bf16[512,256]{1,0:T(8,128)(2,1)S(1)} %get-tuple-element.46), channel_id=1, source_target_pairs={{0,96},{16,112},{32,0},{48,16},{64,32},{80,48},{96,64},{112,80},{1... | collective-permute-start | bytes 786440 | tf_op jit(solution)/shard_map/ppermute | solution.py:50
  13.1 4.9 %load.1 = (bf16[1,768,8192]{2,1,0:T(8,128)(2,1)S(1)}, f32[768,128]{1,0:T(8,128)S(1)}) custom-call(bf16[1,768,8192]{2,1,0:T(8,128)(2,1)} %tokens_hbm.1, bf16[512,1024]{1,0:T(8,128)(2,1)S(1)} %get-tuple-element.39.refs_0_.refs_2_), custom_call_target="tpu_custom_call" | custom-call | flops 6291456 | bytes 12582912 | tf_op jit(solution)/shard_map/load/pallas_call | solution.py:179
  18.1 0.8 collective-permute-done.2.refs_5_.refs_2_
  18.9 0.4 collective-permute-done.3.refs_6_.refs_4_
  19.2 2.2 %collective-permute-done.1.refs_1_ = bf16[256,1024]{1,0:T(8,128)(2,1)S(1)} collective-permute-done((bf16[256,1024]{1,0:T(8,128)(2,1)S(1)}, bf16[256,1024]{1,0:T(8,128)(2,1)S(1)}, u32[]{:S(2)}, u32[]{:S(2)}) %collective-permute-start.1) | collective-permute-done | bytes 524320 | tf_op jit(solution)/shard_map/ppermute | solution.py:37
  21.5 0.0 collective-permute-done.refs_0_
  21.5 1.4 %collective-permute-start.8 = (bf16[512,1024]{1,0:T(8,128)(2,1)S(1)}, bf16[512,1024]{1,0:T(8,128)(2,1)S(1)}, u32[]{:S(2)}, u32[]{:S(2)}) collective-permute-start(bf16[512,1024]{1,0:T(8,128)(2,1)S(1)} %get-tuple-element.50.refs_3_), channel_id=1, source_target_pairs={{0,4},{1,13},{2,6},{3,15},{4,8},{5,1},{6,10},{7,3},{8,12},{9,5},{1... | collective-permute-start | bytes 3145736 | tf_op jit(solution)/shard_map/ppermute | solution.py:31
  22.9 2.7 %collective-permute-start.9 = (bf16[256,1024]{1,0:T(8,128)(2,1)S(1)}, bf16[256,1024]{1,0:T(8,128)(2,1)S(1)}, u32[]{:S(2)}, u32[]{:S(2)}) collective-permute-start(bf16[256,1024]{1,0:T(8,128)(2,1)S(1)} %get-tuple-element.53), channel_id=1, source_target_pairs={{0,2},{1,3},{2,0},{3,1},{4,6},{5,7},{6,4},{7,5},{8,10},{9,11},{10,... | collective-permute-start | bytes 1572872 | tf_op jit(solution)/shard_map/ppermute | solution.py:37
  25.6 2.9 %collective-permute-start.5 = (bf16[512,256]{1,0:T(8,128)(2,1)S(1)}, bf16[512,256]{1,0:T(8,128)(2,1)S(1)}, u32[]{:S(2)}, u32[]{:S(2)}) collective-permute-start(bf16[512,256]{1,0:T(8,128)(2,1)S(1)} %get-tuple-element.49), channel_id=1, source_target_pairs={{0,64},{16,80},{32,96},{48,112},{64,0},{80,16},{96,32},{112,48},{1... | collective-permute-start | bytes 786440 | tf_op jit(solution)/shard_map/ppermute | solution.py:50
  28.5 0.1 collective-permute-start.4
  28.6 4.0 %project.4 = (f32[768,1024]{1,0:T(8,128)S(1)}, f32[768,1024]{1,0:T(8,128)S(1)}) custom-call(bf16[1,768,8192]{2,1,0:T(8,128)(2,1)S(1)} %get-tuple-element.40.refs_0_, bf16[1,768,8192]{2,1,0:T(8,128)(2,1)S(1)} %collective-permute-done.6.refs_1_, bf16[512,1024]{1,0:T(8,128)(2,1)S(1)} %get-tuple-element.39.refs_0_.refs_2_, ...), custom_call_target="tpu_custom_call" | custom-call | flops 3221225472 | bytes 2097152 | tf_op jit(solution)/shard_map/project/pallas_call | solution.py:240
  32.6 2.5 %collective-permute-done.5.refs_3_ = bf16[512,256]{1,0:T(8,128)(2,1)S(1)} collective-permute-done((bf16[512,256]{1,0:T(8,128)(2,1)S(1)}, bf16[512,256]{1,0:T(8,128)(2,1)S(1)}, u32[]{:S(2)}, u32[]{:S(2)}) %collective-permute-start.5) | collective-permute-done | bytes 262176 | tf_op jit(solution)/shard_map/ppermute | solution.py:50
  35.1 1.1 %partial.1 = (f32[512,128]{1,0:T(8,128)S(1)}, bf16[512,128]{1,0:T(8,128)(2,1)S(1)}) custom-call(f32[512,1024]{1,0:T(8,128)S(1)} %copy-done, bf16[512,256]{1,0:T(8,128)(2,1)S(1)} %get-tuple-element.48.refs_1_, bf16[512,256]{1,0:T(8,128)(2,1)S(1)} %collective-permute-done.2.refs_5_.refs_2_, bf16[512,256]{1,0:T(8,128)(2,1)S(1)} %collective-permute-done.5.refs_3_, ...), custom_call_target="tpu_custom_call" | custom-call | flops 25165824 | bytes 6291456 | tf_op jit(solution)/shard_map/partial/pallas_call | solution.py:393
  36.2 0.0 copy-start.1
  36.2 0.1 collective-permute-start.7
  36.3 1.0 %collective-permute-done.9.refs_1_ = bf16[256,1024]{1,0:T(8,128)(2,1)S(1)} collective-permute-done((bf16[256,1024]{1,0:T(8,128)(2,1)S(1)}, bf16[256,1024]{1,0:T(8,128)(2,1)S(1)}, u32[]{:S(2)}, u32[]{:S(2)}) %collective-permute-start.9) | collective-permute-done | bytes 524320 | tf_op jit(solution)/shard_map/ppermute | solution.py:37
  37.4 0.1 fusion
  37.5 0.7 collective-permute-start.12
  38.2 0.1 collective-permute-start.13
  38.2 2.6 %collective-permute-start.14 = (bf16[256,1024]{1,0:T(8,128)(2,1)S(1)}, bf16[256,1024]{1,0:T(8,128)(2,1)S(1)}, u32[]{:S(2)}, u32[]{:S(2)}) collective-permute-start(bf16[256,1024]{1,0:T(8,128)(2,1)S(1)} %get-tuple-element.76), channel_id=1, source_target_pairs={{0,2},{1,3},{2,0},{3,1},{4,6},{5,7},{6,4},{7,5},{8,10},{9,11},{10,... | collective-permute-start | bytes 1572872 | tf_op jit(solution)/shard_map/ppermute | solution.py:37
  40.8 0.2 collective-permute-done.4.refs_0_
  41.0 0.2 collective-permute-done.7.refs_1_
  41.3 2.1 %collective-permute-start.10 = (bf16[256,1024]{1,0:T(8,128)(2,1)S(1)}, bf16[256,1024]{1,0:T(8,128)(2,1)S(1)}, u32[]{:S(2)}, u32[]{:S(2)}) collective-permute-start(bf16[256,1024]{1,0:T(8,128)(2,1)S(1)} %get-tuple-element.56.refs_4_), channel_id=1, source_target_pairs={{0,4},{1,13},{2,6},{3,15},{4,8},{5,1},{6,10},{7,3},{8,12},{9,5},{1... | collective-permute-start | bytes 1572872 | tf_op jit(solution)/shard_map/ppermute | solution.py:31
  43.3 0.8 update.1
  44.1 1.2 %collective-permute-start.11 = (bf16[512,128]{1,0:T(8,128)(2,1)S(1)}, bf16[512,128]{1,0:T(8,128)(2,1)S(1)}, u32[]{:S(2)}, u32[]{:S(2)}) collective-permute-start(bf16[512,128]{1,0:T(8,128)(2,1)S(1)} %get-tuple-element.58.refs_7_.refs_0_), channel_id=1, source_target_pairs={{0,16},{16,0},{32,48},{48,32},{64,80},{80,64},{96,112},{112,96},{1... | collective-permute-start | bytes 393224 | tf_op jit(solution)/shard_map/ppermute | solution.py:50
  45.3 4.5 %project.5 = (f32[768,1024]{1,0:T(8,128)S(1)}, f32[768,1024]{1,0:T(8,128)S(1)}) custom-call(bf16[1,768,8192]{2,1,0:T(8,128)(2,1)S(1)} %get-tuple-element.40.refs_0_, bf16[1,768,8192]{2,1,0:T(8,128)(2,1)S(1)} %collective-permute-done.6.refs_1_, bf16[512,1024]{1,0:T(8,128)(2,1)S(1)} %get-tuple-element.55.refs_2_, ...), custom_call_target="tpu_custom_call", output_to_operand_aliasing={{0}: (5, {}), {1}: (6, {})} | custom-call | flops 1 | bytes 1 | tf_op jit(solution)/shard_map/project/pallas_call | solution.py:240
  49.9 0.1 collective-permute-start.16
  49.9 4.9 %collective-permute-done.11.refs_0_ = bf16[512,128]{1,0:T(8,128)(2,1)S(1)} collective-permute-done((bf16[512,128]{1,0:T(8,128)(2,1)S(1)}, bf16[512,128]{1,0:T(8,128)(2,1)S(1)}, u32[]{:S(2)}, u32[]{:S(2)}) %collective-permute-start.11) | collective-permute-done | bytes 131104 | tf_op jit(solution)/shard_map/ppermute | solution.py:50
  54.8 0.7 collective-permute-start.17
  55.6 2.8 %collective-permute-start.18 = (bf16[512,256]{1,0:T(8,128)(2,1)S(1)}, bf16[512,256]{1,0:T(8,128)(2,1)S(1)}, u32[]{:S(2)}, u32[]{:S(2)}) collective-permute-start(bf16[512,256]{1,0:T(8,128)(2,1)S(1)} %join.1.refs_1_.refs_0_), channel_id=1, source_target_pairs={{0,96},{16,112},{32,0},{48,16},{64,32},{80,48},{96,64},{112,80},{1... | collective-permute-start | bytes 786440 | tf_op jit(solution)/shard_map/ppermute | solution.py:50
  58.4 1.8 %collective-permute-start.15 = (bf16[256,1024]{1,0:T(8,128)(2,1)S(1)}, bf16[256,1024]{1,0:T(8,128)(2,1)S(1)}, u32[]{:S(2)}, u32[]{:S(2)}) collective-permute-start(bf16[256,1024]{1,0:T(8,128)(2,1)S(1)} %phase.13.refs_7_.refs_3_), channel_id=1, source_target_pairs={{0,4},{1,13},{2,6},{3,15},{4,8},{5,1},{6,10},{7,3},{8,12},{9,5},{1... | collective-permute-start | bytes 1572872 | tf_op jit(solution)/shard_map/ppermute | solution.py:31
  60.2 3.7 %project.6 = (f32[768,1024]{1,0:T(8,128)S(1)}, f32[768,1024]{1,0:T(8,128)S(1)}) custom-call(bf16[1,768,8192]{2,1,0:T(8,128)(2,1)S(1)} %get-tuple-element.40.refs_0_, bf16[1,768,8192]{2,1,0:T(8,128)(2,1)S(1)} %collective-permute-done.6.refs_1_, bf16[256,1024]{1,0:T(8,128)(2,1)S(1)} %collective-permute-done.13.refs_2_, ...), custom_call_target="tpu_custom_call", output_to_operand_aliasing={{0}: (5, {}), {1}: (6, {})} | custom-call | flops 1 | bytes 1 | tf_op jit(solution)/shard_map/project/pallas_call | solution.py:240
  63.9 1.2 %collective-permute-done.20.refs_3_ = bf16[512,256]{1,0:T(8,128)(2,1)S(1)} collective-permute-done((bf16[512,256]{1,0:T(8,128)(2,1)S(1)}, bf16[512,256]{1,0:T(8,128)(2,1)S(1)}, u32[]{:S(2)}, u32[]{:S(2)}) %collective-permute-start.20) | collective-permute-done | bytes 262176 | tf_op jit(solution)/shard_map/ppermute | solution.py:50
  65.1 1.8 %collective-permute-start.19 = (bf16[512,256]{1,0:T(8,128)(2,1)S(1)}, bf16[512,256]{1,0:T(8,128)(2,1)S(1)}, u32[]{:S(2)}, u32[]{:S(2)}) collective-permute-start(bf16[512,256]{1,0:T(8,128)(2,1)S(1)} %phase.14.refs_8_.refs_0_), channel_id=1, source_target_pairs={{0,64},{16,80},{32,96},{48,112},{64,0},{80,16},{96,32},{112,48},{1... | collective-permute-start | bytes 786440 | tf_op jit(solution)/shard_map/ppermute | solution.py:50
  66.9 0.6 collective-permute-done.17.refs_5_
  67.6 4.2 %project.7 = (f32[768,1024]{1,0:T(8,128)S(1)}, bf16[768,1024]{1,0:T(8,128)(2,1)S(1)}) custom-call(bf16[1,768,8192]{2,1,0:T(8,128)(2,1)S(1)} %get-tuple-element.40.refs_0_, bf16[1,768,8192]{2,1,0:T(8,128)(2,1)S(1)} %collective-permute-done.6.refs_1_, bf16[256,1024]{1,0:T(8,128)(2,1)S(1)} %collective-permute-done.14.refs_3_.refs_2_, ...), custom_call_target="tpu_custom_call", output_to_operand_aliasing={{0}: (6, {})} | custom-call | flops 1 | bytes 1 | tf_op jit(solution)/shard_map/project/pallas_call | solution.py:240
  71.8 0.0 collective-permute-done.19.refs_2_
  71.8 5.6 %collective-permute-start.22 = (bf16[768,1024]{1,0:T(8,128)(2,1)S(1)}, bf16[768,1024]{1,0:T(8,128)(2,1)S(1)}, u32[]{:S(2)}, u32[]{:S(2)}) collective-permute-start(bf16[768,1024]{1,0:T(8,128)(2,1)S(1)} %get-tuple-element.70), channel_id=1, source_target_pairs={{0,1},{1,0},{2,3},{3,2},{4,5},{5,4},{6,7},{7,6},{8,9},{9,8},{10,11... | collective-permute-start | bytes 4718600 | tf_op jit(solution)/shard_map/ppermute | solution.py:41
  77.4 0.1 collective-permute-start.21
  77.5 1.1 %finish.2.refs_4_.refs_2_ = f32[768,1024]{1,0:T(8,128)S(1)} custom-call(bf16[1,768,8192]{2,1,0:T(8,128)(2,1)S(1)} %get-tuple-element.40.refs_0_, bf16[256,1024]{1,0:T(8,128)(2,1)S(1)} %get-tuple-element.68.refs_1_, f32[768,1024]{1,0:T(8,128)S(1)} %get-tuple-element.69.refs_2_), custom_call_target="tpu_custom_call", output_to_operand_aliasing={{}: (2, {})} | custom-call | flops 402653184 | bytes 524288 | tf_op jit(solution)/shard_map/finish/pallas_call | solution.py:308
  78.6 1.3 %assemble.1 = (bf16[512,1024]{1,0:T(8,128)(2,1)}, f32[8,128]{1,0:T(8,128)S(1)}) custom-call(bf16[512,256]{1,0:T(8,128)(2,1)S(1)} %phase.14.refs_8_.refs_0_, bf16[512,256]{1,0:T(8,128)(2,1)S(1)} %collective-permute-done.18.refs_2_.refs_1_, bf16[512,256]{1,0:T(8,128)(2,1)S(1)} %get-tuple-element.71.refs_2_, ...), custom_call_target="tpu_custom_call" | custom-call | flops 8388608 | bytes 2097152 | tf_op jit(solution)/shard_map/assemble/pallas_call | solution.py:393
  79.9 1.3 %collective-permute-done.21.refs_1_ = bf16[256,1024]{1,0:T(8,128)(2,1)S(1)} collective-permute-done((bf16[256,1024]{1,0:T(8,128)(2,1)S(1)}, bf16[256,1024]{1,0:T(8,128)(2,1)S(1)}, u32[]{:S(2)}, u32[]{:S(2)}) %collective-permute-start.21) | collective-permute-done | bytes 524320 | tf_op jit(solution)/shard_map/ppermute | solution.py:41
  81.2 2.4 %finish.3 = bf16[1,768,1024]{2,1,0:T(8,128)(2,1)} custom-call(bf16[1,768,8192]{2,1,0:T(8,128)(2,1)S(1)} %get-tuple-element.40.refs_0_, bf16[256,1024]{1,0:T(8,128)(2,1)S(1)} %collective-permute-done.21.refs_1_, f32[768,1024]{1,0:T(8,128)S(1)} %finish.2.refs_4_.refs_2_, bf16[768,1024]{1,0:T(8,128)(2,1)S(1)} %collective-permute-done.22.refs_3_, ...), custom_call_target="tpu_custom_call" | custom-call | flops 402653184 | bytes 524288 | tf_op jit(solution)/shard_map/finish/pallas_call | solution.py:308
  (23 shorter events, 0.1 us)
Async XLA Ops:
  0.6 28.0 %collective-permute-start.6 = (bf16[1,768,8192]{2,1,0:T(8,128)(2,1)}, bf16[1,768,8192]{2,1,0:T(8,128)(2,1)S(1)}, u32[]{:S(2)}, u32[]{:S(2)}) collective-permute-start(bf16[1,768,8192]{2,1,0:T(8,128)(2,1)} %tokens_hbm.1), channel_id=1, source_target_pairs={{0,1},{1,0},{2,3},{3,2},{4,5},{5,4},{6,7},{7,6},{8,9},{9,8},{10,11... | collective-permute-start | bytes 37748744 | tf_op jit(solution)/shard_map/ppermute | solution.py:41
  3.8 17.7 %collective-permute-start = (bf16[512,1024]{1,0:T(8,128)(2,1)S(1)}, bf16[512,1024]{1,0:T(8,128)(2,1)S(1)}, u32[]{:S(2)}, u32[]{:S(2)}) collective-permute-start(bf16[512,1024]{1,0:T(8,128)(2,1)S(1)} %get-tuple-element.39.refs_0_.refs_2_), channel_id=1, source_target_pairs={{0,4},{1,13},{2,6},{3,15},{4,8},{5,1},{6,10},{7,3},{8,12},{9,5},{1... | collective-permute-start | bytes 3145736 | tf_op jit(solution)/shard_map/ppermute | solution.py:31
  7.7 13.8 %collective-permute-start.1 = (bf16[256,1024]{1,0:T(8,128)(2,1)S(1)}, bf16[256,1024]{1,0:T(8,128)(2,1)S(1)}, u32[]{:S(2)}, u32[]{:S(2)}) collective-permute-start(bf16[256,1024]{1,0:T(8,128)(2,1)S(1)} %get-tuple-element.41), channel_id=1, source_target_pairs={{0,2},{1,3},{2,0},{3,1},{4,6},{5,7},{6,4},{7,5},{8,10},{9,11},{10,... | collective-permute-start | bytes 1572872 | tf_op jit(solution)/shard_map/ppermute | solution.py:37
  10.4 8.5 %collective-permute-start.2 = (bf16[512,256]{1,0:T(8,128)(2,1)S(1)}, bf16[512,256]{1,0:T(8,128)(2,1)S(1)}, u32[]{:S(2)}, u32[]{:S(2)}) collective-permute-start(bf16[512,256]{1,0:T(8,128)(2,1)S(1)} %get-tuple-element.45), channel_id=1, source_target_pairs={{0,32},{16,48},{32,64},{48,80},{64,96},{80,112},{96,0},{112,16},{1... | collective-permute-start | bytes 786440 | tf_op jit(solution)/shard_map/ppermute | solution.py:50
  11.7 7.5 %collective-permute-start.3 = (bf16[512,256]{1,0:T(8,128)(2,1)S(1)}, bf16[512,256]{1,0:T(8,128)(2,1)S(1)}, u32[]{:S(2)}, u32[]{:S(2)}) collective-permute-start(bf16[512,256]{1,0:T(8,128)(2,1)S(1)} %get-tuple-element.46), channel_id=1, source_target_pairs={{0,96},{16,112},{32,0},{48,16},{64,32},{80,48},{96,64},{112,80},{1... | collective-permute-start | bytes 786440 | tf_op jit(solution)/shard_map/ppermute | solution.py:50
  21.5 15.9 %collective-permute-start.8 = (bf16[512,1024]{1,0:T(8,128)(2,1)S(1)}, bf16[512,1024]{1,0:T(8,128)(2,1)S(1)}, u32[]{:S(2)}, u32[]{:S(2)}) collective-permute-start(bf16[512,1024]{1,0:T(8,128)(2,1)S(1)} %get-tuple-element.50.refs_3_), channel_id=1, source_target_pairs={{0,4},{1,13},{2,6},{3,15},{4,8},{5,1},{6,10},{7,3},{8,12},{9,5},{1... | collective-permute-start | bytes 3145736 | tf_op jit(solution)/shard_map/ppermute | solution.py:31
  22.9 14.5 %collective-permute-start.9 = (bf16[256,1024]{1,0:T(8,128)(2,1)S(1)}, bf16[256,1024]{1,0:T(8,128)(2,1)S(1)}, u32[]{:S(2)}, u32[]{:S(2)}) collective-permute-start(bf16[256,1024]{1,0:T(8,128)(2,1)S(1)} %get-tuple-element.53), channel_id=1, source_target_pairs={{0,2},{1,3},{2,0},{3,1},{4,6},{5,7},{6,4},{7,5},{8,10},{9,11},{10,... | collective-permute-start | bytes 1572872 | tf_op jit(solution)/shard_map/ppermute | solution.py:37
  25.6 9.5 %collective-permute-start.5 = (bf16[512,256]{1,0:T(8,128)(2,1)S(1)}, bf16[512,256]{1,0:T(8,128)(2,1)S(1)}, u32[]{:S(2)}, u32[]{:S(2)}) collective-permute-start(bf16[512,256]{1,0:T(8,128)(2,1)S(1)} %get-tuple-element.49), channel_id=1, source_target_pairs={{0,64},{16,80},{32,96},{48,112},{64,0},{80,16},{96,32},{112,48},{1... | collective-permute-start | bytes 786440 | tf_op jit(solution)/shard_map/ppermute | solution.py:50
  28.5 12.5 %collective-permute-start.4 = (bf16[256,1024]{1,0:T(8,128)(2,1)S(1)}, bf16[256,1024]{1,0:T(8,128)(2,1)S(1)}, u32[]{:S(2)}, u32[]{:S(2)}) collective-permute-start(bf16[256,1024]{1,0:T(8,128)(2,1)S(1)} %get-tuple-element.47.refs_3_), channel_id=1, source_target_pairs={{0,4},{1,13},{2,6},{3,15},{4,8},{5,1},{6,10},{7,3},{8,12},{9,5},{1... | collective-permute-start | bytes 1572872 | tf_op jit(solution)/shard_map/ppermute | solution.py:31
  28.6 6.5 %copy-start = (f32[512,1024]{1,0:T(8,128)S(1)}, f32[512,1024]{1,0:T(8,128)}, u32[]{:S(2)}) copy-start(f32[512,1024]{1,0:T(8,128)} %refs_0_.3) | copy-start | bytes 6291460
  36.2 7.1 %copy-start.1 = (bf16[512,128]{1,0:T(8,128)(2,1)S(1)}, bf16[512,128]{1,0:T(8,128)(2,1)}, u32[]{:S(2)}) copy-start(bf16[512,128]{1,0:T(8,128)(2,1)} %refs_1_.1) | copy-start | bytes 393220
  36.2 5.0 %collective-permute-start.7 = (bf16[512,128]{1,0:T(8,128)(2,1)S(1)}, bf16[512,128]{1,0:T(8,128)(2,1)S(1)}, u32[]{:S(2)}, u32[]{:S(2)}) collective-permute-start(bf16[512,128]{1,0:T(8,128)(2,1)S(1)} %get-tuple-element.52), channel_id=1, source_target_pairs={{0,16},{16,0},{32,48},{48,32},{64,80},{80,64},{96,112},{112,96},{1... | collective-permute-start | bytes 393224 | tf_op jit(solution)/shard_map/ppermute | solution.py:50
  37.5 12.4 %collective-permute-start.12 = (bf16[256,1024]{1,0:T(8,128)(2,1)S(1)}, bf16[256,1024]{1,0:T(8,128)(2,1)S(1)}, u32[]{:S(2)}, u32[]{:S(2)}) collective-permute-start(bf16[256,1024]{1,0:T(8,128)(2,1)S(1)} %get-tuple-element.76), channel_id=1, source_target_pairs={{0,4},{1,13},{2,6},{3,15},{4,8},{5,1},{6,10},{7,3},{8,12},{9,5},{1... | collective-permute-start | bytes 1572872 | tf_op jit(solution)/shard_map/ppermute | solution.py:31
  38.2 17.4 %collective-permute-start.13 = (bf16[256,1024]{1,0:T(8,128)(2,1)S(1)}, bf16[256,1024]{1,0:T(8,128)(2,1)S(1)}, u32[]{:S(2)}, u32[]{:S(2)}) collective-permute-start(bf16[256,1024]{1,0:T(8,128)(2,1)S(1)} %get-tuple-element.75), channel_id=1, source_target_pairs={{0,4},{1,13},{2,6},{3,15},{4,8},{5,1},{6,10},{7,3},{8,12},{9,5},{1... | collective-permute-start | bytes 1572872 | tf_op jit(solution)/shard_map/ppermute | solution.py:31
  38.2 17.3 %collective-permute-start.14 = (bf16[256,1024]{1,0:T(8,128)(2,1)S(1)}, bf16[256,1024]{1,0:T(8,128)(2,1)S(1)}, u32[]{:S(2)}, u32[]{:S(2)}) collective-permute-start(bf16[256,1024]{1,0:T(8,128)(2,1)S(1)} %get-tuple-element.76), channel_id=1, source_target_pairs={{0,2},{1,3},{2,0},{3,1},{4,6},{5,7},{6,4},{7,5},{8,10},{9,11},{10,... | collective-permute-start | bytes 1572872 | tf_op jit(solution)/shard_map/ppermute | solution.py:37
  41.3 17.1 %collective-permute-start.10 = (bf16[256,1024]{1,0:T(8,128)(2,1)S(1)}, bf16[256,1024]{1,0:T(8,128)(2,1)S(1)}, u32[]{:S(2)}, u32[]{:S(2)}) collective-permute-start(bf16[256,1024]{1,0:T(8,128)(2,1)S(1)} %get-tuple-element.56.refs_4_), channel_id=1, source_target_pairs={{0,4},{1,13},{2,6},{3,15},{4,8},{5,1},{6,10},{7,3},{8,12},{9,5},{1... | collective-permute-start | bytes 1572872 | tf_op jit(solution)/shard_map/ppermute | solution.py:31
  44.1 10.7 %collective-permute-start.11 = (bf16[512,128]{1,0:T(8,128)(2,1)S(1)}, bf16[512,128]{1,0:T(8,128)(2,1)S(1)}, u32[]{:S(2)}, u32[]{:S(2)}) collective-permute-start(bf16[512,128]{1,0:T(8,128)(2,1)S(1)} %get-tuple-element.58.refs_7_.refs_0_), channel_id=1, source_target_pairs={{0,16},{16,0},{32,48},{48,32},{64,80},{80,64},{96,112},{112,96},{1... | collective-permute-start | bytes 393224 | tf_op jit(solution)/shard_map/ppermute | solution.py:50
  49.9 17.1 %collective-permute-start.16 = (bf16[256,1024]{1,0:T(8,128)(2,1)S(1)}, bf16[256,1024]{1,0:T(8,128)(2,1)S(1)}, u32[]{:S(2)}, u32[]{:S(2)}) collective-permute-start(bf16[256,1024]{1,0:T(8,128)(2,1)S(1)} %get-tuple-element.63), channel_id=1, source_target_pairs={{0,4},{1,13},{2,6},{3,15},{4,8},{5,1},{6,10},{7,3},{8,12},{9,5},{1... | collective-permute-start | bytes 1572872 | tf_op jit(solution)/shard_map/ppermute | solution.py:31
  54.8 12.7 %collective-permute-start.17 = (bf16[256,1024]{1,0:T(8,128)(2,1)S(1)}, bf16[256,1024]{1,0:T(8,128)(2,1)S(1)}, u32[]{:S(2)}, u32[]{:S(2)}) collective-permute-start(bf16[256,1024]{1,0:T(8,128)(2,1)S(1)} %get-tuple-element.62.refs_1_.refs_3_), channel_id=1, source_target_pairs={{0,2},{1,3},{2,0},{3,1},{4,6},{5,7},{6,4},{7,5},{8,10},{9,11},{10,... | collective-permute-start | bytes 1572872 | tf_op jit(solution)/shard_map/ppermute | solution.py:37
  55.6 8.3 %collective-permute-start.18 = (bf16[512,256]{1,0:T(8,128)(2,1)S(1)}, bf16[512,256]{1,0:T(8,128)(2,1)S(1)}, u32[]{:S(2)}, u32[]{:S(2)}) collective-permute-start(bf16[512,256]{1,0:T(8,128)(2,1)S(1)} %join.1.refs_1_.refs_0_), channel_id=1, source_target_pairs={{0,96},{16,112},{32,0},{48,16},{64,32},{80,48},{96,64},{112,80},{1... | collective-permute-start | bytes 786440 | tf_op jit(solution)/shard_map/ppermute | solution.py:50
  58.4 6.7 %collective-permute-start.20 = (bf16[512,256]{1,0:T(8,128)(2,1)S(1)}, bf16[512,256]{1,0:T(8,128)(2,1)S(1)}, u32[]{:S(2)}, u32[]{:S(2)}) collective-permute-start(bf16[512,256]{1,0:T(8,128)(2,1)S(1)} %join.1.refs_1_.refs_0_), channel_id=1, source_target_pairs={{0,32},{16,48},{32,64},{48,80},{64,96},{80,112},{96,0},{112,16},{1... | collective-permute-start | bytes 786440 | tf_op jit(solution)/shard_map/ppermute | solution.py:50
  58.4 13.5 %collective-permute-start.15 = (bf16[256,1024]{1,0:T(8,128)(2,1)S(1)}, bf16[256,1024]{1,0:T(8,128)(2,1)S(1)}, u32[]{:S(2)}, u32[]{:S(2)}) collective-permute-start(bf16[256,1024]{1,0:T(8,128)(2,1)S(1)} %phase.13.refs_7_.refs_3_), channel_id=1, source_target_pairs={{0,4},{1,13},{2,6},{3,15},{4,8},{5,1},{6,10},{7,3},{8,12},{9,5},{1... | collective-permute-start | bytes 1572872 | tf_op jit(solution)/shard_map/ppermute | solution.py:31
  65.1 6.7 %collective-permute-start.19 = (bf16[512,256]{1,0:T(8,128)(2,1)S(1)}, bf16[512,256]{1,0:T(8,128)(2,1)S(1)}, u32[]{:S(2)}, u32[]{:S(2)}) collective-permute-start(bf16[512,256]{1,0:T(8,128)(2,1)S(1)} %phase.14.refs_8_.refs_0_), channel_id=1, source_target_pairs={{0,64},{16,80},{32,96},{48,112},{64,0},{80,16},{96,32},{112,48},{1... | collective-permute-start | bytes 786440 | tf_op jit(solution)/shard_map/ppermute | solution.py:50
  71.8 9.4 %collective-permute-start.22 = (bf16[768,1024]{1,0:T(8,128)(2,1)S(1)}, bf16[768,1024]{1,0:T(8,128)(2,1)S(1)}, u32[]{:S(2)}, u32[]{:S(2)}) collective-permute-start(bf16[768,1024]{1,0:T(8,128)(2,1)S(1)} %get-tuple-element.70), channel_id=1, source_target_pairs={{0,1},{1,0},{2,3},{3,2},{4,5},{5,4},{6,7},{7,6},{8,9},{9,8},{10,11... | collective-permute-start | bytes 4718600 | tf_op jit(solution)/shard_map/ppermute | solution.py:41
  77.4 3.8 %collective-permute-start.21 = (bf16[256,1024]{1,0:T(8,128)(2,1)S(1)}, bf16[256,1024]{1,0:T(8,128)(2,1)S(1)}, u32[]{:S(2)}, u32[]{:S(2)}) collective-permute-start(bf16[256,1024]{1,0:T(8,128)(2,1)S(1)} %get-tuple-element.68.refs_1_), channel_id=1, source_target_pairs={{0,1},{1,0},{2,3},{3,2},{4,5},{5,4},{6,7},{7,6},{8,9},{9,8},{10,11... | collective-permute-start | bytes 1572872 | tf_op jit(solution)/shard_map/ppermute | solution.py:41

commit v6 on v5

--- a/solution.py
+++ b/solution.py
@@ -357,16 +357,17 @@
     new_ref[...] = rounded(updated).astype(jnp.bfloat16)
 
 
-def join_kernel(left_ref, right_ref, out_ref):
+def join_kernel(left_ref, right_ref, out_ref, copy_ref):
     width = left_ref.shape[1]
-    out_ref[:, :width] = left_ref[...]
-    out_ref[:, width:] = right_ref[...]
-
-
-def join(left, right, after=()):
+    for ref in (out_ref, copy_ref):
+        ref[:, :width] = left_ref[...]
+        ref[:, width:] = right_ref[...]
+
+
+def join(left, right):
     rows, columns = left.shape
     out = jax.ShapeDtypeStruct((rows, 2 * columns), left.dtype)
-    return whole(join_kernel, out, "join", [left, right], after=after)
+    return whole(join_kernel, [out, out], "join", [left, right])
 
 
 def assemble_kernel(*refs):
@@ -474,7 +475,7 @@
     high_3 = along_x(high_r3)
     high_1 = along_z(high_0)
     (new_other,) = phase([new_other], after=[high_r3, low_r3, high_2])
-    pair = join(new, new_other)
+    pair, pair_sent = join(new, new_other)
     pair_1 = across_replicas(pair, lambda y, x: (y - 1, x))
     pair_3 = across_replicas(pair, lambda y, x: (y + 1, x))
     (low_2,) = phase([low_2], after=[pair])
@@ -490,8 +491,8 @@
         after=[low_2],
         counted=False,
     )
-    (pair,) = phase([pair], after=[totals[0], pair_1])
-    pair_2 = across_replicas(pair, lambda y, x: (y + 2, x))
+    (pair_sent,) = phase([pair_sent], after=[totals[0], pair_1])
+    pair_2 = across_replicas(pair_sent, lambda y, x: (y + 2, x))
     own_total, other_total = project_on(
         totals,
         [
@@ -502,7 +503,7 @@
         ],
         last=True,
         counted=False,
-        after=[pair],
+        after=[pair_sent],
     )
     low_3, other_total, pair_2 = phase([low_3, other_total, pair_2], after=[pair_3])
 

time: 83.7 us -> 83.3 us (level)
  starting transfers between devices: 37.7 us -> 36 us
  waiting for transfers between devices: 15.4 us -> 16.6 us
    ppermute x3, starting transfers between devices: 7.18 us -> 3.36 us  [to_core(): return lax.ppermute(value, 'fsdp', fsdp_perm(lambda z, x, c: (z, x, 1 - c)))]
    ppermute x8, starting transfers between devices: 11.6 us -> 13.8 us  [across_replicas(): return lax.ppermute(value, 'replica', pairs)]
    ppermute x8, waiting for transfers between devices: 9.99 us -> 11.7 us  [across_replicas(): return lax.ppermute(value, 'replica', pairs)]
  transfers between devices with their start and end apart: 23 -> 23, of which waited for: 11 -> 10; matrix products, arithmetic and copies ran while one was open for 0% -> 0% of each run, Pallas kernels for 33% -> 33%
where the time goes in v6:
time: 83.3 us; the launch traced here: 83.1 us
  starting transfers between devices  36 us (43%)
  Pallas kernels  29.7 us (36%)
  waiting for transfers between devices  16.6 us (20%)
    pallas_call x4, Pallas kernels, project(): pl.pallas_call(functools.partial(project_kernel, places, rows, bool(total...  16.5 us
    ppermute x8, starting transfers between devices, across_replicas(): return lax.ppermute(value, 'replica', pairs)  13.8 us
    ppermute x8, waiting for transfers between devices, across_replicas(): return lax.ppermute(value, 'replica', pairs)  11.7 us
    ppermute x8, starting transfers between devices, along_z(): lax.ppermute(value, 'fsdp', fsdp_perm(lambda z, x, c: (z + 1 - 2 * c, x,...  10.1 us
    ppermute x4, starting transfers between devices, along_x(): return lax.ppermute(value, 'fsdp', fsdp_perm(lambda z, x, c: (z, 1 - x, c)))  8.78 us
    pallas_call x1, Pallas kernels, fetch(): pl.pallas_call(run, in_specs=[pl.BlockSpec(memory_space=pltpu.HBM)] + [pl...  4.92 us
    pallas_call x2, Pallas kernels, finish(): pl.pallas_call(functools.partial(finish_kernel, places, rows, len(totals)...  3.44 us
    ppermute x3, starting transfers between devices, to_core(): return lax.ppermute(value, 'fsdp', fsdp_perm(lambda z, x, c: (z, x, 1 - c)))  3.36 us
  transfers between devices with their start and end apart: 23, of which 10 were waited for; matrix products, arithmetic and copies ran while one was open for 0% of the time, Pallas kernels for 33%

profile of v6, /device:TPU:1, one launch (start us, length us, event | category | flops | bytes accessed | tf_op | source)
XLA Modules:
  0.0 83.1 jit_solution(649105590884836684)
XLA Ops:
  0.6 1.5 %collective-permute-start.6 = (bf16[1,768,8192]{2,1,0:T(8,128)(2,1)}, bf16[1,768,8192]{2,1,0:T(8,128)(2,1)S(1)}, u32[]{:S(2)}, u32[]{:S(2)}) collective-permute-start(bf16[1,768,8192]{2,1,0:T(8,128)(2,1)} %tokens_hbm.1), channel_id=1, source_target_pairs={{0,1},{1,0},{2,3},{3,2},{4,5},{5,4},{6,7},{7,6},{8,9},{9,8},{10,11... | collective-permute-start | bytes 37748744 | tf_op jit(solution)/shard_map/ppermute | solution.py:41
  2.1 1.6 %prepare.1 = (bf16[512,1024]{1,0:T(8,128)(2,1)S(1)}, bf16[256,1024]{1,0:T(8,128)(2,1)S(1)}, bf16[256,1024]{1,0:T(8,128)(2,1)S(1)}, bf16[512,256]{1,0:T(8,128)(2,...) custom-call(f32[1,8192]{1,0:T(1,128)} %gain_hbm.1, ...), custom_call_target="tpu_custom_call" | custom-call | flops 524288 | bytes 2097152 | tf_op jit(solution)/shard_map/prepare/pallas_call | solution.py:111
  3.8 3.9 %collective-permute-start = (bf16[512,1024]{1,0:T(8,128)(2,1)S(1)}, bf16[512,1024]{1,0:T(8,128)(2,1)S(1)}, u32[]{:S(2)}, u32[]{:S(2)}) collective-permute-start(bf16[512,1024]{1,0:T(8,128)(2,1)S(1)} %get-tuple-element.41.refs_0_.refs_2_), channel_id=1, source_target_pairs={{0,4},{1,13},{2,6},{3,15},{4,8},{5,1},{6,10},{7,3},{8,12},{9,5},{1... | collective-permute-start | bytes 3145736 | tf_op jit(solution)/shard_map/ppermute | solution.py:31
  7.7 2.7 %collective-permute-start.1 = (bf16[256,1024]{1,0:T(8,128)(2,1)S(1)}, bf16[256,1024]{1,0:T(8,128)(2,1)S(1)}, u32[]{:S(2)}, u32[]{:S(2)}) collective-permute-start(bf16[256,1024]{1,0:T(8,128)(2,1)S(1)} %get-tuple-element.43), channel_id=1, source_target_pairs={{0,2},{1,3},{2,0},{3,1},{4,6},{5,7},{6,4},{7,5},{8,10},{9,11},{10,... | collective-permute-start | bytes 1572872 | tf_op jit(solution)/shard_map/ppermute | solution.py:37
  10.4 1.3 %collective-permute-start.2 = (bf16[512,256]{1,0:T(8,128)(2,1)S(1)}, bf16[512,256]{1,0:T(8,128)(2,1)S(1)}, u32[]{:S(2)}, u32[]{:S(2)}) collective-permute-start(bf16[512,256]{1,0:T(8,128)(2,1)S(1)} %get-tuple-element.47), channel_id=1, source_target_pairs={{0,32},{16,48},{32,64},{48,80},{64,96},{80,112},{96,0},{112,16},{1... | collective-permute-start | bytes 786440 | tf_op jit(solution)/shard_map/ppermute | solution.py:50
  11.7 1.4 %collective-permute-start.3 = (bf16[512,256]{1,0:T(8,128)(2,1)S(1)}, bf16[512,256]{1,0:T(8,128)(2,1)S(1)}, u32[]{:S(2)}, u32[]{:S(2)}) collective-permute-start(bf16[512,256]{1,0:T(8,128)(2,1)S(1)} %get-tuple-element.48), channel_id=1, source_target_pairs={{0,96},{16,112},{32,0},{48,16},{64,32},{80,48},{96,64},{112,80},{1... | collective-permute-start | bytes 786440 | tf_op jit(solution)/shard_map/ppermute | solution.py:50
  13.1 4.9 %load.1 = (bf16[1,768,8192]{2,1,0:T(8,128)(2,1)S(1)}, f32[768,128]{1,0:T(8,128)S(1)}) custom-call(bf16[1,768,8192]{2,1,0:T(8,128)(2,1)} %tokens_hbm.1, bf16[512,1024]{1,0:T(8,128)(2,1)S(1)} %get-tuple-element.41.refs_0_.refs_2_), custom_call_target="tpu_custom_call" | custom-call | flops 6291456 | bytes 12582912 | tf_op jit(solution)/shard_map/load/pallas_call | solution.py:179
  18.1 0.8 collective-permute-done.2.refs_5_.refs_2_
  18.9 0.4 collective-permute-done.3.refs_6_.refs_4_
  19.2 2.2 %collective-permute-done.1.refs_1_ = bf16[256,1024]{1,0:T(8,128)(2,1)S(1)} collective-permute-done((bf16[256,1024]{1,0:T(8,128)(2,1)S(1)}, bf16[256,1024]{1,0:T(8,128)(2,1)S(1)}, u32[]{:S(2)}, u32[]{:S(2)}) %collective-permute-start.1) | collective-permute-done | bytes 524320 | tf_op jit(solution)/shard_map/ppermute | solution.py:37
  21.5 1.4 %collective-permute-start.8 = (bf16[512,1024]{1,0:T(8,128)(2,1)S(1)}, bf16[512,1024]{1,0:T(8,128)(2,1)S(1)}, u32[]{:S(2)}, u32[]{:S(2)}) collective-permute-start(bf16[512,1024]{1,0:T(8,128)(2,1)S(1)} %get-tuple-element.52.refs_3_), channel_id=1, source_target_pairs={{0,4},{1,13},{2,6},{3,15},{4,8},{5,1},{6,10},{7,3},{8,12},{9,5},{1... | collective-permute-start | bytes 3145736 | tf_op jit(solution)/shard_map/ppermute | solution.py:31
  22.9 2.7 %collective-permute-start.9 = (bf16[256,1024]{1,0:T(8,128)(2,1)S(1)}, bf16[256,1024]{1,0:T(8,128)(2,1)S(1)}, u32[]{:S(2)}, u32[]{:S(2)}) collective-permute-start(bf16[256,1024]{1,0:T(8,128)(2,1)S(1)} %get-tuple-element.55), channel_id=1, source_target_pairs={{0,2},{1,3},{2,0},{3,1},{4,6},{5,7},{6,4},{7,5},{8,10},{9,11},{10,... | collective-permute-start | bytes 1572872 | tf_op jit(solution)/shard_map/ppermute | solution.py:37
  25.6 2.9 %collective-permute-start.5 = (bf16[512,256]{1,0:T(8,128)(2,1)S(1)}, bf16[512,256]{1,0:T(8,128)(2,1)S(1)}, u32[]{:S(2)}, u32[]{:S(2)}) collective-permute-start(bf16[512,256]{1,0:T(8,128)(2,1)S(1)} %get-tuple-element.51), channel_id=1, source_target_pairs={{0,64},{16,80},{32,96},{48,112},{64,0},{80,16},{96,32},{112,48},{1... | collective-permute-start | bytes 786440 | tf_op jit(solution)/shard_map/ppermute | solution.py:50
  28.5 0.1 collective-permute-start.4
  28.6 0.0 collective-permute-done.6.refs_1_
  28.6 4.0 %project.4 = (f32[768,1024]{1,0:T(8,128)S(1)}, f32[768,1024]{1,0:T(8,128)S(1)}) custom-call(bf16[1,768,8192]{2,1,0:T(8,128)(2,1)S(1)} %get-tuple-element.42.refs_0_, bf16[1,768,8192]{2,1,0:T(8,128)(2,1)S(1)} %collective-permute-done.6.refs_1_, bf16[512,1024]{1,0:T(8,128)(2,1)S(1)} %get-tuple-element.41.refs_0_.refs_2_, ...), custom_call_target="tpu_custom_call" | custom-call | flops 3221225472 | bytes 2097152 | tf_op jit(solution)/shard_map/project/pallas_call | solution.py:240
  32.6 2.5 %collective-permute-done.5.refs_3_ = bf16[512,256]{1,0:T(8,128)(2,1)S(1)} collective-permute-done((bf16[512,256]{1,0:T(8,128)(2,1)S(1)}, bf16[512,256]{1,0:T(8,128)(2,1)S(1)}, u32[]{:S(2)}, u32[]{:S(2)}) %collective-permute-start.5) | collective-permute-done | bytes 262176 | tf_op jit(solution)/shard_map/ppermute | solution.py:50
  35.1 1.1 %partial.1 = (f32[512,128]{1,0:T(8,128)S(1)}, bf16[512,128]{1,0:T(8,128)(2,1)S(1)}) custom-call(f32[512,1024]{1,0:T(8,128)S(1)} %copy-done, bf16[512,256]{1,0:T(8,128)(2,1)S(1)} %get-tuple-element.50.refs_1_, bf16[512,256]{1,0:T(8,128)(2,1)S(1)} %collective-permute-done.2.refs_5_.refs_2_, bf16[512,256]{1,0:T(8,128)(2,1)S(1)} %collective-permute-done.5.refs_3_, ...), custom_call_target="tpu_custom_call" | custom-call | flops 25165824 | bytes 6291456 | tf_op jit(solution)/shard_map/partial/pallas_call | solution.py:394
  36.2 0.0 copy-start.1
  36.2 0.1 collective-permute-start.7
  36.3 1.0 %collective-permute-done.9.refs_1_ = bf16[256,1024]{1,0:T(8,128)(2,1)S(1)} collective-permute-done((bf16[256,1024]{1,0:T(8,128)(2,1)S(1)}, bf16[256,1024]{1,0:T(8,128)(2,1)S(1)}, u32[]{:S(2)}, u32[]{:S(2)}) %collective-permute-start.9) | collective-permute-done | bytes 524320 | tf_op jit(solution)/shard_map/ppermute | solution.py:37
  37.4 0.1 fusion
  37.5 0.7 collective-permute-start.12
  38.2 0.1 collective-permute-start.13
  38.2 2.6 %collective-permute-start.14 = (bf16[256,1024]{1,0:T(8,128)(2,1)S(1)}, bf16[256,1024]{1,0:T(8,128)(2,1)S(1)}, u32[]{:S(2)}, u32[]{:S(2)}) collective-permute-start(bf16[256,1024]{1,0:T(8,128)(2,1)S(1)} %get-tuple-element.80), channel_id=1, source_target_pairs={{0,2},{1,3},{2,0},{3,1},{4,6},{5,7},{6,4},{7,5},{8,10},{9,11},{10,... | collective-permute-start | bytes 1572872 | tf_op jit(solution)/shard_map/ppermute | solution.py:37
  40.8 0.2 collective-permute-done.4.refs_0_
  41.0 0.2 collective-permute-done.7.refs_1_
  41.3 2.1 %collective-permute-start.10 = (bf16[256,1024]{1,0:T(8,128)(2,1)S(1)}, bf16[256,1024]{1,0:T(8,128)(2,1)S(1)}, u32[]{:S(2)}, u32[]{:S(2)}) collective-permute-start(bf16[256,1024]{1,0:T(8,128)(2,1)S(1)} %get-tuple-element.58.refs_4_), channel_id=1, source_target_pairs={{0,4},{1,13},{2,6},{3,15},{4,8},{5,1},{6,10},{7,3},{8,12},{9,5},{1... | collective-permute-start | bytes 1572872 | tf_op jit(solution)/shard_map/ppermute | solution.py:31
  43.3 0.8 update.1
  44.1 1.2 %collective-permute-start.11 = (bf16[512,128]{1,0:T(8,128)(2,1)S(1)}, bf16[512,128]{1,0:T(8,128)(2,1)S(1)}, u32[]{:S(2)}, u32[]{:S(2)}) collective-permute-start(bf16[512,128]{1,0:T(8,128)(2,1)S(1)} %get-tuple-element.60.refs_7_.refs_0_), channel_id=1, source_target_pairs={{0,16},{16,0},{32,48},{48,32},{64,80},{80,64},{96,112},{112,96},{1... | collective-permute-start | bytes 393224 | tf_op jit(solution)/shard_map/ppermute | solution.py:50
  45.3 4.5 %project.5 = (f32[768,1024]{1,0:T(8,128)S(1)}, f32[768,1024]{1,0:T(8,128)S(1)}) custom-call(bf16[1,768,8192]{2,1,0:T(8,128)(2,1)S(1)} %get-tuple-element.42.refs_0_, bf16[1,768,8192]{2,1,0:T(8,128)(2,1)S(1)} %collective-permute-done.6.refs_1_, bf16[512,1024]{1,0:T(8,128)(2,1)S(1)} %get-tuple-element.57.refs_2_, ...), custom_call_target="tpu_custom_call", output_to_operand_aliasing={{0}: (5, {}), {1}: (6, {})} | custom-call | flops 1 | bytes 1 | tf_op jit(solution)/shard_map/project/pallas_call | solution.py:240
  49.9 0.1 collective-permute-start.16
  49.9 4.9 %collective-permute-done.11.refs_0_ = bf16[512,128]{1,0:T(8,128)(2,1)S(1)} collective-permute-done((bf16[512,128]{1,0:T(8,128)(2,1)S(1)}, bf16[512,128]{1,0:T(8,128)(2,1)S(1)}, u32[]{:S(2)}, u32[]{:S(2)}) %collective-permute-start.11) | collective-permute-done | bytes 131104 | tf_op jit(solution)/shard_map/ppermute | solution.py:50
  54.8 0.7 collective-permute-start.17
  55.5 0.1 join.1
  55.6 2.8 %collective-permute-start.18 = (bf16[512,256]{1,0:T(8,128)(2,1)S(1)}, bf16[512,256]{1,0:T(8,128)(2,1)S(1)}, u32[]{:S(2)}, u32[]{:S(2)}) collective-permute-start(bf16[512,256]{1,0:T(8,128)(2,1)S(1)} %get-tuple-element.65.refs_1_.refs_0_), channel_id=1, source_target_pairs={{0,96},{16,112},{32,0},{48,16},{64,32},{80,48},{96,64},{112,80},{1... | collective-permute-start | bytes 786440 | tf_op jit(solution)/shard_map/ppermute | solution.py:50
  58.4 1.8 %collective-permute-start.15 = (bf16[256,1024]{1,0:T(8,128)(2,1)S(1)}, bf16[256,1024]{1,0:T(8,128)(2,1)S(1)}, u32[]{:S(2)}, u32[]{:S(2)}) collective-permute-start(bf16[256,1024]{1,0:T(8,128)(2,1)S(1)} %phase.13.refs_7_.refs_3_), channel_id=1, source_target_pairs={{0,4},{1,13},{2,6},{3,15},{4,8},{5,1},{6,10},{7,3},{8,12},{9,5},{1... | collective-permute-start | bytes 1572872 | tf_op jit(solution)/shard_map/ppermute | solution.py:31
  60.2 1.3 %collective-permute-start.20 = (bf16[512,256]{1,0:T(8,128)(2,1)S(1)}, bf16[512,256]{1,0:T(8,128)(2,1)S(1)}, u32[]{:S(2)}, u32[]{:S(2)}) collective-permute-start(bf16[512,256]{1,0:T(8,128)(2,1)S(1)} %get-tuple-element.65.refs_1_.refs_0_), channel_id=1, source_target_pairs={{0,32},{16,48},{32,64},{48,80},{64,96},{80,112},{96,0},{112,16},{1... | collective-permute-start | bytes 786440 | tf_op jit(solution)/shard_map/ppermute | solution.py:50
  61.5 3.7 %project.6 = (f32[768,1024]{1,0:T(8,128)S(1)}, f32[768,1024]{1,0:T(8,128)S(1)}) custom-call(bf16[1,768,8192]{2,1,0:T(8,128)(2,1)S(1)} %get-tuple-element.42.refs_0_, bf16[1,768,8192]{2,1,0:T(8,128)(2,1)S(1)} %collective-permute-done.6.refs_1_, bf16[256,1024]{1,0:T(8,128)(2,1)S(1)} %collective-permute-done.13.refs_2_, ...), custom_call_target="tpu_custom_call", output_to_operand_aliasing={{0}: (5, {}), {1}: (6, {})} | custom-call | flops 1 | bytes 1 | tf_op jit(solution)/shard_map/project/pallas_call | solution.py:240
  65.2 2.7 %collective-permute-start.19 = (bf16[512,256]{1,0:T(8,128)(2,1)S(1)}, bf16[512,256]{1,0:T(8,128)(2,1)S(1)}, u32[]{:S(2)}, u32[]{:S(2)}) collective-permute-start(bf16[512,256]{1,0:T(8,128)(2,1)S(1)} %phase.14.refs_8_), channel_id=1, source_target_pairs={{0,64},{16,80},{32,96},{48,112},{64,0},{80,16},{96,32},{112,48},{1... | collective-permute-start | bytes 786440 | tf_op jit(solution)/shard_map/ppermute | solution.py:50
  67.9 4.3 %project.7 = (f32[768,1024]{1,0:T(8,128)S(1)}, bf16[768,1024]{1,0:T(8,128)(2,1)S(1)}) custom-call(bf16[1,768,8192]{2,1,0:T(8,128)(2,1)S(1)} %get-tuple-element.42.refs_0_, bf16[1,768,8192]{2,1,0:T(8,128)(2,1)S(1)} %collective-permute-done.6.refs_1_, bf16[256,1024]{1,0:T(8,128)(2,1)S(1)} %collective-permute-done.14.refs_3_.refs_2_, ...), custom_call_target="tpu_custom_call", output_to_operand_aliasing={{0}: (6, {})} | custom-call | flops 1 | bytes 1 | tf_op jit(solution)/shard_map/project/pallas_call | solution.py:240
  72.2 3.0 %collective-permute-done.19.refs_2_ = bf16[512,256]{1,0:T(8,128)(2,1)S(1)} collective-permute-done((bf16[512,256]{1,0:T(8,128)(2,1)S(1)}, bf16[512,256]{1,0:T(8,128)(2,1)S(1)}, u32[]{:S(2)}, u32[]{:S(2)}) %collective-permute-start.19) | collective-permute-done | bytes 262176 | tf_op jit(solution)/shard_map/ppermute | solution.py:50
  75.2 1.8 %collective-permute-start.22 = (bf16[768,1024]{1,0:T(8,128)(2,1)S(1)}, bf16[768,1024]{1,0:T(8,128)(2,1)S(1)}, u32[]{:S(2)}, u32[]{:S(2)}) collective-permute-start(bf16[768,1024]{1,0:T(8,128)(2,1)S(1)} %get-tuple-element.74), channel_id=1, source_target_pairs={{0,1},{1,0},{2,3},{3,2},{4,5},{5,4},{6,7},{7,6},{8,9},{9,8},{10,11... | collective-permute-start | bytes 4718600 | tf_op jit(solution)/shard_map/ppermute | solution.py:41
  77.0 0.1 collective-permute-start.21
  77.1 1.1 %finish.2.refs_4_.refs_2_ = f32[768,1024]{1,0:T(8,128)S(1)} custom-call(bf16[1,768,8192]{2,1,0:T(8,128)(2,1)S(1)} %get-tuple-element.42.refs_0_, bf16[256,1024]{1,0:T(8,128)(2,1)S(1)} %get-tuple-element.72.refs_1_, f32[768,1024]{1,0:T(8,128)S(1)} %get-tuple-element.73.refs_2_), custom_call_target="tpu_custom_call", output_to_operand_aliasing={{}: (2, {})} | custom-call | flops 402653184 | bytes 524288 | tf_op jit(solution)/shard_map/finish/pallas_call | solution.py:308
  78.2 1.3 %assemble.1 = (bf16[512,1024]{1,0:T(8,128)(2,1)}, f32[8,128]{1,0:T(8,128)S(1)}) custom-call(bf16[512,256]{1,0:T(8,128)(2,1)S(1)} %get-tuple-element.65.refs_1_.refs_0_, bf16[512,256]{1,0:T(8,128)(2,1)S(1)} %collective-permute-done.18.refs_2_.refs_1_, bf16[512,256]{1,0:T(8,128)(2,1)S(1)} %get-tuple-element.75.refs_2_, ...), custom_call_target="tpu_custom_call" | custom-call | flops 8388608 | bytes 2097152 | tf_op jit(solution)/shard_map/assemble/pallas_call | solution.py:394
  79.5 1.3 %collective-permute-done.21.refs_1_ = bf16[256,1024]{1,0:T(8,128)(2,1)S(1)} collective-permute-done((bf16[256,1024]{1,0:T(8,128)(2,1)S(1)}, bf16[256,1024]{1,0:T(8,128)(2,1)S(1)}, u32[]{:S(2)}, u32[]{:S(2)}) %collective-permute-start.21) | collective-permute-done | bytes 524320 | tf_op jit(solution)/shard_map/ppermute | solution.py:41
  80.8 2.4 %finish.3 = bf16[1,768,1024]{2,1,0:T(8,128)(2,1)} custom-call(bf16[1,768,8192]{2,1,0:T(8,128)(2,1)S(1)} %get-tuple-element.42.refs_0_, bf16[256,1024]{1,0:T(8,128)(2,1)S(1)} %collective-permute-done.21.refs_1_, f32[768,1024]{1,0:T(8,128)S(1)} %finish.2.refs_4_.refs_2_, bf16[768,1024]{1,0:T(8,128)(2,1)S(1)} %collective-permute-done.22.refs_3_, ...), custom_call_target="tpu_custom_call" | custom-call | flops 402653184 | bytes 524288 | tf_op jit(solution)/shard_map/finish/pallas_call | solution.py:308
  (23 shorter events, 0.0 us)
Async XLA Ops:
  0.6 28.0 %collective-permute-start.6 = (bf16[1,768,8192]{2,1,0:T(8,128)(2,1)}, bf16[1,768,8192]{2,1,0:T(8,128)(2,1)S(1)}, u32[]{:S(2)}, u32[]{:S(2)}) collective-permute-start(bf16[1,768,8192]{2,1,0:T(8,128)(2,1)} %tokens_hbm.1), channel_id=1, source_target_pairs={{0,1},{1,0},{2,3},{3,2},{4,5},{5,4},{6,7},{7,6},{8,9},{9,8},{10,11... | collective-permute-start | bytes 37748744 | tf_op jit(solution)/shard_map/ppermute | solution.py:41
  3.8 17.7 %collective-permute-start = (bf16[512,1024]{1,0:T(8,128)(2,1)S(1)}, bf16[512,1024]{1,0:T(8,128)(2,1)S(1)}, u32[]{:S(2)}, u32[]{:S(2)}) collective-permute-start(bf16[512,1024]{1,0:T(8,128)(2,1)S(1)} %get-tuple-element.41.refs_0_.refs_2_), channel_id=1, source_target_pairs={{0,4},{1,13},{2,6},{3,15},{4,8},{5,1},{6,10},{7,3},{8,12},{9,5},{1... | collective-permute-start | bytes 3145736 | tf_op jit(solution)/shard_map/ppermute | solution.py:31
  7.7 13.8 %collective-permute-start.1 = (bf16[256,1024]{1,0:T(8,128)(2,1)S(1)}, bf16[256,1024]{1,0:T(8,128)(2,1)S(1)}, u32[]{:S(2)}, u32[]{:S(2)}) collective-permute-start(bf16[256,1024]{1,0:T(8,128)(2,1)S(1)} %get-tuple-element.43), channel_id=1, source_target_pairs={{0,2},{1,3},{2,0},{3,1},{4,6},{5,7},{6,4},{7,5},{8,10},{9,11},{10,... | collective-permute-start | bytes 1572872 | tf_op jit(solution)/shard_map/ppermute | solution.py:37
  10.4 8.5 %collective-permute-start.2 = (bf16[512,256]{1,0:T(8,128)(2,1)S(1)}, bf16[512,256]{1,0:T(8,128)(2,1)S(1)}, u32[]{:S(2)}, u32[]{:S(2)}) collective-permute-start(bf16[512,256]{1,0:T(8,128)(2,1)S(1)} %get-tuple-element.47), channel_id=1, source_target_pairs={{0,32},{16,48},{32,64},{48,80},{64,96},{80,112},{96,0},{112,16},{1... | collective-permute-start | bytes 786440 | tf_op jit(solution)/shard_map/ppermute | solution.py:50
  11.7 7.5 %collective-permute-start.3 = (bf16[512,256]{1,0:T(8,128)(2,1)S(1)}, bf16[512,256]{1,0:T(8,128)(2,1)S(1)}, u32[]{:S(2)}, u32[]{:S(2)}) collective-permute-start(bf16[512,256]{1,0:T(8,128)(2,1)S(1)} %get-tuple-element.48), channel_id=1, source_target_pairs={{0,96},{16,112},{32,0},{48,16},{64,32},{80,48},{96,64},{112,80},{1... | collective-permute-start | bytes 786440 | tf_op jit(solution)/shard_map/ppermute | solution.py:50
  21.5 15.9 %collective-permute-start.8 = (bf16[512,1024]{1,0:T(8,128)(2,1)S(1)}, bf16[512,1024]{1,0:T(8,128)(2,1)S(1)}, u32[]{:S(2)}, u32[]{:S(2)}) collective-permute-start(bf16[512,1024]{1,0:T(8,128)(2,1)S(1)} %get-tuple-element.52.refs_3_), channel_id=1, source_target_pairs={{0,4},{1,13},{2,6},{3,15},{4,8},{5,1},{6,10},{7,3},{8,12},{9,5},{1... | collective-permute-start | bytes 3145736 | tf_op jit(solution)/shard_map/ppermute | solution.py:31
  22.9 14.5 %collective-permute-start.9 = (bf16[256,1024]{1,0:T(8,128)(2,1)S(1)}, bf16[256,1024]{1,0:T(8,128)(2,1)S(1)}, u32[]{:S(2)}, u32[]{:S(2)}) collective-permute-start(bf16[256,1024]{1,0:T(8,128)(2,1)S(1)} %get-tuple-element.55), channel_id=1, source_target_pairs={{0,2},{1,3},{2,0},{3,1},{4,6},{5,7},{6,4},{7,5},{8,10},{9,11},{10,... | collective-permute-start | bytes 1572872 | tf_op jit(solution)/shard_map/ppermute | solution.py:37
  25.6 9.5 %collective-permute-start.5 = (bf16[512,256]{1,0:T(8,128)(2,1)S(1)}, bf16[512,256]{1,0:T(8,128)(2,1)S(1)}, u32[]{:S(2)}, u32[]{:S(2)}) collective-permute-start(bf16[512,256]{1,0:T(8,128)(2,1)S(1)} %get-tuple-element.51), channel_id=1, source_target_pairs={{0,64},{16,80},{32,96},{48,112},{64,0},{80,16},{96,32},{112,48},{1... | collective-permute-start | bytes 786440 | tf_op jit(solution)/shard_map/ppermute | solution.py:50
  28.5 12.5 %collective-permute-start.4 = (bf16[256,1024]{1,0:T(8,128)(2,1)S(1)}, bf16[256,1024]{1,0:T(8,128)(2,1)S(1)}, u32[]{:S(2)}, u32[]{:S(2)}) collective-permute-start(bf16[256,1024]{1,0:T(8,128)(2,1)S(1)} %get-tuple-element.49.refs_3_), channel_id=1, source_target_pairs={{0,4},{1,13},{2,6},{3,15},{4,8},{5,1},{6,10},{7,3},{8,12},{9,5},{1... | collective-permute-start | bytes 1572872 | tf_op jit(solution)/shard_map/ppermute | solution.py:31
  28.6 6.5 %copy-start = (f32[512,1024]{1,0:T(8,128)S(1)}, f32[512,1024]{1,0:T(8,128)}, u32[]{:S(2)}) copy-start(f32[512,1024]{1,0:T(8,128)} %refs_0_.3) | copy-start | bytes 6291460
  36.2 7.1 %copy-start.1 = (bf16[512,128]{1,0:T(8,128)(2,1)S(1)}, bf16[512,128]{1,0:T(8,128)(2,1)}, u32[]{:S(2)}) copy-start(bf16[512,128]{1,0:T(8,128)(2,1)} %refs_1_.1) | copy-start | bytes 393220
  36.2 5.0 %collective-permute-start.7 = (bf16[512,128]{1,0:T(8,128)(2,1)S(1)}, bf16[512,128]{1,0:T(8,128)(2,1)S(1)}, u32[]{:S(2)}, u32[]{:S(2)}) collective-permute-start(bf16[512,128]{1,0:T(8,128)(2,1)S(1)} %get-tuple-element.54), channel_id=1, source_target_pairs={{0,16},{16,0},{32,48},{48,32},{64,80},{80,64},{96,112},{112,96},{1... | collective-permute-start | bytes 393224 | tf_op jit(solution)/shard_map/ppermute | solution.py:50
  37.5 12.4 %collective-permute-start.12 = (bf16[256,1024]{1,0:T(8,128)(2,1)S(1)}, bf16[256,1024]{1,0:T(8,128)(2,1)S(1)}, u32[]{:S(2)}, u32[]{:S(2)}) collective-permute-start(bf16[256,1024]{1,0:T(8,128)(2,1)S(1)} %get-tuple-element.80), channel_id=1, source_target_pairs={{0,4},{1,13},{2,6},{3,15},{4,8},{5,1},{6,10},{7,3},{8,12},{9,5},{1... | collective-permute-start | bytes 1572872 | tf_op jit(solution)/shard_map/ppermute | solution.py:31
  38.2 17.4 %collective-permute-start.13 = (bf16[256,1024]{1,0:T(8,128)(2,1)S(1)}, bf16[256,1024]{1,0:T(8,128)(2,1)S(1)}, u32[]{:S(2)}, u32[]{:S(2)}) collective-permute-start(bf16[256,1024]{1,0:T(8,128)(2,1)S(1)} %get-tuple-element.79), channel_id=1, source_target_pairs={{0,4},{1,13},{2,6},{3,15},{4,8},{5,1},{6,10},{7,3},{8,12},{9,5},{1... | collective-permute-start | bytes 1572872 | tf_op jit(solution)/shard_map/ppermute | solution.py:31
  38.2 17.3 %collective-permute-start.14 = (bf16[256,1024]{1,0:T(8,128)(2,1)S(1)}, bf16[256,1024]{1,0:T(8,128)(2,1)S(1)}, u32[]{:S(2)}, u32[]{:S(2)}) collective-permute-start(bf16[256,1024]{1,0:T(8,128)(2,1)S(1)} %get-tuple-element.80), channel_id=1, source_target_pairs={{0,2},{1,3},{2,0},{3,1},{4,6},{5,7},{6,4},{7,5},{8,10},{9,11},{10,... | collective-permute-start | bytes 1572872 | tf_op jit(solution)/shard_map/ppermute | solution.py:37
  41.3 17.1 %collective-permute-start.10 = (bf16[256,1024]{1,0:T(8,128)(2,1)S(1)}, bf16[256,1024]{1,0:T(8,128)(2,1)S(1)}, u32[]{:S(2)}, u32[]{:S(2)}) collective-permute-start(bf16[256,1024]{1,0:T(8,128)(2,1)S(1)} %get-tuple-element.58.refs_4_), channel_id=1, source_target_pairs={{0,4},{1,13},{2,6},{3,15},{4,8},{5,1},{6,10},{7,3},{8,12},{9,5},{1... | collective-permute-start | bytes 1572872 | tf_op jit(solution)/shard_map/ppermute | solution.py:31
  44.1 10.7 %collective-permute-start.11 = (bf16[512,128]{1,0:T(8,128)(2,1)S(1)}, bf16[512,128]{1,0:T(8,128)(2,1)S(1)}, u32[]{:S(2)}, u32[]{:S(2)}) collective-permute-start(bf16[512,128]{1,0:T(8,128)(2,1)S(1)} %get-tuple-element.60.refs_7_.refs_0_), channel_id=1, source_target_pairs={{0,16},{16,0},{32,48},{48,32},{64,80},{80,64},{96,112},{112,96},{1... | collective-permute-start | bytes 393224 | tf_op jit(solution)/shard_map/ppermute | solution.py:50
  49.9 18.1 %collective-permute-start.16 = (bf16[256,1024]{1,0:T(8,128)(2,1)S(1)}, bf16[256,1024]{1,0:T(8,128)(2,1)S(1)}, u32[]{:S(2)}, u32[]{:S(2)}) collective-permute-start(bf16[256,1024]{1,0:T(8,128)(2,1)S(1)} %get-tuple-element.66), channel_id=1, source_target_pairs={{0,4},{1,13},{2,6},{3,15},{4,8},{5,1},{6,10},{7,3},{8,12},{9,5},{1... | collective-permute-start | bytes 1572872 | tf_op jit(solution)/shard_map/ppermute | solution.py:31
  54.8 13.1 %collective-permute-start.17 = (bf16[256,1024]{1,0:T(8,128)(2,1)S(1)}, bf16[256,1024]{1,0:T(8,128)(2,1)S(1)}, u32[]{:S(2)}, u32[]{:S(2)}) collective-permute-start(bf16[256,1024]{1,0:T(8,128)(2,1)S(1)} %get-tuple-element.64.refs_1_.refs_3_), channel_id=1, source_target_pairs={{0,2},{1,3},{2,0},{3,1},{4,6},{5,7},{6,4},{7,5},{8,10},{9,11},{10,... | collective-permute-start | bytes 1572872 | tf_op jit(solution)/shard_map/ppermute | solution.py:37
  55.6 9.6 %collective-permute-start.18 = (bf16[512,256]{1,0:T(8,128)(2,1)S(1)}, bf16[512,256]{1,0:T(8,128)(2,1)S(1)}, u32[]{:S(2)}, u32[]{:S(2)}) collective-permute-start(bf16[512,256]{1,0:T(8,128)(2,1)S(1)} %get-tuple-element.65.refs_1_.refs_0_), channel_id=1, source_target_pairs={{0,96},{16,112},{32,0},{48,16},{64,32},{80,48},{96,64},{112,80},{1... | collective-permute-start | bytes 786440 | tf_op jit(solution)/shard_map/ppermute | solution.py:50
  58.4 16.8 %collective-permute-start.15 = (bf16[256,1024]{1,0:T(8,128)(2,1)S(1)}, bf16[256,1024]{1,0:T(8,128)(2,1)S(1)}, u32[]{:S(2)}, u32[]{:S(2)}) collective-permute-start(bf16[256,1024]{1,0:T(8,128)(2,1)S(1)} %phase.13.refs_7_.refs_3_), channel_id=1, source_target_pairs={{0,4},{1,13},{2,6},{3,15},{4,8},{5,1},{6,10},{7,3},{8,12},{9,5},{1... | collective-permute-start | bytes 1572872 | tf_op jit(solution)/shard_map/ppermute | solution.py:31
  60.2 12.0 %collective-permute-start.20 = (bf16[512,256]{1,0:T(8,128)(2,1)S(1)}, bf16[512,256]{1,0:T(8,128)(2,1)S(1)}, u32[]{:S(2)}, u32[]{:S(2)}) collective-permute-start(bf16[512,256]{1,0:T(8,128)(2,1)S(1)} %get-tuple-element.65.refs_1_.refs_0_), channel_id=1, source_target_pairs={{0,32},{16,48},{32,64},{48,80},{64,96},{80,112},{96,0},{112,16},{1... | collective-permute-start | bytes 786440 | tf_op jit(solution)/shard_map/ppermute | solution.py:50
  65.2 10.0 %collective-permute-start.19 = (bf16[512,256]{1,0:T(8,128)(2,1)S(1)}, bf16[512,256]{1,0:T(8,128)(2,1)S(1)}, u32[]{:S(2)}, u32[]{:S(2)}) collective-permute-start(bf16[512,256]{1,0:T(8,128)(2,1)S(1)} %phase.14.refs_8_), channel_id=1, source_target_pairs={{0,64},{16,80},{32,96},{48,112},{64,0},{80,16},{96,32},{112,48},{1... | collective-permute-start | bytes 786440 | tf_op jit(solution)/shard_map/ppermute | solution.py:50
  75.2 5.6 %collective-permute-start.22 = (bf16[768,1024]{1,0:T(8,128)(2,1)S(1)}, bf16[768,1024]{1,0:T(8,128)(2,1)S(1)}, u32[]{:S(2)}, u32[]{:S(2)}) collective-permute-start(bf16[768,1024]{1,0:T(8,128)(2,1)S(1)} %get-tuple-element.74), channel_id=1, source_target_pairs={{0,1},{1,0},{2,3},{3,2},{4,5},{5,4},{6,7},{7,6},{8,9},{9,8},{10,11... | collective-permute-start | bytes 4718600 | tf_op jit(solution)/shard_map/ppermute | solution.py:41
  77.0 3.8 %collective-permute-start.21 = (bf16[256,1024]{1,0:T(8,128)(2,1)S(1)}, bf16[256,1024]{1,0:T(8,128)(2,1)S(1)}, u32[]{:S(2)}, u32[]{:S(2)}) collective-permute-start(bf16[256,1024]{1,0:T(8,128)(2,1)S(1)} %get-tuple-element.72.refs_1_), channel_id=1, source_target_pairs={{0,1},{1,0},{2,3},{3,2},{4,5},{5,4},{6,7},{7,6},{8,9},{9,8},{10,11... | collective-permute-start | bytes 1572872 | tf_op jit(solution)/shard_map/ppermute | solution.py:41

commit v7 on v6

--- a/solution.py
+++ b/solution.py
@@ -269,7 +269,7 @@
         core = (c + dc) % 2
         shard = ((z + (2 * core - 1) * step + Z) % Z) * 4 + ((x + dx) % 2) * 2 + core
         starts.append(pl.multiple_of(shard * rows + first, BLOCK))
-    tile = 256
+    tile = 512
 
     def column(n, carry):
         at = pl.ds(pl.multiple_of(n * tile, tile), tile)

time: 83.3 us -> 82.9 us (level)
  no operation moved by 1% of the time
where the time goes in v7:
time: 82.9 us; the launch traced here: 82.7 us
  starting transfers between devices  36 us (43%)
  Pallas kernels  29.1 us (35%)
  waiting for transfers between devices  16.7 us (20%)
    pallas_call x4, Pallas kernels, project(): pl.pallas_call(functools.partial(project_kernel, places, rows, bool(total...  16.5 us
    ppermute x8, starting transfers between devices, across_replicas(): return lax.ppermute(value, 'replica', pairs)  13.8 us
    ppermute x8, waiting for transfers between devices, across_replicas(): return lax.ppermute(value, 'replica', pairs)  11.7 us
    ppermute x8, starting transfers between devices, along_z(): lax.ppermute(value, 'fsdp', fsdp_perm(lambda z, x, c: (z + 1 - 2 * c, x,...  10.1 us
    ppermute x4, starting transfers between devices, along_x(): return lax.ppermute(value, 'fsdp', fsdp_perm(lambda z, x, c: (z, 1 - x, c)))  8.78 us
    pallas_call x1, Pallas kernels, fetch(): pl.pallas_call(run, in_specs=[pl.BlockSpec(memory_space=pltpu.HBM)] + [pl...  4.92 us
    ppermute x3, starting transfers between devices, to_core(): return lax.ppermute(value, 'fsdp', fsdp_perm(lambda z, x, c: (z, x, 1 - c)))  3.36 us
    ppermute x4, waiting for transfers between devices, along_x(): return lax.ppermute(value, 'fsdp', fsdp_perm(lambda z, x, c: (z, 1 - x, c)))  3.28 us
  transfers between devices with their start and end apart: 23, of which 10 were waited for; matrix products, arithmetic and copies ran while one was open for 0% of the time, Pallas kernels for 33%

profile of v7, /device:TPU:1, one launch (start us, length us, event | category | flops | bytes accessed | tf_op | source)
XLA Modules:
  0.0 82.7 jit_solution(3222512446304056736)
XLA Ops:
  0.6 1.5 %collective-permute-start.6 = (bf16[1,768,8192]{2,1,0:T(8,128)(2,1)}, bf16[1,768,8192]{2,1,0:T(8,128)(2,1)S(1)}, u32[]{:S(2)}, u32[]{:S(2)}) collective-permute-start(bf16[1,768,8192]{2,1,0:T(8,128)(2,1)} %tokens_hbm.1), channel_id=1, source_target_pairs={{0,1},{1,0},{2,3},{3,2},{4,5},{5,4},{6,7},{7,6},{8,9},{9,8},{10,11... | collective-permute-start | bytes 37748744 | tf_op jit(solution)/shard_map/ppermute | solution.py:41
  2.1 1.6 %prepare.1 = (bf16[512,1024]{1,0:T(8,128)(2,1)S(1)}, bf16[256,1024]{1,0:T(8,128)(2,1)S(1)}, bf16[256,1024]{1,0:T(8,128)(2,1)S(1)}, bf16[512,256]{1,0:T(8,128)(2,...) custom-call(f32[1,8192]{1,0:T(1,128)} %gain_hbm.1, ...), custom_call_target="tpu_custom_call" | custom-call | flops 524288 | bytes 2097152 | tf_op jit(solution)/shard_map/prepare/pallas_call | solution.py:111
  3.8 3.9 %collective-permute-start = (bf16[512,1024]{1,0:T(8,128)(2,1)S(1)}, bf16[512,1024]{1,0:T(8,128)(2,1)S(1)}, u32[]{:S(2)}, u32[]{:S(2)}) collective-permute-start(bf16[512,1024]{1,0:T(8,128)(2,1)S(1)} %get-tuple-element.41.refs_0_.refs_2_), channel_id=1, source_target_pairs={{0,4},{1,13},{2,6},{3,15},{4,8},{5,1},{6,10},{7,3},{8,12},{9,5},{1... | collective-permute-start | bytes 3145736 | tf_op jit(solution)/shard_map/ppermute | solution.py:31
  7.7 2.7 %collective-permute-start.1 = (bf16[256,1024]{1,0:T(8,128)(2,1)S(1)}, bf16[256,1024]{1,0:T(8,128)(2,1)S(1)}, u32[]{:S(2)}, u32[]{:S(2)}) collective-permute-start(bf16[256,1024]{1,0:T(8,128)(2,1)S(1)} %get-tuple-element.43), channel_id=1, source_target_pairs={{0,2},{1,3},{2,0},{3,1},{4,6},{5,7},{6,4},{7,5},{8,10},{9,11},{10,... | collective-permute-start | bytes 1572872 | tf_op jit(solution)/shard_map/ppermute | solution.py:37
  10.4 1.3 %collective-permute-start.2 = (bf16[512,256]{1,0:T(8,128)(2,1)S(1)}, bf16[512,256]{1,0:T(8,128)(2,1)S(1)}, u32[]{:S(2)}, u32[]{:S(2)}) collective-permute-start(bf16[512,256]{1,0:T(8,128)(2,1)S(1)} %get-tuple-element.47), channel_id=1, source_target_pairs={{0,32},{16,48},{32,64},{48,80},{64,96},{80,112},{96,0},{112,16},{1... | collective-permute-start | bytes 786440 | tf_op jit(solution)/shard_map/ppermute | solution.py:50
  11.7 1.4 %collective-permute-start.3 = (bf16[512,256]{1,0:T(8,128)(2,1)S(1)}, bf16[512,256]{1,0:T(8,128)(2,1)S(1)}, u32[]{:S(2)}, u32[]{:S(2)}) collective-permute-start(bf16[512,256]{1,0:T(8,128)(2,1)S(1)} %get-tuple-element.48), channel_id=1, source_target_pairs={{0,96},{16,112},{32,0},{48,16},{64,32},{80,48},{96,64},{112,80},{1... | collective-permute-start | bytes 786440 | tf_op jit(solution)/shard_map/ppermute | solution.py:50
  13.1 4.9 %load.1 = (bf16[1,768,8192]{2,1,0:T(8,128)(2,1)S(1)}, f32[768,128]{1,0:T(8,128)S(1)}) custom-call(bf16[1,768,8192]{2,1,0:T(8,128)(2,1)} %tokens_hbm.1, bf16[512,1024]{1,0:T(8,128)(2,1)S(1)} %get-tuple-element.41.refs_0_.refs_2_), custom_call_target="tpu_custom_call" | custom-call | flops 6291456 | bytes 12582912 | tf_op jit(solution)/shard_map/load/pallas_call | solution.py:179
  18.1 0.8 collective-permute-done.2.refs_5_.refs_2_
  18.9 0.4 collective-permute-done.3.refs_6_.refs_4_
  19.2 2.2 %collective-permute-done.1.refs_1_ = bf16[256,1024]{1,0:T(8,128)(2,1)S(1)} collective-permute-done((bf16[256,1024]{1,0:T(8,128)(2,1)S(1)}, bf16[256,1024]{1,0:T(8,128)(2,1)S(1)}, u32[]{:S(2)}, u32[]{:S(2)}) %collective-permute-start.1) | collective-permute-done | bytes 524320 | tf_op jit(solution)/shard_map/ppermute | solution.py:37
  21.5 1.4 %collective-permute-start.8 = (bf16[512,1024]{1,0:T(8,128)(2,1)S(1)}, bf16[512,1024]{1,0:T(8,128)(2,1)S(1)}, u32[]{:S(2)}, u32[]{:S(2)}) collective-permute-start(bf16[512,1024]{1,0:T(8,128)(2,1)S(1)} %get-tuple-element.52.refs_3_), channel_id=1, source_target_pairs={{0,4},{1,13},{2,6},{3,15},{4,8},{5,1},{6,10},{7,3},{8,12},{9,5},{1... | collective-permute-start | bytes 3145736 | tf_op jit(solution)/shard_map/ppermute | solution.py:31
  22.9 2.7 %collective-permute-start.9 = (bf16[256,1024]{1,0:T(8,128)(2,1)S(1)}, bf16[256,1024]{1,0:T(8,128)(2,1)S(1)}, u32[]{:S(2)}, u32[]{:S(2)}) collective-permute-start(bf16[256,1024]{1,0:T(8,128)(2,1)S(1)} %get-tuple-element.55), channel_id=1, source_target_pairs={{0,2},{1,3},{2,0},{3,1},{4,6},{5,7},{6,4},{7,5},{8,10},{9,11},{10,... | collective-permute-start | bytes 1572872 | tf_op jit(solution)/shard_map/ppermute | solution.py:37
  25.6 2.9 %collective-permute-start.5 = (bf16[512,256]{1,0:T(8,128)(2,1)S(1)}, bf16[512,256]{1,0:T(8,128)(2,1)S(1)}, u32[]{:S(2)}, u32[]{:S(2)}) collective-permute-start(bf16[512,256]{1,0:T(8,128)(2,1)S(1)} %get-tuple-element.51), channel_id=1, source_target_pairs={{0,64},{16,80},{32,96},{48,112},{64,0},{80,16},{96,32},{112,48},{1... | collective-permute-start | bytes 786440 | tf_op jit(solution)/shard_map/ppermute | solution.py:50
  28.5 0.1 collective-permute-start.4
  28.6 0.0 collective-permute-done.6.refs_1_
  28.6 4.0 %project.4 = (f32[768,1024]{1,0:T(8,128)S(1)}, f32[768,1024]{1,0:T(8,128)S(1)}) custom-call(bf16[1,768,8192]{2,1,0:T(8,128)(2,1)S(1)} %get-tuple-element.42.refs_0_, bf16[1,768,8192]{2,1,0:T(8,128)(2,1)S(1)} %collective-permute-done.6.refs_1_, bf16[512,1024]{1,0:T(8,128)(2,1)S(1)} %get-tuple-element.41.refs_0_.refs_2_, ...), custom_call_target="tpu_custom_call" | custom-call | flops 3221225472 | bytes 2097152 | tf_op jit(solution)/shard_map/project/pallas_call | solution.py:240
  32.6 2.5 %collective-permute-done.5.refs_3_ = bf16[512,256]{1,0:T(8,128)(2,1)S(1)} collective-permute-done((bf16[512,256]{1,0:T(8,128)(2,1)S(1)}, bf16[512,256]{1,0:T(8,128)(2,1)S(1)}, u32[]{:S(2)}, u32[]{:S(2)}) %collective-permute-start.5) | collective-permute-done | bytes 262176 | tf_op jit(solution)/shard_map/ppermute | solution.py:50
  35.1 1.1 %partial.1 = (f32[512,128]{1,0:T(8,128)S(1)}, bf16[512,128]{1,0:T(8,128)(2,1)S(1)}) custom-call(f32[512,1024]{1,0:T(8,128)S(1)} %copy-done, bf16[512,256]{1,0:T(8,128)(2,1)S(1)} %get-tuple-element.50.refs_1_, bf16[512,256]{1,0:T(8,128)(2,1)S(1)} %collective-permute-done.2.refs_5_.refs_2_, bf16[512,256]{1,0:T(8,128)(2,1)S(1)} %collective-permute-done.5.refs_3_, ...), custom_call_target="tpu_custom_call" | custom-call | flops 25165824 | bytes 6291456 | tf_op jit(solution)/shard_map/partial/pallas_call | solution.py:394
  36.2 0.0 copy-start.1
  36.2 0.1 collective-permute-start.7
  36.3 1.0 %collective-permute-done.9.refs_1_ = bf16[256,1024]{1,0:T(8,128)(2,1)S(1)} collective-permute-done((bf16[256,1024]{1,0:T(8,128)(2,1)S(1)}, bf16[256,1024]{1,0:T(8,128)(2,1)S(1)}, u32[]{:S(2)}, u32[]{:S(2)}) %collective-permute-start.9) | collective-permute-done | bytes 524320 | tf_op jit(solution)/shard_map/ppermute | solution.py:37
  37.4 0.1 fusion
  37.5 0.7 collective-permute-start.12
  38.2 0.1 collective-permute-start.13
  38.2 2.6 %collective-permute-start.14 = (bf16[256,1024]{1,0:T(8,128)(2,1)S(1)}, bf16[256,1024]{1,0:T(8,128)(2,1)S(1)}, u32[]{:S(2)}, u32[]{:S(2)}) collective-permute-start(bf16[256,1024]{1,0:T(8,128)(2,1)S(1)} %get-tuple-element.80), channel_id=1, source_target_pairs={{0,2},{1,3},{2,0},{3,1},{4,6},{5,7},{6,4},{7,5},{8,10},{9,11},{10,... | collective-permute-start | bytes 1572872 | tf_op jit(solution)/shard_map/ppermute | solution.py:37
  40.8 0.2 collective-permute-done.4.refs_0_
  41.0 0.2 collective-permute-done.7.refs_1_
  41.3 2.1 %collective-permute-start.10 = (bf16[256,1024]{1,0:T(8,128)(2,1)S(1)}, bf16[256,1024]{1,0:T(8,128)(2,1)S(1)}, u32[]{:S(2)}, u32[]{:S(2)}) collective-permute-start(bf16[256,1024]{1,0:T(8,128)(2,1)S(1)} %get-tuple-element.58.refs_4_), channel_id=1, source_target_pairs={{0,4},{1,13},{2,6},{3,15},{4,8},{5,1},{6,10},{7,3},{8,12},{9,5},{1... | collective-permute-start | bytes 1572872 | tf_op jit(solution)/shard_map/ppermute | solution.py:31
  43.3 0.8 update.1
  44.1 1.2 %collective-permute-start.11 = (bf16[512,128]{1,0:T(8,128)(2,1)S(1)}, bf16[512,128]{1,0:T(8,128)(2,1)S(1)}, u32[]{:S(2)}, u32[]{:S(2)}) collective-permute-start(bf16[512,128]{1,0:T(8,128)(2,1)S(1)} %get-tuple-element.60.refs_7_.refs_0_), channel_id=1, source_target_pairs={{0,16},{16,0},{32,48},{48,32},{64,80},{80,64},{96,112},{112,96},{1... | collective-permute-start | bytes 393224 | tf_op jit(solution)/shard_map/ppermute | solution.py:50
  45.3 4.5 %project.5 = (f32[768,1024]{1,0:T(8,128)S(1)}, f32[768,1024]{1,0:T(8,128)S(1)}) custom-call(bf16[1,768,8192]{2,1,0:T(8,128)(2,1)S(1)} %get-tuple-element.42.refs_0_, bf16[1,768,8192]{2,1,0:T(8,128)(2,1)S(1)} %collective-permute-done.6.refs_1_, bf16[512,1024]{1,0:T(8,128)(2,1)S(1)} %get-tuple-element.57.refs_2_, ...), custom_call_target="tpu_custom_call", output_to_operand_aliasing={{0}: (5, {}), {1}: (6, {})} | custom-call | flops 1 | bytes 1 | tf_op jit(solution)/shard_map/project/pallas_call | solution.py:240
  49.9 0.1 collective-permute-start.16
  49.9 4.9 %collective-permute-done.11.refs_0_ = bf16[512,128]{1,0:T(8,128)(2,1)S(1)} collective-permute-done((bf16[512,128]{1,0:T(8,128)(2,1)S(1)}, bf16[512,128]{1,0:T(8,128)(2,1)S(1)}, u32[]{:S(2)}, u32[]{:S(2)}) %collective-permute-start.11) | collective-permute-done | bytes 131104 | tf_op jit(solution)/shard_map/ppermute | solution.py:50
  54.8 0.7 collective-permute-start.17
  55.5 0.1 join.1
  55.6 2.8 %collective-permute-start.18 = (bf16[512,256]{1,0:T(8,128)(2,1)S(1)}, bf16[512,256]{1,0:T(8,128)(2,1)S(1)}, u32[]{:S(2)}, u32[]{:S(2)}) collective-permute-start(bf16[512,256]{1,0:T(8,128)(2,1)S(1)} %get-tuple-element.65.refs_1_.refs_0_), channel_id=1, source_target_pairs={{0,96},{16,112},{32,0},{48,16},{64,32},{80,48},{96,64},{112,80},{1... | collective-permute-start | bytes 786440 | tf_op jit(solution)/shard_map/ppermute | solution.py:50
  58.4 1.8 %collective-permute-start.15 = (bf16[256,1024]{1,0:T(8,128)(2,1)S(1)}, bf16[256,1024]{1,0:T(8,128)(2,1)S(1)}, u32[]{:S(2)}, u32[]{:S(2)}) collective-permute-start(bf16[256,1024]{1,0:T(8,128)(2,1)S(1)} %phase.13.refs_7_.refs_3_), channel_id=1, source_target_pairs={{0,4},{1,13},{2,6},{3,15},{4,8},{5,1},{6,10},{7,3},{8,12},{9,5},{1... | collective-permute-start | bytes 1572872 | tf_op jit(solution)/shard_map/ppermute | solution.py:31
  60.2 1.3 %collective-permute-start.20 = (bf16[512,256]{1,0:T(8,128)(2,1)S(1)}, bf16[512,256]{1,0:T(8,128)(2,1)S(1)}, u32[]{:S(2)}, u32[]{:S(2)}) collective-permute-start(bf16[512,256]{1,0:T(8,128)(2,1)S(1)} %get-tuple-element.65.refs_1_.refs_0_), channel_id=1, source_target_pairs={{0,32},{16,48},{32,64},{48,80},{64,96},{80,112},{96,0},{112,16},{1... | collective-permute-start | bytes 786440 | tf_op jit(solution)/shard_map/ppermute | solution.py:50
  61.5 3.7 %project.6 = (f32[768,1024]{1,0:T(8,128)S(1)}, f32[768,1024]{1,0:T(8,128)S(1)}) custom-call(bf16[1,768,8192]{2,1,0:T(8,128)(2,1)S(1)} %get-tuple-element.42.refs_0_, bf16[1,768,8192]{2,1,0:T(8,128)(2,1)S(1)} %collective-permute-done.6.refs_1_, bf16[256,1024]{1,0:T(8,128)(2,1)S(1)} %collective-permute-done.13.refs_2_, ...), custom_call_target="tpu_custom_call", output_to_operand_aliasing={{0}: (5, {}), {1}: (6, {})} | custom-call | flops 1 | bytes 1 | tf_op jit(solution)/shard_map/project/pallas_call | solution.py:240
  65.2 2.7 %collective-permute-start.19 = (bf16[512,256]{1,0:T(8,128)(2,1)S(1)}, bf16[512,256]{1,0:T(8,128)(2,1)S(1)}, u32[]{:S(2)}, u32[]{:S(2)}) collective-permute-start(bf16[512,256]{1,0:T(8,128)(2,1)S(1)} %phase.14.refs_8_), channel_id=1, source_target_pairs={{0,64},{16,80},{32,96},{48,112},{64,0},{80,16},{96,32},{112,48},{1... | collective-permute-start | bytes 786440 | tf_op jit(solution)/shard_map/ppermute | solution.py:50
  67.9 4.3 %project.7 = (f32[768,1024]{1,0:T(8,128)S(1)}, bf16[768,1024]{1,0:T(8,128)(2,1)S(1)}) custom-call(bf16[1,768,8192]{2,1,0:T(8,128)(2,1)S(1)} %get-tuple-element.42.refs_0_, bf16[1,768,8192]{2,1,0:T(8,128)(2,1)S(1)} %collective-permute-done.6.refs_1_, bf16[256,1024]{1,0:T(8,128)(2,1)S(1)} %collective-permute-done.14.refs_3_.refs_2_, ...), custom_call_target="tpu_custom_call", output_to_operand_aliasing={{0}: (6, {})} | custom-call | flops 1 | bytes 1 | tf_op jit(solution)/shard_map/project/pallas_call | solution.py:240
  72.2 3.0 %collective-permute-done.19.refs_2_ = bf16[512,256]{1,0:T(8,128)(2,1)S(1)} collective-permute-done((bf16[512,256]{1,0:T(8,128)(2,1)S(1)}, bf16[512,256]{1,0:T(8,128)(2,1)S(1)}, u32[]{:S(2)}, u32[]{:S(2)}) %collective-permute-start.19) | collective-permute-done | bytes 262176 | tf_op jit(solution)/shard_map/ppermute | solution.py:50
  75.2 1.8 %collective-permute-start.22 = (bf16[768,1024]{1,0:T(8,128)(2,1)S(1)}, bf16[768,1024]{1,0:T(8,128)(2,1)S(1)}, u32[]{:S(2)}, u32[]{:S(2)}) collective-permute-start(bf16[768,1024]{1,0:T(8,128)(2,1)S(1)} %get-tuple-element.74), channel_id=1, source_target_pairs={{0,1},{1,0},{2,3},{3,2},{4,5},{5,4},{6,7},{7,6},{8,9},{9,8},{10,11... | collective-permute-start | bytes 4718600 | tf_op jit(solution)/shard_map/ppermute | solution.py:41
  77.0 0.1 collective-permute-start.21
  77.1 1.0 %finish.2.refs_4_.refs_2_ = f32[768,1024]{1,0:T(8,128)S(1)} custom-call(bf16[1,768,8192]{2,1,0:T(8,128)(2,1)S(1)} %get-tuple-element.42.refs_0_, bf16[256,1024]{1,0:T(8,128)(2,1)S(1)} %get-tuple-element.72.refs_1_, f32[768,1024]{1,0:T(8,128)S(1)} %get-tuple-element.73.refs_2_), custom_call_target="tpu_custom_call", output_to_operand_aliasing={{}: (2, {})} | custom-call | flops 402653184 | bytes 524288 | tf_op jit(solution)/shard_map/finish/pallas_call | solution.py:308
  78.0 1.3 %assemble.1 = (bf16[512,1024]{1,0:T(8,128)(2,1)}, f32[8,128]{1,0:T(8,128)S(1)}) custom-call(bf16[512,256]{1,0:T(8,128)(2,1)S(1)} %get-tuple-element.65.refs_1_.refs_0_, bf16[512,256]{1,0:T(8,128)(2,1)S(1)} %collective-permute-done.18.refs_2_.refs_1_, bf16[512,256]{1,0:T(8,128)(2,1)S(1)} %get-tuple-element.75.refs_2_, ...), custom_call_target="tpu_custom_call" | custom-call | flops 8388608 | bytes 2097152 | tf_op jit(solution)/shard_map/assemble/pallas_call | solution.py:394
  79.3 1.4 %collective-permute-done.21.refs_1_ = bf16[256,1024]{1,0:T(8,128)(2,1)S(1)} collective-permute-done((bf16[256,1024]{1,0:T(8,128)(2,1)S(1)}, bf16[256,1024]{1,0:T(8,128)(2,1)S(1)}, u32[]{:S(2)}, u32[]{:S(2)}) %collective-permute-start.21) | collective-permute-done | bytes 524320 | tf_op jit(solution)/shard_map/ppermute | solution.py:41
  80.8 1.9 %finish.3 = bf16[1,768,1024]{2,1,0:T(8,128)(2,1)} custom-call(bf16[1,768,8192]{2,1,0:T(8,128)(2,1)S(1)} %get-tuple-element.42.refs_0_, bf16[256,1024]{1,0:T(8,128)(2,1)S(1)} %collective-permute-done.21.refs_1_, f32[768,1024]{1,0:T(8,128)S(1)} %finish.2.refs_4_.refs_2_, bf16[768,1024]{1,0:T(8,128)(2,1)S(1)} %collective-permute-done.22.refs_3_, ...), custom_call_target="tpu_custom_call" | custom-call | flops 402653184 | bytes 524288 | tf_op jit(solution)/shard_map/finish/pallas_call | solution.py:308
  (23 shorter events, 0.0 us)
Async XLA Ops:
  0.6 28.0 %collective-permute-start.6 = (bf16[1,768,8192]{2,1,0:T(8,128)(2,1)}, bf16[1,768,8192]{2,1,0:T(8,128)(2,1)S(1)}, u32[]{:S(2)}, u32[]{:S(2)}) collective-permute-start(bf16[1,768,8192]{2,1,0:T(8,128)(2,1)} %tokens_hbm.1), channel_id=1, source_target_pairs={{0,1},{1,0},{2,3},{3,2},{4,5},{5,4},{6,7},{7,6},{8,9},{9,8},{10,11... | collective-permute-start | bytes 37748744 | tf_op jit(solution)/shard_map/ppermute | solution.py:41
  3.8 17.7 %collective-permute-start = (bf16[512,1024]{1,0:T(8,128)(2,1)S(1)}, bf16[512,1024]{1,0:T(8,128)(2,1)S(1)}, u32[]{:S(2)}, u32[]{:S(2)}) collective-permute-start(bf16[512,1024]{1,0:T(8,128)(2,1)S(1)} %get-tuple-element.41.refs_0_.refs_2_), channel_id=1, source_target_pairs={{0,4},{1,13},{2,6},{3,15},{4,8},{5,1},{6,10},{7,3},{8,12},{9,5},{1... | collective-permute-start | bytes 3145736 | tf_op jit(solution)/shard_map/ppermute | solution.py:31
  7.7 13.8 %collective-permute-start.1 = (bf16[256,1024]{1,0:T(8,128)(2,1)S(1)}, bf16[256,1024]{1,0:T(8,128)(2,1)S(1)}, u32[]{:S(2)}, u32[]{:S(2)}) collective-permute-start(bf16[256,1024]{1,0:T(8,128)(2,1)S(1)} %get-tuple-element.43), channel_id=1, source_target_pairs={{0,2},{1,3},{2,0},{3,1},{4,6},{5,7},{6,4},{7,5},{8,10},{9,11},{10,... | collective-permute-start | bytes 1572872 | tf_op jit(solution)/shard_map/ppermute | solution.py:37
  10.4 8.5 %collective-permute-start.2 = (bf16[512,256]{1,0:T(8,128)(2,1)S(1)}, bf16[512,256]{1,0:T(8,128)(2,1)S(1)}, u32[]{:S(2)}, u32[]{:S(2)}) collective-permute-start(bf16[512,256]{1,0:T(8,128)(2,1)S(1)} %get-tuple-element.47), channel_id=1, source_target_pairs={{0,32},{16,48},{32,64},{48,80},{64,96},{80,112},{96,0},{112,16},{1... | collective-permute-start | bytes 786440 | tf_op jit(solution)/shard_map/ppermute | solution.py:50
  11.7 7.5 %collective-permute-start.3 = (bf16[512,256]{1,0:T(8,128)(2,1)S(1)}, bf16[512,256]{1,0:T(8,128)(2,1)S(1)}, u32[]{:S(2)}, u32[]{:S(2)}) collective-permute-start(bf16[512,256]{1,0:T(8,128)(2,1)S(1)} %get-tuple-element.48), channel_id=1, source_target_pairs={{0,96},{16,112},{32,0},{48,16},{64,32},{80,48},{96,64},{112,80},{1... | collective-permute-start | bytes 786440 | tf_op jit(solution)/shard_map/ppermute | solution.py:50
  21.5 15.9 %collective-permute-start.8 = (bf16[512,1024]{1,0:T(8,128)(2,1)S(1)}, bf16[512,1024]{1,0:T(8,128)(2,1)S(1)}, u32[]{:S(2)}, u32[]{:S(2)}) collective-permute-start(bf16[512,1024]{1,0:T(8,128)(2,1)S(1)} %get-tuple-element.52.refs_3_), channel_id=1, source_target_pairs={{0,4},{1,13},{2,6},{3,15},{4,8},{5,1},{6,10},{7,3},{8,12},{9,5},{1... | collective-permute-start | bytes 3145736 | tf_op jit(solution)/shard_map/ppermute | solution.py:31
  22.9 14.5 %collective-permute-start.9 = (bf16[256,1024]{1,0:T(8,128)(2,1)S(1)}, bf16[256,1024]{1,0:T(8,128)(2,1)S(1)}, u32[]{:S(2)}, u32[]{:S(2)}) collective-permute-start(bf16[256,1024]{1,0:T(8,128)(2,1)S(1)} %get-tuple-element.55), channel_id=1, source_target_pairs={{0,2},{1,3},{2,0},{3,1},{4,6},{5,7},{6,4},{7,5},{8,10},{9,11},{10,... | collective-permute-start | bytes 1572872 | tf_op jit(solution)/shard_map/ppermute | solution.py:37
  25.6 9.5 %collective-permute-start.5 = (bf16[512,256]{1,0:T(8,128)(2,1)S(1)}, bf16[512,256]{1,0:T(8,128)(2,1)S(1)}, u32[]{:S(2)}, u32[]{:S(2)}) collective-permute-start(bf16[512,256]{1,0:T(8,128)(2,1)S(1)} %get-tuple-element.51), channel_id=1, source_target_pairs={{0,64},{16,80},{32,96},{48,112},{64,0},{80,16},{96,32},{112,48},{1... | collective-permute-start | bytes 786440 | tf_op jit(solution)/shard_map/ppermute | solution.py:50
  28.5 12.5 %collective-permute-start.4 = (bf16[256,1024]{1,0:T(8,128)(2,1)S(1)}, bf16[256,1024]{1,0:T(8,128)(2,1)S(1)}, u32[]{:S(2)}, u32[]{:S(2)}) collective-permute-start(bf16[256,1024]{1,0:T(8,128)(2,1)S(1)} %get-tuple-element.49.refs_3_), channel_id=1, source_target_pairs={{0,4},{1,13},{2,6},{3,15},{4,8},{5,1},{6,10},{7,3},{8,12},{9,5},{1... | collective-permute-start | bytes 1572872 | tf_op jit(solution)/shard_map/ppermute | solution.py:31
  28.6 6.5 %copy-start = (f32[512,1024]{1,0:T(8,128)S(1)}, f32[512,1024]{1,0:T(8,128)}, u32[]{:S(2)}) copy-start(f32[512,1024]{1,0:T(8,128)} %refs_0_.3) | copy-start | bytes 6291460
  36.2 7.1 %copy-start.1 = (bf16[512,128]{1,0:T(8,128)(2,1)S(1)}, bf16[512,128]{1,0:T(8,128)(2,1)}, u32[]{:S(2)}) copy-start(bf16[512,128]{1,0:T(8,128)(2,1)} %refs_1_.1) | copy-start | bytes 393220
  36.2 5.0 %collective-permute-start.7 = (bf16[512,128]{1,0:T(8,128)(2,1)S(1)}, bf16[512,128]{1,0:T(8,128)(2,1)S(1)}, u32[]{:S(2)}, u32[]{:S(2)}) collective-permute-start(bf16[512,128]{1,0:T(8,128)(2,1)S(1)} %get-tuple-element.54), channel_id=1, source_target_pairs={{0,16},{16,0},{32,48},{48,32},{64,80},{80,64},{96,112},{112,96},{1... | collective-permute-start | bytes 393224 | tf_op jit(solution)/shard_map/ppermute | solution.py:50
  37.5 12.4 %collective-permute-start.12 = (bf16[256,1024]{1,0:T(8,128)(2,1)S(1)}, bf16[256,1024]{1,0:T(8,128)(2,1)S(1)}, u32[]{:S(2)}, u32[]{:S(2)}) collective-permute-start(bf16[256,1024]{1,0:T(8,128)(2,1)S(1)} %get-tuple-element.80), channel_id=1, source_target_pairs={{0,4},{1,13},{2,6},{3,15},{4,8},{5,1},{6,10},{7,3},{8,12},{9,5},{1... | collective-permute-start | bytes 1572872 | tf_op jit(solution)/shard_map/ppermute | solution.py:31
  38.2 17.4 %collective-permute-start.13 = (bf16[256,1024]{1,0:T(8,128)(2,1)S(1)}, bf16[256,1024]{1,0:T(8,128)(2,1)S(1)}, u32[]{:S(2)}, u32[]{:S(2)}) collective-permute-start(bf16[256,1024]{1,0:T(8,128)(2,1)S(1)} %get-tuple-element.79), channel_id=1, source_target_pairs={{0,4},{1,13},{2,6},{3,15},{4,8},{5,1},{6,10},{7,3},{8,12},{9,5},{1... | collective-permute-start | bytes 1572872 | tf_op jit(solution)/shard_map/ppermute | solution.py:31
  38.2 17.3 %collective-permute-start.14 = (bf16[256,1024]{1,0:T(8,128)(2,1)S(1)}, bf16[256,1024]{1,0:T(8,128)(2,1)S(1)}, u32[]{:S(2)}, u32[]{:S(2)}) collective-permute-start(bf16[256,1024]{1,0:T(8,128)(2,1)S(1)} %get-tuple-element.80), channel_id=1, source_target_pairs={{0,2},{1,3},{2,0},{3,1},{4,6},{5,7},{6,4},{7,5},{8,10},{9,11},{10,... | collective-permute-start | bytes 1572872 | tf_op jit(solution)/shard_map/ppermute | solution.py:37
  41.3 17.1 %collective-permute-start.10 = (bf16[256,1024]{1,0:T(8,128)(2,1)S(1)}, bf16[256,1024]{1,0:T(8,128)(2,1)S(1)}, u32[]{:S(2)}, u32[]{:S(2)}) collective-permute-start(bf16[256,1024]{1,0:T(8,128)(2,1)S(1)} %get-tuple-element.58.refs_4_), channel_id=1, source_target_pairs={{0,4},{1,13},{2,6},{3,15},{4,8},{5,1},{6,10},{7,3},{8,12},{9,5},{1... | collective-permute-start | bytes 1572872 | tf_op jit(solution)/shard_map/ppermute | solution.py:31
  44.1 10.7 %collective-permute-start.11 = (bf16[512,128]{1,0:T(8,128)(2,1)S(1)}, bf16[512,128]{1,0:T(8,128)(2,1)S(1)}, u32[]{:S(2)}, u32[]{:S(2)}) collective-permute-start(bf16[512,128]{1,0:T(8,128)(2,1)S(1)} %get-tuple-element.60.refs_7_.refs_0_), channel_id=1, source_target_pairs={{0,16},{16,0},{32,48},{48,32},{64,80},{80,64},{96,112},{112,96},{1... | collective-permute-start | bytes 393224 | tf_op jit(solution)/shard_map/ppermute | solution.py:50
  49.9 18.1 %collective-permute-start.16 = (bf16[256,1024]{1,0:T(8,128)(2,1)S(1)}, bf16[256,1024]{1,0:T(8,128)(2,1)S(1)}, u32[]{:S(2)}, u32[]{:S(2)}) collective-permute-start(bf16[256,1024]{1,0:T(8,128)(2,1)S(1)} %get-tuple-element.66), channel_id=1, source_target_pairs={{0,4},{1,13},{2,6},{3,15},{4,8},{5,1},{6,10},{7,3},{8,12},{9,5},{1... | collective-permute-start | bytes 1572872 | tf_op jit(solution)/shard_map/ppermute | solution.py:31
  54.8 13.1 %collective-permute-start.17 = (bf16[256,1024]{1,0:T(8,128)(2,1)S(1)}, bf16[256,1024]{1,0:T(8,128)(2,1)S(1)}, u32[]{:S(2)}, u32[]{:S(2)}) collective-permute-start(bf16[256,1024]{1,0:T(8,128)(2,1)S(1)} %get-tuple-element.64.refs_1_.refs_3_), channel_id=1, source_target_pairs={{0,2},{1,3},{2,0},{3,1},{4,6},{5,7},{6,4},{7,5},{8,10},{9,11},{10,... | collective-permute-start | bytes 1572872 | tf_op jit(solution)/shard_map/ppermute | solution.py:37
  55.6 9.6 %collective-permute-start.18 = (bf16[512,256]{1,0:T(8,128)(2,1)S(1)}, bf16[512,256]{1,0:T(8,128)(2,1)S(1)}, u32[]{:S(2)}, u32[]{:S(2)}) collective-permute-start(bf16[512,256]{1,0:T(8,128)(2,1)S(1)} %get-tuple-element.65.refs_1_.refs_0_), channel_id=1, source_target_pairs={{0,96},{16,112},{32,0},{48,16},{64,32},{80,48},{96,64},{112,80},{1... | collective-permute-start | bytes 786440 | tf_op jit(solution)/shard_map/ppermute | solution.py:50
  58.4 16.8 %collective-permute-start.15 = (bf16[256,1024]{1,0:T(8,128)(2,1)S(1)}, bf16[256,1024]{1,0:T(8,128)(2,1)S(1)}, u32[]{:S(2)}, u32[]{:S(2)}) collective-permute-start(bf16[256,1024]{1,0:T(8,128)(2,1)S(1)} %phase.13.refs_7_.refs_3_), channel_id=1, source_target_pairs={{0,4},{1,13},{2,6},{3,15},{4,8},{5,1},{6,10},{7,3},{8,12},{9,5},{1... | collective-permute-start | bytes 1572872 | tf_op jit(solution)/shard_map/ppermute | solution.py:31
  60.2 12.0 %collective-permute-start.20 = (bf16[512,256]{1,0:T(8,128)(2,1)S(1)}, bf16[512,256]{1,0:T(8,128)(2,1)S(1)}, u32[]{:S(2)}, u32[]{:S(2)}) collective-permute-start(bf16[512,256]{1,0:T(8,128)(2,1)S(1)} %get-tuple-element.65.refs_1_.refs_0_), channel_id=1, source_target_pairs={{0,32},{16,48},{32,64},{48,80},{64,96},{80,112},{96,0},{112,16},{1... | collective-permute-start | bytes 786440 | tf_op jit(solution)/shard_map/ppermute | solution.py:50
  65.2 10.0 %collective-permute-start.19 = (bf16[512,256]{1,0:T(8,128)(2,1)S(1)}, bf16[512,256]{1,0:T(8,128)(2,1)S(1)}, u32[]{:S(2)}, u32[]{:S(2)}) collective-permute-start(bf16[512,256]{1,0:T(8,128)(2,1)S(1)} %phase.14.refs_8_), channel_id=1, source_target_pairs={{0,64},{16,80},{32,96},{48,112},{64,0},{80,16},{96,32},{112,48},{1... | collective-permute-start | bytes 786440 | tf_op jit(solution)/shard_map/ppermute | solution.py:50
  75.2 5.6 %collective-permute-start.22 = (bf16[768,1024]{1,0:T(8,128)(2,1)S(1)}, bf16[768,1024]{1,0:T(8,128)(2,1)S(1)}, u32[]{:S(2)}, u32[]{:S(2)}) collective-permute-start(bf16[768,1024]{1,0:T(8,128)(2,1)S(1)} %get-tuple-element.74), channel_id=1, source_target_pairs={{0,1},{1,0},{2,3},{3,2},{4,5},{5,4},{6,7},{7,6},{8,9},{9,8},{10,11... | collective-permute-start | bytes 4718600 | tf_op jit(solution)/shard_map/ppermute | solution.py:41
  77.0 3.8 %collective-permute-start.21 = (bf16[256,1024]{1,0:T(8,128)(2,1)S(1)}, bf16[256,1024]{1,0:T(8,128)(2,1)S(1)}, u32[]{:S(2)}, u32[]{:S(2)}) collective-permute-start(bf16[256,1024]{1,0:T(8,128)(2,1)S(1)} %get-tuple-element.72.refs_1_), channel_id=1, source_target_pairs={{0,1},{1,0},{2,3},{3,2},{4,5},{5,4},{6,7},{7,6},{8,9},{9,8},{10,11... | collective-permute-start | bytes 1572872 | tf_op jit(solution)/shard_map/ppermute | solution.py:41
